TPU v7x, 1024 devices: a whole 4x8x16 slice. The times are simulated.
1024 devices in a mesh: inter: 16 (over x_hi, y), intra: 64 (over x_lo, z, core).
Axes of the slice: x: 4 (x_hi: 2, x_lo: 2; x = x_hi * 2 + x_lo), y: 8, z: 16, core: 2. Of those that a mesh axis runs over, the one named last changes fastest.
Arguments:
- tokens: bfloat16 [131072, 4096], P(('inter', 'intra')), may hold values from -6 to 6
- key_grad: bfloat16 [131072, 512], P(('inter', 'intra')), may hold values from -6 to 6
- codes: bfloat16 [4096, 512], P(('intra', 'inter')), may hold values from -6 to 6
- scales: bfloat16 [4096, 4], P(('intra', 'inter')), may hold values from 0.0039978027 to 0.039794922
Outputs:
- keys: bfloat16 [131072, 512], P(('inter', 'intra'))
- input_grad: bfloat16 [131072, 4096], P(('inter', 'intra'))
- weight_grad: float32 [4096, 512], P(('intra', 'inter'))
All inputs are finite; a program needn't handle non-finite values.
Results may differ from a plain program's by a relative error of at most 0.0049.
Values may be sent and summed in bfloat16 or wider, within the bound.
No kernel may reach another device: no remote copies, remote signals or barrier semaphores. Data moves between devices by JAX's collectives and lax.ppermute only.
A program may use at most 128 MiB of HBM per device.

v0:
```python
import jax
import jax.numpy as jnp
from jax import lax
from jax.sharding import PartitionSpec as P

KV = 512
BLOCK = 128


def dequantize(codes, scales):
    rows = codes.shape[0]
    blocks = codes.astype(jnp.float32).reshape(rows, KV // BLOCK, BLOCK)
    scaled = blocks * scales.astype(jnp.float32)[:, :, None]
    return scaled.reshape(rows, KV).astype(jnp.bfloat16)


def partial_product(tokens, columns):
    partial_value = lax.dot_general(
        tokens, columns, (((0,), (0,)), ((), ())), preferred_element_type=jnp.float32
    )
    return partial_value.astype(jnp.bfloat16)


def shards(tokens, key_grad, codes, scales):
    group_codes, group_scales = (
        lax.all_gather(codes, "inter", axis=0, tiled=True),
        lax.all_gather(scales, "inter", axis=0, tiled=True),
    )
    all_codes, all_scales = (
        lax.all_gather(group_codes, "intra", axis=0, tiled=True),
        lax.all_gather(group_scales, "intra", axis=0, tiled=True),
    )
    weight = dequantize(all_codes, all_scales)
    keys = jnp.dot(tokens, weight, preferred_element_type=jnp.float32).astype(jnp.bfloat16)
    input_grad = lax.dot_general(
        key_grad, weight, (((1,), (1,)), ((), ())), preferred_element_type=jnp.float32
    ).astype(jnp.bfloat16)
    rounded = partial_product(tokens, key_grad)
    received = lax.all_to_all(rounded[None], "intra", split_axis=1, concat_axis=0, tiled=True)
    group_total = jnp.sum(received, axis=0, dtype=jnp.float32)
    weight_grad = lax.psum_scatter(group_total, "inter", scatter_dimension=0, tiled=True)
    return (keys, input_grad, weight_grad)


def solution(mesh):
    return jax.shard_map(
        shards,
        mesh=mesh,
        in_specs=(
            P(("inter", "intra"), None),
            P(("inter", "intra"), None),
            P(("intra", "inter"), None),
            P(("intra", "inter"), None),
        ),
        out_specs=(
            P(("inter", "intra"), None),
            P(("inter", "intra"), None),
            P(("intra", "inter"), None),
        ),
        check_vma=False,
    )
```

profile of v0, /device:TPU:1, one launch (start us, length us, event | category | flops | bytes accessed | tf_op | source)
XLA Modules:
  0.0 574.2 jit_solution(12683015177603002448)
XLA Ops:
  8.0 0.0 copy-start
  8.0 1.2 copy-done
  9.2 2.2 fusion.1
  11.4 36.5 %copy.33 = bf16[1,4096,512]{2,0,1:T(2,128)(2,1)} copy(bf16[1,4096,512]{2,1,0:T(8,128)(2,1)S(1)} %fusion.1) | data formatting | bytes 8388608 | tf_op jit(solution)/shard_map/broadcast_in_dim | solution.py:39
  47.9 0.5 broadcast.2
  48.4 28.5 %reduce = bf16[4096,512]{1,0:T(8,128)(2,1)} reduce(bf16[4096,1,512]{2,1,0:T(2,128)(2,1)} %bitcast.29, bf16[]{:T(256)} %broadcast.2), dimensions={1}, to_apply=%bitcast.26.reduce_sub_computation | reduce | bytes 8388610
  76.9 7.9 %reshape.25 = bf16[64,2,16384]{2,1,0:T(2,128)(2,1)} reshape(bf16[4096,512]{1,0:T(8,128)(2,1)} %reduce) | data formatting | bytes 8388608
  84.7 0.0 copy-start.4
  84.7 0.0 copy-start.5
  84.7 22.1 %all-to-all-start = ((bf16[64,2,16384]{2,1,0:T(2,128)(2,1)}), bf16[64,2,16384]{2,1,0:T(2,128)(2,1)}, u32[]{:S(2)}, u32[]{:S(2)}) async-start(bf16[64,2,16384]{2,1,0:T(2,128)(2,1)} %reshape.25), calls=%async_computation | async-start | bytes 8388608 | tf_op jit(solution)/shard_map/all_to_all | solution.py:39
  106.8 0.0 all-gather.5.cloned.1.call-start
  106.9 0.0 copy-done.4
  106.9 36.9 %all-gather = bf16[16,4,512]{2,1,0:T(4,128)(2,1)S(1)} all-gather(bf16[1,4,512]{2,1,0:T(4,128)(2,1)S(1)} %bitcast.34), channel_id=1, replica_groups=mesh['inter'=16,'intra'=64] {'inter'}, dimensions={0}, use_global_device_ids=true | all-gather | bytes 69632 | tf_op jit(solution)/shard_map/all_gather | solution.py:26
  143.7 0.6 reshape.17
  144.4 0.0 all-gather.5.cloned.1.call-update
  144.4 0.0 all-reduce.3.cloned.1.call-start
  144.5 0.0 copy-done.5
  144.5 31.8 %all-gather.1 = bf16[16,4,4]{2,1,0:T(4,128)(2,1)S(1)} all-gather(bf16[1,4,4]{2,1,0:T(4,128)(2,1)S(1)} %bitcast.35), channel_id=1, replica_groups=mesh['inter'=16,'intra'=64] {'inter'}, dimensions={0}, use_global_device_ids=true | all-gather | bytes 544 | tf_op jit(solution)/shard_map/all_gather | solution.py:27
  176.3 0.1 copy.19
  176.4 184.2 %all-gather.2 = bf16[64,64,4]{1,2,0:T(4,128)(2,1)S(1)} all-gather(bf16[1,64,4]{1,2,0:T(4,128)(2,1)S(1)} %copy.19), channel_id=1, replica_groups=mesh['inter'=16,'intra'=64] {'intra'}, dimensions={0}, use_global_device_ids=true | all-gather | bytes 33280 | tf_op jit(solution)/shard_map/all_gather | solution.py:31
  360.6 0.7 copy.25
  361.3 1.3 dynamic-slice
  363.2 0.0 all-gather.5.cloned.1.call-done
  363.3 0.0 copy-start.2
  363.3 9.5 %mul.11 = f32[4096,4,128]{2,1,0:T(4,128)S(1)} broadcast(f32[4096,4]{1,0:T(8,128)S(1)} %bitcast.32), dimensions={0,1} | broadcast | bytes 8454144 | tf_op jit(solution)/shard_map/mul | solution.py:13
  372.8 0.0 copy-start.1
  372.8 3.2 copy-done.1
  376.0 0.0 copy-done.2
  376.0 2.3 fusion.3
  378.4 0.0 all-to-all-done
  378.4 19.8 %reshape.26 = bf16[4096,1,512]{2,1,0:T(2,128)(2,1)} reshape(bf16[64,2,16384]{2,1,0:T(2,128)(2,1)} %all-to-all-done) | data formatting | bytes 8388608
  398.1 7.6 %copy.26 = f32[1,4096,512]{2,1,0:T(8,128)} copy(bf16[1,4096,512]{2,0,1:T(2,128)(2,1)} %bitcast.31) | data formatting | bytes 12582912
  405.8 0.0 copy-start.3
  405.8 4.7 reduce_sum.9
  410.5 0.0 all-reduce.3.cloned.1.call-update
  410.5 0.0 copy-done.3
  410.6 5.8 %fusion.2 = bf16[128,4096]{0,1:T(8,128)(2,1)S(1)} fusion(bf16[128,512]{1,0:T(8,128)(2,1)S(1)} %copy-done.3, f32[512,8,4,128]{3,2,1,0:T(4,128)} %bitcast.28, bf16[4096,512]{1,0:T(8,128)(2,1)} %all-gather.5.cloned.1.call-done), kind=kOutput, calls=%fused_computation.5 | convolution fusion | flops 543686656 | bytes 13762560 | tf_op jit(solution)/shard_map/dot_general | solution.py:35
  416.4 1.3 copy.24
  417.7 0.8 copy.23
  418.5 147.0 %all-reduce.3.cloned.1.call-done = f32[64,512]{1,0:T(8,128)} async-done(((f32[64,512]{1,0:T(8,128)}), f32[64,512]{1,0:T(8,128)}) %all-reduce.3.cloned.1.call-update) | async-done | bytes 131088
  565.4 1.3 constant_dynamic-slice_fusion
  (1 shorter events, 0.0 us)
Async XLA Ops:
  8.0 1.2 copy-start
  84.7 22.1 %copy-start.4 = (bf16[4,512]{1,0:T(4,128)(2,1)S(1)}, bf16[4,512]{1,0:T(4,128)(2,1)}, u32[]{:S(2)}) copy-start(bf16[4,512]{1,0:T(4,128)(2,1)} %param.6) | copy-start | bytes 12292
  84.7 59.7 %copy-start.5 = (bf16[4,4]{1,0:T(4,128)(2,1)S(1)}, bf16[4,4]{1,0:T(4,128)(2,1)}, u32[]{:S(2)}) copy-start(bf16[4,4]{1,0:T(4,128)(2,1)} %param.7) | copy-start | bytes 100
  84.7 293.6 %all-to-all-start = ((bf16[64,2,16384]{2,1,0:T(2,128)(2,1)}), bf16[64,2,16384]{2,1,0:T(2,128)(2,1)}, u32[]{:S(2)}, u32[]{:S(2)}) async-start(bf16[64,2,16384]{2,1,0:T(2,128)(2,1)} %reshape.25), calls=%async_computation | async-start | bytes 8388608 | tf_op jit(solution)/shard_map/all_to_all | solution.py:39
  106.8 256.5 %all-gather.5.cloned.1.call-start = ((), (), s32[]{:S(2)}) async-start(), calls=%async_computation.1 | async-start | bytes 4259840 | tf_op jit(solution)/shard_map/all_gather | solution.py:30
  144.4 421.0 %all-reduce.3.cloned.1.call-start = ((), (), s32[]{:S(2)}) async-start(), calls=%async_computation.2 | async-start | bytes 262144
  363.3 12.7 %copy-start.2 = (bf16[4096,512]{1,0:T(8,128)(2,1)S(1)}, bf16[4096,512]{1,0:T(8,128)(2,1)}, u32[]{:S(2)}) copy-start(bf16[4096,512]{1,0:T(8,128)(2,1)} %all-gather.5.cloned.1.call-done) | copy-start | bytes 12582916
  372.8 3.2 copy-start.1
  405.8 4.8 copy-start.3
Sparse Core Ops, SparseCore 0:
  144.5 189.5 all-gather.4
Sparse Core Ops, SparseCore 1:
  410.6 154.7 all-reduce.2
where the time goes:
time: 583 us; the launch traced here: 574 us
  blocking collectives  253 us (43%)
  waiting for transfers between devices  147 us (25%)
  local copies, waits for them, and re-layouts  92.3 us (16%)
  other arithmetic  33.2 us (6%)
  starting transfers between devices  22.2 us (4%)
  between operations  16.3 us (3%)
  matrix products  10.3 us (2%)
    all_gather x1, blocking collectives, shards(): lax.all_gather(group_scales, 'intra', axis=0, tiled=True)  184 us
    unnamed x3, waiting for transfers between devices  147 us
    unnamed x22, local copies, waits for them, and re-layouts  45.6 us
    all_gather x1, blocking collectives, shards(): lax.all_gather(codes, 'inter', axis=0, tiled=True)  36.9 us
    broadcast_in_dim x1, local copies, waits for them, and re-layouts, shards(): rounded[None]  36.5 us
    all_gather x1, blocking collectives, shards(): lax.all_gather(scales, 'inter', axis=0, tiled=True)  31.8 us
    unnamed x1, other arithmetic  28.5 us
    all_to_all x1, starting transfers between devices, shards(): lax.all_to_all(rounded[None], 'intra', split_axis=1, concat_axis=0, tiled...  22.1 us
  transfers between devices with their start and end apart: 3, of which 1 were waited for; matrix products, arithmetic and copies ran while one was open for 4% of the time, Pallas kernels for 0%

commit v1 on v0

v1 whole, which is shorter than its diff:
```python
import jax
import jax.numpy as jnp
from jax import lax
from jax.sharding import Mesh, PartitionSpec as P

KV = 512
BLOCK = 128
D_IN = 4096
INTER = ("xh", "y")
INTRA = ("xl", "z", "c")
SIZES = (2, 8, 2, 16, 2)
F32 = jnp.float32
BF16 = jnp.bfloat16


def dequantize(codes, scales):
    rows = codes.shape[0]
    blocks = codes.astype(F32).reshape(rows, KV // BLOCK, BLOCK)
    scaled = blocks * scales.astype(F32)[:, :, None]
    return scaled.reshape(rows, KV).astype(BF16)


def exchange(blocks, axis):
    return lax.all_to_all(blocks, axis, split_axis=0, concat_axis=0, tiled=True)


def gather_weight(part):
    by_z = exchange(jnp.broadcast_to(part[None], (16, 4, KV)), "z").reshape(64, KV)
    by_y = exchange(jnp.broadcast_to(by_z[None], (8, 64, KV)), "y")
    rows = by_y.reshape(8, 16, 4, KV).transpose(1, 0, 2, 3).reshape(512, KV)
    by_x = exchange(jnp.broadcast_to(rows[None], (4, 512, KV)), ("xh", "xl"))
    own = by_x.reshape(2048, KV)
    other = lax.ppermute(own, "c", [(0, 1), (1, 0)])
    first = lax.axis_index("c") == 0
    both = jnp.stack([jnp.where(first, own, other), jnp.where(first, other, own)])
    both = both.reshape(2, 2, 2, 16, 32, KV).transpose(2, 3, 0, 1, 4, 5)
    return both.reshape(D_IN, KV)


def scatter_sum(partial):
    blocks = partial.reshape(2, 16, 2, 2, 32, KV).transpose(2, 3, 0, 1, 4, 5)
    by_c = exchange(blocks.reshape(2, 2048, KV), "c")
    total = (by_c[0].astype(F32) + by_c[1].astype(F32)).astype(BF16)
    by_x = exchange(total.reshape(4, 512, KV), ("xh", "xl"))
    total = jnp.sum(by_x.astype(F32), axis=0).astype(BF16)
    total = total.reshape(16, 8, 4, KV).transpose(1, 0, 2, 3).reshape(8, 64, KV)
    by_y = exchange(total, "y")
    total = jnp.sum(by_y.astype(F32), axis=0).astype(BF16)
    by_z = exchange(total.reshape(16, 4, KV), "z")
    return jnp.sum(by_z.astype(F32), axis=0)


def shards(tokens, key_grad, codes, scales):
    part = dequantize(codes, scales)
    partial = lax.dot_general(
        tokens, key_grad, (((0,), (0,)), ((), ())), preferred_element_type=F32
    ).astype(BF16)
    weight_grad = scatter_sum(partial)
    weight = gather_weight(part)
    keys = jnp.dot(tokens, weight, preferred_element_type=F32).astype(BF16)
    input_grad = lax.dot_general(
        key_grad, weight, (((1,), (1,)), ((), ())), preferred_element_type=F32
    ).astype(BF16)
    return keys, input_grad, weight_grad


def solution(mesh):
    torus = Mesh(mesh.devices.reshape(SIZES), ("xh", "y", "xl", "z", "c"))
    tokens_over = P(INTER + INTRA, None)
    rows_over = P(INTRA + INTER, None)
    return jax.shard_map(
        shards,
        mesh=torus,
        in_specs=(tokens_over, tokens_over, rows_over, rows_over),
        out_specs=(tokens_over, tokens_over, rows_over),
        check_vma=False,
    )
```

time: 583 us -> 181 us (0.31)
  blocking collectives: 253 us -> 48.3 us
  local copies, waits for them, and re-layouts: 92.3 us -> 13.7 us
  waiting for transfers between devices: 147 us -> 68.4 us
  other arithmetic: 33.2 us -> 10.8 us
  between operations: 16.3 us -> 0.77 us
  starting transfers between devices: 22.2 us -> 30.3 us
    all_gather x3 -> x0, blocking collectives: 253 us -> none  [the longest x1 184 us: shards(): lax.all_gather(group_scales, 'intra', axis=0, tiled=True)]
    unnamed x3 -> x0, waiting for transfers between devices: 147 us -> none
    all_to_all x1 -> x5, waiting for transfers between devices: 0.01 us -> 68.4 us  [exchange(): return lax.all_to_all(blocks, axis, split_axis=0, concat_axis=0, tiled=True)]
    all_to_all x0 -> x2, blocking collectives: none -> 48.3 us  [exchange(): return lax.all_to_all(blocks, axis, split_axis=0, concat_axis=0, tiled=True)]
    unnamed x22 -> x11, local copies, waits for them, and re-layouts: 45.6 us -> 3.52 us
    broadcast_in_dim x1 -> x5, local copies, waits for them, and re-layouts: 36.5 us -> 2.53 us  [the longest x2 1.65 us: gather_weight(): by_x = exchange(jnp.broadcast_to(rows[None], (4, 512, KV)), ('xh', 'xl'))]
    unnamed x1 -> x0, other arithmetic: 28.5 us -> none
    mul x1 -> x0, local copies, waits for them, and re-layouts: 9.49 us -> none  [dequantize(): scaled = blocks * scales.astype(jnp.float32)[:, :, None]]
  transfers between devices with their start and end apart: 3 -> 6, of which waited for: 1 -> 5; matrix products, arithmetic and copies ran while one was open for 4% -> 9% of each run, Pallas kernels for 0% -> 0%
where the time goes in v1:
time: 181 us; the launch traced here: 177 us
  waiting for transfers between devices  68.4 us (38%)
  blocking collectives  48.3 us (27%)
  starting transfers between devices  30.3 us (17%)
  local copies, waits for them, and re-layouts  13.7 us (8%)
  other arithmetic  10.8 us (6%)
  matrix products  4.72 us (3%)
    all_to_all x5, waiting for transfers between devices, exchange(): return lax.all_to_all(blocks, axis, split_axis=0, concat_axis=0, tiled=True)  68.4 us
    all_to_all x2, blocking collectives, exchange(): return lax.all_to_all(blocks, axis, split_axis=0, concat_axis=0, tiled=True)  48.3 us
    all_to_all x5, starting transfers between devices, exchange(): return lax.all_to_all(blocks, axis, split_axis=0, concat_axis=0, tiled=True)  26.9 us
    convert_element_type x1, other arithmetic, scatter_sum(): total = (by_c[0].astype(F32) + by_c[1].astype(F32)).astype(BF16)  4.14 us
  transfers between devices with their start and end apart: 6, of which 5 were waited for; matrix products, arithmetic and copies ran while one was open for 9% of the time, Pallas kernels for 0%

profile of v1, /device:TPU:1, one launch (start us, length us, event | category | flops | bytes accessed | tf_op | source)
XLA Modules:
  0.0 177.2 jit_solution(14811395379920258577)
XLA Ops:
  0.6 0.0 copy-start
  0.6 0.8 convert_element_type.49
  1.4 0.1 broadcast_bitcast_fusion
  1.5 0.7 fusion.2
  2.2 30.8 %all_to_all.35 = bf16[16,4,512]{2,1,0:T(4,128)(2,1)S(1)} all-to-all(bf16[16,4,512]{2,1,0:T(4,128)(2,1)S(1)} %broadcast_in_dim.10), channel_id=1, replica_groups=mesh['xh'=2,'y'=8,'xl'=2,'z'=16,'c'=2] {'z'}, dimensions={0} | all-to-all | bytes 131072 | tf_op jit(solution)/shard_map/all_to_all | solution.py:24
  33.0 0.8 broadcast_in_dim.23
  33.9 6.8 %all-to-all-start.1 = ((bf16[8,64,512]{2,1,0:T(8,128)(2,1)}), bf16[8,64,512]{2,1,0:T(8,128)(2,1)S(1)}, u32[]{:S(2)}, u32[]{:S(2)}) async-start(bf16[8,64,512]{2,1,0:T(8,128)(2,1)} %broadcast_in_dim.23), calls=%async_computation.1 | async-start | bytes 1048576 | tf_op jit(solution)/shard_map/all_to_all | solution.py:24
  40.7 0.0 copy-done
  40.7 2.2 %convolution_convert_fusion = bf16[4096,512]{1,0:T(8,128)(2,1)S(1)} fusion(bf16[128,4096]{1,0:T(8,128)(2,1)S(1)} %copy-done, bf16[128,512]{1,0:T(8,128)(2,1)} %param.5), kind=kOutput, calls=%fused_computation | convolution fusion | flops 538968064 | bytes 5373952 | tf_op jit(solution)/shard_map/dot_general | solution.py:55
  42.9 2.5 %copy.55 = bf16[2,16,2,2,32,512]{5,4,1,0,3,2:T(8,128)(2,1)} copy(bf16[2,16,2,2,32,512]{5,4,3,2,1,0:T(8,128)(2,1)S(1)} %bitcast.34) | data formatting | bytes 8388608 | tf_op jit(solution)/shard_map/reshape | solution.py:41
  45.3 10.4 %all-to-all-done.1 = bf16[8,64,512]{2,1,0:T(8,128)(2,1)S(1)} async-done(((bf16[8,64,512]{2,1,0:T(8,128)(2,1)}), bf16[8,64,512]{2,1,0:T(8,128)(2,1)S(1)}, u32[]{:S(2)}, u32[]{:S(2)}) %all-to-all-start.1) | async-done | bytes 524320 | tf_op jit(solution)/shard_map/all_to_all | solution.py:24
  55.8 9.0 %all-to-all-start.3 = ((bf16[2,2048,512]{2,1,0:T(8,128)(2,1)}), bf16[2,2048,512]{2,1,0:T(8,128)(2,1)}, u32[]{:S(2)}, u32[]{:S(2)}) async-start(bf16[2,2048,512]{2,1,0:T(8,128)(2,1)} %bitcast.37), calls=%async_computation.3 | async-start | bytes 8388608 | tf_op jit(solution)/shard_map/all_to_all | solution.py:24
  64.7 0.3 copy.52
  65.0 0.3 copy.53
  65.3 0.1 broadcast_in_dim.24
  65.4 3.4 %all-to-all-done.3 = bf16[2,2048,512]{2,1,0:T(8,128)(2,1)} async-done(((bf16[2,2048,512]{2,1,0:T(8,128)(2,1)}), bf16[2,2048,512]{2,1,0:T(8,128)(2,1)}, u32[]{:S(2)}, u32[]{:S(2)}) %all-to-all-start.3) | async-done | bytes 4194336 | tf_op jit(solution)/shard_map/all_to_all | solution.py:24
  68.9 1.5 broadcast_in_dim.25
  70.4 4.0 %all-to-all-start.2 = ((bf16[4,512,512]{2,1,0:T(8,128)(2,1)}), bf16[4,512,512]{2,1,0:T(8,128)(2,1)S(1)}, u32[]{:S(2)}, u32[]{:S(2)}) async-start(bf16[4,512,512]{2,1,0:T(8,128)(2,1)} %broadcast_in_dim.25), calls=%async_computation.2 | async-start | bytes 4194304 | tf_op jit(solution)/shard_map/all_to_all | solution.py:24
  74.4 4.1 %add_convert_fusion = bf16[1,2048,512]{2,1,0:T(8,128)(2,1)} fusion(bf16[2,2048,512]{2,1,0:T(8,128)(2,1)} %all-to-all-done.3), kind=kLoop, calls=%fused_computation.4 | loop fusion | flops 4194304 | bytes 6291456 | tf_op jit(solution)/shard_map/convert_element_type | solution.py:43
  78.5 21.6 %all-to-all-done.2 = bf16[4,512,512]{2,1,0:T(8,128)(2,1)S(1)} async-done(((bf16[4,512,512]{2,1,0:T(8,128)(2,1)}), bf16[4,512,512]{2,1,0:T(8,128)(2,1)S(1)}, u32[]{:S(2)}, u32[]{:S(2)}) %all-to-all-start.2) | async-done | bytes 2097184 | tf_op jit(solution)/shard_map/all_to_all | solution.py:24
  100.2 0.0 copy-start.1
  100.2 1.3 copy-done.1
  101.5 3.6 %all-to-all-start.4 = ((bf16[4,512,512]{2,1,0:T(8,128)(2,1)}), bf16[4,512,512]{2,1,0:T(8,128)(2,1)S(1)}, u32[]{:S(2)}, u32[]{:S(2)}) async-start(bf16[4,512,512]{2,1,0:T(8,128)(2,1)} %bitcast.12), calls=%async_computation.4 | async-start | bytes 4194304 | tf_op jit(solution)/shard_map/all_to_all | solution.py:24
  105.1 3.4 %collective-permute-start = (bf16[2048,512]{1,0:T(8,128)(2,1)}, bf16[2048,512]{1,0:T(8,128)(2,1)}, u32[]{:S(2)}, u32[]{:S(2)}) collective-permute-start(bf16[2048,512]{1,0:T(8,128)(2,1)} %bitcast.38), channel_id=1, source_target_pairs={{0,1},{1,0},{2,3},{3,2},{4,5},{5,4},{6,7},{7,6},{8,9},{9,8},{10,11... | collective-permute-start | bytes 6291464 | tf_op jit(solution)/shard_map/ppermute | solution.py:33
  108.6 21.4 %all-to-all-done.4 = bf16[4,512,512]{2,1,0:T(8,128)(2,1)S(1)} async-done(((bf16[4,512,512]{2,1,0:T(8,128)(2,1)}), bf16[4,512,512]{2,1,0:T(8,128)(2,1)S(1)}, u32[]{:S(2)}, u32[]{:S(2)}) %all-to-all-start.4) | async-done | bytes 2097184 | tf_op jit(solution)/shard_map/all_to_all | solution.py:24
  129.9 1.2 reduce_sum.33
  131.2 0.0 copy-start.2
  131.2 2.1 %reshape.54 = bf16[16,8,4,512]{3,2,1,0:T(4,128)(2,1)} reshape(bf16[512,512]{1,0:T(8,128)(2,1)} %reduce_sum.33) | data formatting | bytes 1048576 | tf_op jit(solution)/shard_map/reshape | solution.py:46
  133.3 1.1 copy.56
  134.4 0.2 copy.57
  134.6 17.6 %all_to_all.36 = bf16[8,64,512]{2,1,0:T(8,128)(2,1)} all-to-all(bf16[8,64,512]{2,1,0:T(8,128)(2,1)S(1)} %copy.57), channel_id=1, replica_groups=mesh['xh'=2,'y'=8,'xl'=2,'z'=16,'c'=2] {'y'}, dimensions={0} | all-to-all | bytes 1048576 | tf_op jit(solution)/shard_map/all_to_all | solution.py:24
  152.1 1.1 reduce_sum.34
  153.3 0.7 reshape.56
  153.9 3.5 %all-to-all-start.6 = ((bf16[16,4,512]{2,1,0:T(4,128)(2,1)}), bf16[16,4,512]{2,1,0:T(4,128)(2,1)S(1)}, u32[]{:S(2)}, u32[]{:S(2)}) async-start(bf16[16,4,512]{2,1,0:T(4,128)(2,1)} %reshape.56), calls=%async_computation.6 | async-start | bytes 131072 | tf_op jit(solution)/shard_map/all_to_all | solution.py:24
  157.4 11.6 %all-to-all-done.6 = bf16[16,4,512]{2,1,0:T(4,128)(2,1)S(1)} async-done(((bf16[16,4,512]{2,1,0:T(4,128)(2,1)}), bf16[16,4,512]{2,1,0:T(4,128)(2,1)S(1)}, u32[]{:S(2)}, u32[]{:S(2)}) %all-to-all-start.6) | async-done | bytes 65568 | tf_op jit(solution)/shard_map/all_to_all | solution.py:24
  169.0 0.6 convert_reduce_fusion
  169.7 0.0 collective-permute-done
  169.7 0.0 copy-done.2
  169.7 1.9 %broadcast_select_fusion.1 = (bf16[2048,512]{1,0:T(8,128)(2,1)S(1)}, bf16[2048,512]{1,0:T(8,128)(2,1)S(1)}) fusion(bf16[2048,512]{1,0:T(8,128)(2,1)} %collective-permute-done, pred[]{:T(512)S(6)} %eq.3, bf16[4,512,512]{2,1,0:T(8,128)(2,1)S(1)} %copy-done.2), kind=kLoop, calls=%fused_computation.6 | loop fusion | flops 2097152 | bytes 8388609 | tf_op jit(solution)/shard_map/jit(_where)/select_n | solution.py:35
  171.5 0.4 maximum_bitcast_fusion
  171.9 0.6 copy.54
  172.5 0.0 copy-start.3
  172.5 1.3 fusion.1
  173.8 0.0 copy-done.3
  173.8 1.3 fusion
  175.1 1.3 copy.60
  176.4 0.8 copy.59
  (2 shorter events, 0.0 us)
Async XLA Ops:
  0.6 40.0 %copy-start = (bf16[128,4096]{1,0:T(8,128)(2,1)S(1)}, bf16[128,4096]{1,0:T(8,128)(2,1)}, u32[]{:S(2)}) copy-start(bf16[128,4096]{1,0:T(8,128)(2,1)} %param.4) | copy-start | bytes 3145732
  33.9 21.9 %all-to-all-start.1 = ((bf16[8,64,512]{2,1,0:T(8,128)(2,1)}), bf16[8,64,512]{2,1,0:T(8,128)(2,1)S(1)}, u32[]{:S(2)}, u32[]{:S(2)}) async-start(bf16[8,64,512]{2,1,0:T(8,128)(2,1)} %broadcast_in_dim.23), calls=%async_computation.1 | async-start | bytes 1048576 | tf_op jit(solution)/shard_map/all_to_all | solution.py:24
  55.8 13.1 %all-to-all-start.3 = ((bf16[2,2048,512]{2,1,0:T(8,128)(2,1)}), bf16[2,2048,512]{2,1,0:T(8,128)(2,1)}, u32[]{:S(2)}, u32[]{:S(2)}) async-start(bf16[2,2048,512]{2,1,0:T(8,128)(2,1)} %bitcast.37), calls=%async_computation.3 | async-start | bytes 8388608 | tf_op jit(solution)/shard_map/all_to_all | solution.py:24
  70.4 29.8 %all-to-all-start.2 = ((bf16[4,512,512]{2,1,0:T(8,128)(2,1)}), bf16[4,512,512]{2,1,0:T(8,128)(2,1)S(1)}, u32[]{:S(2)}, u32[]{:S(2)}) async-start(bf16[4,512,512]{2,1,0:T(8,128)(2,1)} %broadcast_in_dim.25), calls=%async_computation.2 | async-start | bytes 4194304 | tf_op jit(solution)/shard_map/all_to_all | solution.py:24
  100.2 1.3 copy-start.1
  101.5 28.4 %all-to-all-start.4 = ((bf16[4,512,512]{2,1,0:T(8,128)(2,1)}), bf16[4,512,512]{2,1,0:T(8,128)(2,1)S(1)}, u32[]{:S(2)}, u32[]{:S(2)}) async-start(bf16[4,512,512]{2,1,0:T(8,128)(2,1)} %bitcast.12), calls=%async_computation.4 | async-start | bytes 4194304 | tf_op jit(solution)/shard_map/all_to_all | solution.py:24
  105.1 64.5 %collective-permute-start = (bf16[2048,512]{1,0:T(8,128)(2,1)}, bf16[2048,512]{1,0:T(8,128)(2,1)}, u32[]{:S(2)}, u32[]{:S(2)}) collective-permute-start(bf16[2048,512]{1,0:T(8,128)(2,1)} %bitcast.38), channel_id=1, source_target_pairs={{0,1},{1,0},{2,3},{3,2},{4,5},{5,4},{6,7},{7,6},{8,9},{9,8},{10,11... | collective-permute-start | bytes 6291464 | tf_op jit(solution)/shard_map/ppermute | solution.py:33
  131.2 38.5 %copy-start.2 = (bf16[4,512,512]{2,1,0:T(8,128)(2,1)S(1)}, bf16[4,512,512]{2,1,0:T(8,128)(2,1)}, u32[]{:S(2)}) copy-start(bf16[4,512,512]{2,1,0:T(8,128)(2,1)} %copy-done.1) | copy-start | bytes 6291460
  153.9 15.1 %all-to-all-start.6 = ((bf16[16,4,512]{2,1,0:T(4,128)(2,1)}), bf16[16,4,512]{2,1,0:T(4,128)(2,1)S(1)}, u32[]{:S(2)}, u32[]{:S(2)}) async-start(bf16[16,4,512]{2,1,0:T(4,128)(2,1)} %reshape.56), calls=%async_computation.6 | async-start | bytes 131072 | tf_op jit(solution)/shard_map/all_to_all | solution.py:24
  172.5 1.3 copy-start.3

commit v2 on v1

v2 whole, which is shorter than its diff:
```python
import jax
import jax.numpy as jnp
from jax import lax
from jax.experimental import pallas as pl
from jax.experimental.pallas import tpu as pltpu
from jax.sharding import Mesh, PartitionSpec as P

KV = 512
BLOCK = 128
TOK = 128
NY = 8
NZ = 16
ROWS = 4
HALF = NZ * NY * ROWS
SLICE = 2 * HALF
PAY = SLICE + KV
INTER = ("xh", "y")
INTRA = ("xl", "z", "c")
F32 = jnp.float32
BF16 = jnp.bfloat16
INTERPRET = False
SWAP = [(0, 1), (1, 0)]
NN = (((1,), (0,)), ((), ()))
NT = (((1,), (1,)), ((), ()))
TN = (((0,), (0,)), ((), ()))


def dot(a, b, dims):
    return lax.dot_general(a, b, dims, preferred_element_type=F32)


def iota(shape, dim):
    return lax.broadcasted_iota(jnp.int32, shape, dim)


def one_hot(hit):
    return jnp.where(hit, 1.0, 0.0).astype(BF16)


def x_split(xh):
    row, lane = iota((128, 128), 0), iota((128, 128), 1)
    c, q = (row >> 5) & 1, row & 31
    half = jnp.where(row < 64, xh, 1 - xh)
    return one_hot(lane == c * 64 + half * 32 + q)


def y_outer():
    row, col = iota((HALF, HALF), 0), iota((HALF, HALF), 1)
    r = row & (ROWS - 1)
    z = (row >> 2) & (NZ - 1)
    y = row // (NZ * ROWS)
    return one_hot(col == z * (NY * ROWS) + y * ROWS + r)


def eye():
    return one_hot(iota((128, 128), 0) == iota((128, 128), 1))


def prepare(tok_ref, grad_ref, *outs):
    xh, xl = lax.axis_index("xh"), lax.axis_index("xl")
    split = x_split(xh)
    for kl in range(2):
        col = (xl if kl == 0 else 1 - xl) * (NZ * 128)
        for z in range(NZ):
            block = tok_ref[:, pl.ds(pl.multiple_of(col + z * 128, 128), 128)]
            piece = dot(split, block, NT).astype(BF16)
            for kh in range(2):
                for c in range(2):
                    at = kh * 64 + c * 32
                    outs[2 * kh + kl][pl.ds(c * HALF + z * 32, 32), :] = piece[at : at + 32]
    same = eye()
    for b in range(KV // 128):
        piece = dot(same, grad_ref[:, b * 128 : (b + 1) * 128], NT).astype(BF16)
        for out in outs:
            out[pl.ds(SLICE + b * 128, 128), :] = piece


def partial_sums(r0, r1, r2, r3, keep, send):
    c = lax.axis_index("c")
    refs = (r0, r1, r2, r3)
    grads = jnp.concatenate([r[SLICE:, :] for r in refs], axis=1)
    for out, half in ((send, 1 - c), (keep, c)):
        at = pl.ds(pl.multiple_of(half * HALF, HALF), HALF)
        rows = jnp.concatenate([r[at, :] for r in refs], axis=1)
        out[...] = dot(rows, grads, NT).astype(BF16)


def add_cores(a, b, out):
    total = (a[...].astype(F32) + b[...].astype(F32)).astype(BF16)
    out[...] = dot(y_outer(), total, NN).astype(BF16)


def apply_weight(own, other, r0, r1, r2, r3, o0, o1, o2, o3, weight):
    c = lax.axis_index("c")
    refs, outs = (r0, r1, r2, r3), (o0, o1, o2, o3)
    order = y_outer()
    for ref, half in ((own, c), (other, 1 - c)):
        at = pl.ds(pl.multiple_of(half * HALF, HALF), HALF)
        weight[at, :] = dot(order, ref[...], TN).astype(BF16)
    w = weight[...]
    grads = jnp.concatenate([r[SLICE:, :] for r in refs], axis=1)
    back = dot(w, grads, NN).astype(BF16)
    for k, out in enumerate(outs):
        out[:SLICE, :] = back[:, k * TOK : (k + 1) * TOK]
    rows = jnp.concatenate([r[:SLICE, :] for r in refs], axis=1)
    keys = dot(w, rows, TN).astype(BF16)
    for k, out in enumerate(outs):
        out[SLICE:, :] = keys[:, k * TOK : (k + 1) * TOK]


def finish(f0, f1, f2, f3, keys, input_grad):
    xh, xl = lax.axis_index("xh"), lax.axis_index("xl")
    refs = (f0, f1, f2, f3)
    same, split = eye(), x_split(xh)
    for b in range(KV // 128):
        at = pl.ds(SLICE + b * 128, 128)
        total = sum(r[at, :].astype(F32) for r in refs).astype(BF16)
        keys[:, b * 128 : (b + 1) * 128] = dot(total, same, TN).astype(BF16)
    for kl in range(2):
        col = (xl if kl == 0 else 1 - xl) * (NZ * 128)
        for z in range(NZ):
            piece = jnp.concatenate(
                [
                    refs[2 * kh + kl][pl.ds(c * HALF + z * 32, 32), :]
                    for kh in range(2)
                    for c in range(2)
                ],
                axis=0,
            )
            block = dot(piece, split, TN).astype(BF16)
            input_grad[:, pl.ds(pl.multiple_of(col + z * 128, 128), 128)] = block


def kernel(body, outs, flops, moved, scratch=()):
    return pl.pallas_call(
        body,
        out_shape=[jax.ShapeDtypeStruct(s, BF16) for s in outs],
        scratch_shapes=list(scratch),
        compiler_params=pltpu.CompilerParams(vmem_limit_bytes=24 * 1024 * 1024),
        cost_estimate=pl.CostEstimate(flops=flops, bytes_accessed=moved, transcendentals=0),
        interpret=INTERPRET,
    )


def dequantize(codes, scales):
    rows = codes.shape[0]
    blocks = codes.astype(F32).reshape(rows, KV // BLOCK, BLOCK)
    scaled = blocks * scales.astype(F32)[:, :, None]
    return scaled.reshape(rows, KV).astype(BF16)


def exchange(blocks, axis):
    return lax.all_to_all(blocks, axis, split_axis=0, concat_axis=0, tiled=True)


def to_members(blocks):
    return (
        blocks[0],
        lax.ppermute(blocks[1], "xl", SWAP),
        lax.ppermute(blocks[2], "xh", SWAP),
        lax.ppermute(blocks[3], ("xh", "xl"), [(0, 3), (1, 2), (2, 1), (3, 0)]),
    )


def shards(tokens, key_grad, codes, scales):
    part = dequantize(codes, scales)
    blocks = kernel(prepare, [(PAY, TOK)] * 4, 1 << 28, 3 << 20)(tokens, key_grad)
    work = to_members(blocks)
    by_z = exchange(jnp.broadcast_to(part[None], (NZ, ROWS, KV)), "z")
    by_z = by_z.reshape(NZ * ROWS, KV)
    by_y = exchange(jnp.broadcast_to(by_z[None], (NY, NZ * ROWS, KV)), "y")
    own = by_y.reshape(HALF, KV)
    other = lax.ppermute(own, "c", SWAP)
    keep, send = kernel(partial_sums, [(HALF, KV)] * 2, 1 << 29, 3 << 20)(*work)
    got = lax.ppermute(send, "c", SWAP)
    (total,) = kernel(add_cores, [(HALF, KV)], 1 << 28, 3 << 19)(keep, got)
    total = exchange(total.reshape(NY, NZ * ROWS, KV), "y")
    total = jnp.sum(total.astype(F32), axis=0).astype(BF16)
    total = exchange(total.reshape(NZ, ROWS, KV), "z")
    weight_grad = jnp.sum(total.astype(F32), axis=0)
    results = kernel(
        apply_weight, [(PAY, TOK)] * 4, 1 << 30, 4 << 20, [pltpu.VMEM((SLICE, KV), BF16)]
    )(own, other, *work)
    results = to_members(results)
    d_in = 4 * SLICE
    keys, input_grad = kernel(finish, [(TOK, KV), (TOK, d_in)], 1 << 28, 3 << 20)(*results)
    return keys, input_grad, weight_grad


def solution(mesh):
    torus = Mesh(mesh.devices.reshape(2, NY, 2, NZ, 2), ("xh", "y", "xl", "z", "c"))
    tokens_over = P(INTER + INTRA, None)
    rows_over = P(INTRA + INTER, None)
    return jax.shard_map(
        shards,
        mesh=torus,
        in_specs=(tokens_over, tokens_over, rows_over, rows_over),
        out_specs=(tokens_over, tokens_over, rows_over),
        check_vma=False,
    )
```

time: 181 us -> 112 us (0.62); the launches traced: 177 us -> 111 us
  waiting for transfers between devices: 68.4 us -> 16.3 us
  starting transfers between devices: 30.3 us -> 58.3 us
  blocking collectives: 48.3 us -> 22.8 us
  local copies, waits for them, and re-layouts: 13.7 us -> 2.83 us
  other arithmetic: 10.8 us -> 3.16 us
  Pallas kernels: 0 us -> 7.19 us
  matrix products: 4.72 us -> 0 us
    all_to_all x5 -> x3, waiting for transfers between devices: 68.4 us -> 1.71 us  [exchange(): return lax.all_to_all(blocks, axis, split_axis=0, concat_axis=0, tiled=True)]
    all_to_all x2 -> x1, blocking collectives: 48.3 us -> 22.8 us  [exchange(): return lax.all_to_all(blocks, axis, split_axis=0, concat_axis=0, tiled=True)]
    ppermute x1 -> x8, starting transfers between devices: 3.43 us -> 25.3 us  [the longest x2 7.63 us: to_members(): lax.ppermute(blocks[2], 'xh', SWAP)]
    ppermute x1 -> x8, waiting for transfers between devices: 0.01 us -> 14.6 us  [the longest x2 6.66 us: to_members(): lax.ppermute(blocks[3], ('xh', 'xl'), [(0, 3), (1, 2), (2, 1), (3, 0)])]
    pallas_call x0 -> x5, Pallas kernels: none -> 7.19 us  [the longest x1 2.69 us: shards(): kernel(apply_weight, [(PAY, TOK)] * 4, 1 << 30, 4 << 20, [pltpu.VMEM((SLI...]
    all_to_all x5 -> x3, starting transfers between devices: 26.9 us -> 33.1 us  [exchange(): return lax.all_to_all(blocks, axis, split_axis=0, concat_axis=0, tiled=True)]
    reshape x4 -> x1, local copies, waits for them, and re-layouts: 5.41 us -> 0.02 us  [shards(): total = exchange(total.reshape(NZ, ROWS, KV), 'z')]
    dot_general x3 -> x0, matrix products: 4.72 us -> none  [the longest x1 2.17 us: shards(): lax.dot_general(tokens, key_grad, (((0,), (0,)), ((), ())), preferred_ele...]
  transfers between devices with their start and end apart: 6 -> 11, of which waited for: 5 -> 5; matrix products, arithmetic and copies ran while one was open for 9% -> 2% of each run, Pallas kernels for 0% -> 5%
where the time goes in v2:
time: 112 us; the launch traced here: 111 us
  starting transfers between devices  58.3 us (52%)
  blocking collectives  22.8 us (20%)
  waiting for transfers between devices  16.3 us (15%)
  Pallas kernels  7.19 us (6%)
  other arithmetic  3.16 us (3%)
  local copies, waits for them, and re-layouts  2.83 us (3%)
    all_to_all x3, starting transfers between devices, exchange(): return lax.all_to_all(blocks, axis, split_axis=0, concat_axis=0, tiled=True)  33.1 us
    all_to_all x1, blocking collectives, exchange(): return lax.all_to_all(blocks, axis, split_axis=0, concat_axis=0, tiled=True)  22.8 us
    ppermute x2, starting transfers between devices, to_members(): lax.ppermute(blocks[2], 'xh', SWAP)  7.63 us
    ppermute x2, waiting for transfers between devices, to_members(): lax.ppermute(blocks[3], ('xh', 'xl'), [(0, 3), (1, 2), (2, 1), (3, 0)])  6.66 us
    ppermute x2, starting transfers between devices, to_members(): lax.ppermute(blocks[3], ('xh', 'xl'), [(0, 3), (1, 2), (2, 1), (3, 0)])  6.5 us
    ppermute x2, starting transfers between devices, to_members(): lax.ppermute(blocks[1], 'xl', SWAP)  5.03 us
    ppermute x2, waiting for transfers between devices, to_members(): lax.ppermute(blocks[2], 'xh', SWAP)  4.92 us
    ppermute x1, starting transfers between devices, shards(): got = lax.ppermute(send, 'c', SWAP)  3.58 us
  transfers between devices with their start and end apart: 11, of which 5 were waited for; matrix products, arithmetic and copies ran while one was open for 2% of the time, Pallas kernels for 5%

profile of v2, /device:TPU:1, one launch (start us, length us, event | category | flops | bytes accessed | tf_op | source)
XLA Modules:
  0.0 111.4 jit_solution(11045115844724692866)
XLA Ops:
  0.6 0.0 copy-start.1
  0.6 0.7 convert_element_type.15
  1.4 0.1 broadcast_bitcast_fusion
  1.4 0.7 fusion
  2.1 0.7 broadcast_in_dim.6
  2.8 19.4 %all-to-all-start = ((bf16[16,4,512]{2,1,0:T(4,128)(2,1)}), bf16[16,4,512]{2,1,0:T(4,128)(2,1)S(1)}, u32[]{:S(2)}, u32[]{:S(2)}) async-start(bf16[16,4,512]{2,1,0:T(4,128)(2,1)} %broadcast_in_dim.6), calls=%async_computation | async-start | bytes 131072 | tf_op jit(solution)/shard_map/all_to_all | solution.py:153
  22.2 0.0 copy-done.1
  22.2 0.0 copy-start
  22.2 1.2 %copy-done = bf16[128,4096]{1,0:T(8,128)(2,1)S(1)} copy-done((bf16[128,4096]{1,0:T(8,128)(2,1)S(1)}, bf16[128,4096]{1,0:T(8,128)(2,1)}, u32[]{:S(2)}) %copy-start) | copy-done | bytes 1048600
  23.4 0.9 shard_map.67
  24.4 3.1 %collective-permute-start.1 = (bf16[1536,128]{1,0:T(8,128)(2,1)S(1)}, bf16[1536,128]{1,0:T(8,128)(2,1)S(1)}, u32[]{:S(2)}, u32[]{:S(2)}) collective-permute-start(bf16[1536,128]{1,0:T(8,128)(2,1)S(1)} %get-tuple-element.16), channel_id=1, source_target_pairs={{0,32},{32,0},{1,33},{33,1},{2,34},{34,2},{3,35},{35,3},{4,36},{36... | collective-permute-start | bytes 1179656 | tf_op jit(solution)/shard_map/ppermute | solution.py:159
  27.5 4.4 %collective-permute-start.2 = (bf16[1536,128]{1,0:T(8,128)(2,1)S(1)}, bf16[1536,128]{1,0:T(8,128)(2,1)S(1)}, u32[]{:S(2)}, u32[]{:S(2)}) collective-permute-start(bf16[1536,128]{1,0:T(8,128)(2,1)S(1)} %get-tuple-element.17), channel_id=1, source_target_pairs={{0,512},{512,0},{1,513},{513,1},{2,514},{514,2},{3,515},{515,3},{4... | collective-permute-start | bytes 1179656 | tf_op jit(solution)/shard_map/ppermute | solution.py:160
  31.9 2.1 %collective-permute-start.3 = (bf16[1536,128]{1,0:T(8,128)(2,1)S(1)}, bf16[1536,128]{1,0:T(8,128)(2,1)S(1)}, u32[]{:S(2)}, u32[]{:S(2)}) collective-permute-start(bf16[1536,128]{1,0:T(8,128)(2,1)S(1)} %get-tuple-element.18), channel_id=1, source_target_pairs={{0,544},{32,512},{512,32},{544,0},{1,545},{33,513},{513,33},{545,1... | collective-permute-start | bytes 1179656 | tf_op jit(solution)/shard_map/ppermute | solution.py:161
  34.0 0.0 all-to-all-done
  34.0 0.8 broadcast_in_dim.16
  34.9 6.8 %all-to-all-start.1 = ((bf16[8,64,512]{2,1,0:T(8,128)(2,1)}), bf16[8,64,512]{2,1,0:T(8,128)(2,1)S(1)}, u32[]{:S(2)}, u32[]{:S(2)}) async-start(bf16[8,64,512]{2,1,0:T(8,128)(2,1)} %broadcast_in_dim.16), calls=%async_computation.1 | async-start | bytes 1048576 | tf_op jit(solution)/shard_map/all_to_all | solution.py:153
  41.7 0.0 collective-permute-done.1.r1
  41.7 4.9 %collective-permute-done.2.r2 = bf16[1536,128]{1,0:T(8,128)(2,1)S(1)} collective-permute-done((bf16[1536,128]{1,0:T(8,128)(2,1)S(1)}, bf16[1536,128]{1,0:T(8,128)(2,1)S(1)}, u32[]{:S(2)}, u32[]{:S(2)}) %collective-permute-start.2) | collective-permute-done | bytes 393248 | tf_op jit(solution)/shard_map/ppermute | solution.py:160
  46.6 6.7 %collective-permute-done.3.r3 = bf16[1536,128]{1,0:T(8,128)(2,1)S(1)} collective-permute-done((bf16[1536,128]{1,0:T(8,128)(2,1)S(1)}, bf16[1536,128]{1,0:T(8,128)(2,1)S(1)}, u32[]{:S(2)}, u32[]{:S(2)}) %collective-permute-start.3) | collective-permute-done | bytes 393248 | tf_op jit(solution)/shard_map/ppermute | solution.py:161
  53.3 0.7 shard_map.70
  54.0 3.6 %collective-permute-start.7 = (bf16[512,512]{1,0:T(8,128)(2,1)S(1)}, bf16[512,512]{1,0:T(8,128)(2,1)S(1)}, u32[]{:S(2)}, u32[]{:S(2)}) collective-permute-start(bf16[512,512]{1,0:T(8,128)(2,1)S(1)} %get-tuple-element.26), channel_id=1, source_target_pairs={{0,1},{1,0},{2,3},{3,2},{4,5},{5,4},{6,7},{7,6},{8,9},{9,8},{10,11... | collective-permute-start | bytes 1572872 | tf_op jit(solution)/shard_map/ppermute | solution.py:175
  57.6 1.5 %collective-permute-done.7.b = bf16[512,512]{1,0:T(8,128)(2,1)S(1)} collective-permute-done((bf16[512,512]{1,0:T(8,128)(2,1)S(1)}, bf16[512,512]{1,0:T(8,128)(2,1)S(1)}, u32[]{:S(2)}, u32[]{:S(2)}) %collective-permute-start.7) | collective-permute-done | bytes 524320 | tf_op jit(solution)/shard_map/ppermute | solution.py:175
  59.1 1.3 %shard_map.71 = bf16[512,512]{1,0:T(8,128)(2,1)} custom-call(bf16[512,512]{1,0:T(8,128)(2,1)S(1)} %get-tuple-element.25.a, bf16[512,512]{1,0:T(8,128)(2,1)S(1)} %collective-permute-done.7.b), custom_call_target="tpu_custom_call" | custom-call | flops 268435456 | bytes 1572864 | tf_op jit(solution)/shard_map/pallas_call | solution.py:176
  60.4 0.0 all-to-all-done.1
  60.4 6.8 %all-to-all-start.2 = ((bf16[8,64,512]{2,1,0:T(8,128)(2,1)}), bf16[8,64,512]{2,1,0:T(8,128)(2,1)}, u32[]{:S(2)}, u32[]{:S(2)}) async-start(bf16[8,64,512]{2,1,0:T(8,128)(2,1)} %bitcast.1), calls=%async_computation.2 | async-start | bytes 1048576 | tf_op jit(solution)/shard_map/all_to_all | solution.py:153
  67.3 2.6 %collective-permute-start = (bf16[512,512]{1,0:T(8,128)(2,1)S(1)}, bf16[512,512]{1,0:T(8,128)(2,1)S(1)}, u32[]{:S(2)}, u32[]{:S(2)}) collective-permute-start(bf16[512,512]{1,0:T(8,128)(2,1)S(1)} %bitcast.8), channel_id=1, source_target_pairs={{0,1},{1,0},{2,3},{3,2},{4,5},{5,4},{6,7},{7,6},{8,9},{9,8},{10,11... | collective-permute-start | bytes 1572872 | tf_op jit(solution)/shard_map/ppermute | solution.py:173
  69.8 1.5 %collective-permute-done.other = bf16[512,512]{1,0:T(8,128)(2,1)S(1)} collective-permute-done((bf16[512,512]{1,0:T(8,128)(2,1)S(1)}, bf16[512,512]{1,0:T(8,128)(2,1)S(1)}, u32[]{:S(2)}, u32[]{:S(2)}) %collective-permute-start) | collective-permute-done | bytes 524320 | tf_op jit(solution)/shard_map/ppermute | solution.py:173
  71.3 2.7 %shard_map.68 = (bf16[1536,128]{1,0:T(8,128)(2,1)S(1)}, bf16[1536,128]{1,0:T(8,128)(2,1)}, bf16[1536,128]{1,0:T(8,128)(2,1)S(1)}, bf16[1536,128]{1,0:T(8,128)(2,1)S(1)}) custom-call(bf16[512,512]{1,0:T(8,128)(2,1)S(1)} %bitcast.9, bf16[512,512]{1,0:T(8,128)(2,1)S(1)} %collective-permute-done.other, bf16[1536,128]{1,0:T(8,128)(2,1)S(1)} %get-tuple-element.15.r0, ...), custom_call_target="tpu_custom_call" | custom-call | flops 1073741824 | bytes 4194304 | tf_op jit(solution)/shard_map/pallas_call | solution.py:181
  74.0 1.9 %collective-permute-start.4 = (bf16[1536,128]{1,0:T(8,128)(2,1)}, bf16[1536,128]{1,0:T(8,128)(2,1)S(1)}, u32[]{:S(2)}, u32[]{:S(2)}) collective-permute-start(bf16[1536,128]{1,0:T(8,128)(2,1)} %get-tuple-element.20), channel_id=1, source_target_pairs={{0,32},{32,0},{1,33},{33,1},{2,34},{34,2},{3,35},{35,3},{4,36},{36... | collective-permute-start | bytes 1179656 | tf_op jit(solution)/shard_map/ppermute | solution.py:159
  75.9 3.3 %collective-permute-start.5 = (bf16[1536,128]{1,0:T(8,128)(2,1)S(1)}, bf16[1536,128]{1,0:T(8,128)(2,1)S(1)}, u32[]{:S(2)}, u32[]{:S(2)}) collective-permute-start(bf16[1536,128]{1,0:T(8,128)(2,1)S(1)} %get-tuple-element.21), channel_id=1, source_target_pairs={{0,512},{512,0},{1,513},{513,1},{2,514},{514,2},{3,515},{515,3},{4... | collective-permute-start | bytes 1179656 | tf_op jit(solution)/shard_map/ppermute | solution.py:160
  79.2 4.4 %collective-permute-start.6 = (bf16[1536,128]{1,0:T(8,128)(2,1)S(1)}, bf16[1536,128]{1,0:T(8,128)(2,1)S(1)}, u32[]{:S(2)}, u32[]{:S(2)}) collective-permute-start(bf16[1536,128]{1,0:T(8,128)(2,1)S(1)} %get-tuple-element.22), channel_id=1, source_target_pairs={{0,544},{32,512},{512,32},{544,0},{1,545},{33,513},{513,33},{545,1... | collective-permute-start | bytes 1179656 | tf_op jit(solution)/shard_map/ppermute | solution.py:161
  83.6 1.7 %all-to-all-done.2 = bf16[8,64,512]{2,1,0:T(8,128)(2,1)} async-done(((bf16[8,64,512]{2,1,0:T(8,128)(2,1)}), bf16[8,64,512]{2,1,0:T(8,128)(2,1)}, u32[]{:S(2)}, u32[]{:S(2)}) %all-to-all-start.2) | async-done | bytes 524320 | tf_op jit(solution)/shard_map/all_to_all | solution.py:153
  85.3 1.1 %reduce_sum.21 = bf16[64,512]{1,0:T(8,128)(2,1)S(1)} reduce(bf16[8,64,512]{2,1,0:T(8,128)(2,1)} %all-to-all-done.2, bf16[]{:T(256)} %constant.2.clone.1), dimensions={0}, to_apply=%region_0.0 | reduce | flops 229376 | bytes 589826 | tf_op jit(solution)/shard_map/reduce_sum | solution.py:178
  86.5 22.8 %all_to_all.20 = bf16[16,4,512]{2,1,0:T(4,128)(2,1)S(1)} all-to-all(bf16[16,4,512]{2,1,0:T(4,128)(2,1)S(1)} %reshape.23), channel_id=1, replica_groups=mesh['xh'=2,'y'=8,'xl'=2,'z'=16,'c'=2] {'z'}, dimensions={0} | all-to-all | bytes 131072 | tf_op jit(solution)/shard_map/all_to_all | solution.py:153
  109.3 0.6 convert_reduce_fusion
  109.9 0.0 collective-permute-done.4.f1
  109.9 0.0 collective-permute-done.5.f2
  109.9 0.0 collective-permute-done.6.f3
  109.9 1.5 %shard_map.69 = (bf16[128,512]{1,0:T(8,128)(2,1)}, bf16[128,4096]{1,0:T(8,128)(2,1)}) custom-call(bf16[1536,128]{1,0:T(8,128)(2,1)S(1)} %get-tuple-element.19.f0, bf16[1536,128]{1,0:T(8,128)(2,1)S(1)} %collective-permute-done.4.f1, bf16[1536,128]{1,0:T(8,128)(2,1)S(1)} %collective-permute-done.5.f2, bf16[1536,128]{1,0:T(8,128)(2,1)S(1)} %collective-permute-done.6.f3), custom_call_target="tpu_custom_call" | custom-call | flops 268435456 | bytes 3145728 | tf_op jit(solution)/shard_map/pallas_call | solution.py:186
  (2 shorter events, 0.0 us)
Async XLA Ops:
  0.6 21.6 %copy-start.1 = (bf16[128,512]{1,0:T(8,128)(2,1)S(1)}, bf16[128,512]{1,0:T(8,128)(2,1)}, u32[]{:S(2)}) copy-start(bf16[128,512]{1,0:T(8,128)(2,1)} %grad_ref.1) | copy-start | bytes 393220
  2.8 31.2 %all-to-all-start = ((bf16[16,4,512]{2,1,0:T(4,128)(2,1)}), bf16[16,4,512]{2,1,0:T(4,128)(2,1)S(1)}, u32[]{:S(2)}, u32[]{:S(2)}) async-start(bf16[16,4,512]{2,1,0:T(4,128)(2,1)} %broadcast_in_dim.6), calls=%async_computation | async-start | bytes 131072 | tf_op jit(solution)/shard_map/all_to_all | solution.py:153
  22.2 1.2 %copy-start = (bf16[128,4096]{1,0:T(8,128)(2,1)S(1)}, bf16[128,4096]{1,0:T(8,128)(2,1)}, u32[]{:S(2)}) copy-start(bf16[128,4096]{1,0:T(8,128)(2,1)} %tok_ref.1) | copy-start | bytes 3145732
  24.4 17.3 %collective-permute-start.1 = (bf16[1536,128]{1,0:T(8,128)(2,1)S(1)}, bf16[1536,128]{1,0:T(8,128)(2,1)S(1)}, u32[]{:S(2)}, u32[]{:S(2)}) collective-permute-start(bf16[1536,128]{1,0:T(8,128)(2,1)S(1)} %get-tuple-element.16), channel_id=1, source_target_pairs={{0,32},{32,0},{1,33},{33,1},{2,34},{34,2},{3,35},{35,3},{4,36},{36... | collective-permute-start | bytes 1179656 | tf_op jit(solution)/shard_map/ppermute | solution.py:159
  27.5 19.1 %collective-permute-start.2 = (bf16[1536,128]{1,0:T(8,128)(2,1)S(1)}, bf16[1536,128]{1,0:T(8,128)(2,1)S(1)}, u32[]{:S(2)}, u32[]{:S(2)}) collective-permute-start(bf16[1536,128]{1,0:T(8,128)(2,1)S(1)} %get-tuple-element.17), channel_id=1, source_target_pairs={{0,512},{512,0},{1,513},{513,1},{2,514},{514,2},{3,515},{515,3},{4... | collective-permute-start | bytes 1179656 | tf_op jit(solution)/shard_map/ppermute | solution.py:160
  31.9 21.4 %collective-permute-start.3 = (bf16[1536,128]{1,0:T(8,128)(2,1)S(1)}, bf16[1536,128]{1,0:T(8,128)(2,1)S(1)}, u32[]{:S(2)}, u32[]{:S(2)}) collective-permute-start(bf16[1536,128]{1,0:T(8,128)(2,1)S(1)} %get-tuple-element.18), channel_id=1, source_target_pairs={{0,544},{32,512},{512,32},{544,0},{1,545},{33,513},{513,33},{545,1... | collective-permute-start | bytes 1179656 | tf_op jit(solution)/shard_map/ppermute | solution.py:161
  34.9 25.6 %all-to-all-start.1 = ((bf16[8,64,512]{2,1,0:T(8,128)(2,1)}), bf16[8,64,512]{2,1,0:T(8,128)(2,1)S(1)}, u32[]{:S(2)}, u32[]{:S(2)}) async-start(bf16[8,64,512]{2,1,0:T(8,128)(2,1)} %broadcast_in_dim.16), calls=%async_computation.1 | async-start | bytes 1048576 | tf_op jit(solution)/shard_map/all_to_all | solution.py:153
  54.0 5.1 %collective-permute-start.7 = (bf16[512,512]{1,0:T(8,128)(2,1)S(1)}, bf16[512,512]{1,0:T(8,128)(2,1)S(1)}, u32[]{:S(2)}, u32[]{:S(2)}) collective-permute-start(bf16[512,512]{1,0:T(8,128)(2,1)S(1)} %get-tuple-element.26), channel_id=1, source_target_pairs={{0,1},{1,0},{2,3},{3,2},{4,5},{5,4},{6,7},{7,6},{8,9},{9,8},{10,11... | collective-permute-start | bytes 1572872 | tf_op jit(solution)/shard_map/ppermute | solution.py:175
  60.4 24.9 %all-to-all-start.2 = ((bf16[8,64,512]{2,1,0:T(8,128)(2,1)}), bf16[8,64,512]{2,1,0:T(8,128)(2,1)}, u32[]{:S(2)}, u32[]{:S(2)}) async-start(bf16[8,64,512]{2,1,0:T(8,128)(2,1)} %bitcast.1), calls=%async_computation.2 | async-start | bytes 1048576 | tf_op jit(solution)/shard_map/all_to_all | solution.py:153
  67.3 4.1 %collective-permute-start = (bf16[512,512]{1,0:T(8,128)(2,1)S(1)}, bf16[512,512]{1,0:T(8,128)(2,1)S(1)}, u32[]{:S(2)}, u32[]{:S(2)}) collective-permute-start(bf16[512,512]{1,0:T(8,128)(2,1)S(1)} %bitcast.8), channel_id=1, source_target_pairs={{0,1},{1,0},{2,3},{3,2},{4,5},{5,4},{6,7},{7,6},{8,9},{9,8},{10,11... | collective-permute-start | bytes 1572872 | tf_op jit(solution)/shard_map/ppermute | solution.py:173
  74.0 35.9 %collective-permute-start.4 = (bf16[1536,128]{1,0:T(8,128)(2,1)}, bf16[1536,128]{1,0:T(8,128)(2,1)S(1)}, u32[]{:S(2)}, u32[]{:S(2)}) collective-permute-start(bf16[1536,128]{1,0:T(8,128)(2,1)} %get-tuple-element.20), channel_id=1, source_target_pairs={{0,32},{32,0},{1,33},{33,1},{2,34},{34,2},{3,35},{35,3},{4,36},{36... | collective-permute-start | bytes 1179656 | tf_op jit(solution)/shard_map/ppermute | solution.py:159
  75.9 34.0 %collective-permute-start.5 = (bf16[1536,128]{1,0:T(8,128)(2,1)S(1)}, bf16[1536,128]{1,0:T(8,128)(2,1)S(1)}, u32[]{:S(2)}, u32[]{:S(2)}) collective-permute-start(bf16[1536,128]{1,0:T(8,128)(2,1)S(1)} %get-tuple-element.21), channel_id=1, source_target_pairs={{0,512},{512,0},{1,513},{513,1},{2,514},{514,2},{3,515},{515,3},{4... | collective-permute-start | bytes 1179656 | tf_op jit(solution)/shard_map/ppermute | solution.py:160
  79.2 30.7 %collective-permute-start.6 = (bf16[1536,128]{1,0:T(8,128)(2,1)S(1)}, bf16[1536,128]{1,0:T(8,128)(2,1)S(1)}, u32[]{:S(2)}, u32[]{:S(2)}) collective-permute-start(bf16[1536,128]{1,0:T(8,128)(2,1)S(1)} %get-tuple-element.22), channel_id=1, source_target_pairs={{0,544},{32,512},{512,32},{544,0},{1,545},{33,513},{513,33},{545,1... | collective-permute-start | bytes 1179656 | tf_op jit(solution)/shard_map/ppermute | solution.py:161

commit v3 on v2

--- a/solution.py
+++ b/solution.py
@@ -73,6 +73,14 @@
         piece = dot(same, grad_ref[:, b * 128 : (b + 1) * 128], NT).astype(BF16)
         for out in outs:
             out[pl.ds(SLICE + b * 128, 128), :] = piece
+
+
+def scale_rows(codes, scales, later, copies):
+    del later
+    for b in range(KV // BLOCK):
+        at = slice(b * BLOCK, (b + 1) * BLOCK)
+        scaled = codes[:, at].astype(F32) * scales[:, b : b + 1].astype(F32)
+        copies[:, :, at] = jnp.broadcast_to(scaled.astype(BF16)[None], (NZ, ROWS, BLOCK))
 
 
 def partial_sums(r0, r1, r2, r3, keep, send):
@@ -131,22 +139,20 @@
             input_grad[:, pl.ds(pl.multiple_of(col + z * 128, 128), 128)] = block
 
 
-def kernel(body, outs, flops, moved, scratch=()):
+def kernel(body, outs, flops, moved, scratch=(), any_of=None):
+    specs = {}
+    if any_of is not None:
+        whole = [pl.BlockSpec(memory_space=pltpu.VMEM)] * any_of
+        specs = {"in_specs": [*whole, pl.BlockSpec(memory_space=pl.ANY)]}
     return pl.pallas_call(
         body,
+        **specs,
         out_shape=[jax.ShapeDtypeStruct(s, BF16) for s in outs],
         scratch_shapes=list(scratch),
         compiler_params=pltpu.CompilerParams(vmem_limit_bytes=24 * 1024 * 1024),
         cost_estimate=pl.CostEstimate(flops=flops, bytes_accessed=moved, transcendentals=0),
         interpret=INTERPRET,
     )
-
-
-def dequantize(codes, scales):
-    rows = codes.shape[0]
-    blocks = codes.astype(F32).reshape(rows, KV // BLOCK, BLOCK)
-    scaled = blocks * scales.astype(F32)[:, :, None]
-    return scaled.reshape(rows, KV).astype(BF16)
 
 
 def exchange(blocks, axis):
@@ -163,10 +169,14 @@
 
 
 def shards(tokens, key_grad, codes, scales):
-    part = dequantize(codes, scales)
     blocks = kernel(prepare, [(PAY, TOK)] * 4, 1 << 28, 3 << 20)(tokens, key_grad)
     work = to_members(blocks)
-    by_z = exchange(jnp.broadcast_to(part[None], (NZ, ROWS, KV)), "z")
+    (copies,) = kernel(scale_rows, [(NZ, ROWS, KV)], 1 << 12, 1 << 17, any_of=2)(
+        codes, scales, blocks[0]
+    )
+    by_z = exchange(copies, "z")
+    by_z, one, two = lax.optimization_barrier((by_z, work[1], work[2]))
+    work = (work[0], one, two, work[3])
     by_z = by_z.reshape(NZ * ROWS, KV)
     by_y = exchange(jnp.broadcast_to(by_z[None], (NY, NZ * ROWS, KV)), "y")
     own = by_y.reshape(HALF, KV)

time: 112 us -> 109 us (0.973)
  blocking collectives: 22.8 us -> 14.4 us
  waiting for transfers between devices: 16.3 us -> 19.2 us
  starting transfers between devices: 58.3 us -> 60.5 us
  other arithmetic: 3.16 us -> 1.75 us
    all_to_all x3, waiting for transfers between devices: 1.71 us -> 15.5 us  [exchange(): return lax.all_to_all(blocks, axis, split_axis=0, concat_axis=0, tiled=True)]
    all_to_all x1, blocking collectives: 22.8 us -> 14.4 us  [exchange(): return lax.all_to_all(blocks, axis, split_axis=0, concat_axis=0, tiled=True)]
    ppermute x2, waiting for transfers between devices: 6.66 us -> 0.68 us  [to_members(): lax.ppermute(blocks[3], ('xh', 'xl'), [(0, 3), (1, 2), (2, 1), (3, 0)])]
    ppermute x2, waiting for transfers between devices: 4.92 us -> 0.01 us  [to_members(): lax.ppermute(blocks[2], 'xh', SWAP)]
    ppermute x1, starting transfers between devices: 2.55 us -> 5.98 us  [shards(): other = lax.ppermute(own, 'c', SWAP)]
    all_to_all x3, starting transfers between devices: 33.1 us -> 29.7 us  [exchange(): return lax.all_to_all(blocks, axis, split_axis=0, concat_axis=0, tiled=True)]
    convert_element_type x2 -> x0, other arithmetic: 1.41 us -> none  [the longest x1 0.72 us: dequantize(): scaled = blocks * scales.astype(F32)[:, :, None]]
    ppermute x1, starting transfers between devices: 3.58 us -> 4.91 us  [shards(): got = lax.ppermute(send, 'c', SWAP)]
where the time goes in v3:
time: 109 us; the launch traced here: 108 us
  starting transfers between devices  60.5 us (56%)
  waiting for transfers between devices  19.2 us (18%)
  blocking collectives  14.4 us (13%)
  Pallas kernels  7.92 us (7%)
  local copies, waits for them, and re-layouts  3.01 us (3%)
  other arithmetic  1.75 us (2%)
    all_to_all x3, starting transfers between devices, exchange(): return lax.all_to_all(blocks, axis, split_axis=0, concat_axis=0, tiled=True)  29.7 us
    all_to_all x3, waiting for transfers between devices, exchange(): return lax.all_to_all(blocks, axis, split_axis=0, concat_axis=0, tiled=True)  15.5 us
    all_to_all x1, blocking collectives, exchange(): return lax.all_to_all(blocks, axis, split_axis=0, concat_axis=0, tiled=True)  14.4 us
    ppermute x2, starting transfers between devices, to_members(): lax.ppermute(blocks[2], 'xh', SWAP)  7.52 us
    ppermute x2, starting transfers between devices, to_members(): lax.ppermute(blocks[3], ('xh', 'xl'), [(0, 3), (1, 2), (2, 1), (3, 0)])  6.47 us
    ppermute x2, starting transfers between devices, to_members(): lax.ppermute(blocks[1], 'xl', SWAP)  5.99 us
    ppermute x1, starting transfers between devices, shards(): other = lax.ppermute(own, 'c', SWAP)  5.98 us
    ppermute x1, starting transfers between devices, shards(): got = lax.ppermute(send, 'c', SWAP)  4.91 us
  transfers between devices with their start and end apart: 11, of which 5 were waited for; matrix products, arithmetic and copies ran while one was open for 2% of the time, Pallas kernels for 5%

profile of v3, /device:TPU:1, one launch (start us, length us, event | category | flops | bytes accessed | tf_op | source)
XLA Modules:
  0.0 107.6 jit_solution(217648662993887145)
XLA Ops:
  0.6 0.0 copy-start
  0.6 1.2 %copy-done = bf16[128,4096]{1,0:T(8,128)(2,1)S(1)} copy-done((bf16[128,4096]{1,0:T(8,128)(2,1)S(1)}, bf16[128,4096]{1,0:T(8,128)(2,1)}, u32[]{:S(2)}) %copy-start) | copy-done | bytes 1048600
  1.9 0.0 copy-start.1
  1.9 0.9 copy-done.1
  2.8 0.9 shard_map.67
  3.7 0.0 copy-start.2
  3.7 4.1 %collective-permute-start = (bf16[1536,128]{1,0:T(8,128)(2,1)S(1)}, bf16[1536,128]{1,0:T(8,128)(2,1)S(1)}, u32[]{:S(2)}, u32[]{:S(2)}) collective-permute-start(bf16[1536,128]{1,0:T(8,128)(2,1)S(1)} %get-tuple-element.19), channel_id=1, source_target_pairs={{0,32},{32,0},{1,33},{33,1},{2,34},{34,2},{3,35},{35,3},{4,36},{36... | collective-permute-start | bytes 1179656 | tf_op jit(solution)/shard_map/ppermute | solution.py:165
  7.8 0.0 copy-start.3
  7.8 4.2 %collective-permute-start.1 = (bf16[1536,128]{1,0:T(8,128)(2,1)S(1)}, bf16[1536,128]{1,0:T(8,128)(2,1)S(1)}, u32[]{:S(2)}, u32[]{:S(2)}) collective-permute-start(bf16[1536,128]{1,0:T(8,128)(2,1)S(1)} %get-tuple-element.20), channel_id=1, source_target_pairs={{0,512},{512,0},{1,513},{513,1},{2,514},{514,2},{3,515},{515,3},{4... | collective-permute-start | bytes 1179656 | tf_op jit(solution)/shard_map/ppermute | solution.py:166
  12.1 0.0 copy-done.2
  12.1 0.0 copy-done.3
  12.1 0.7 shard_map.68
  12.8 18.7 %all-to-all-start = ((bf16[16,4,512]{2,1,0:T(4,128)(2,1)}), bf16[16,4,512]{2,1,0:T(4,128)(2,1)S(1)}, u32[]{:S(2)}, u32[]{:S(2)}) async-start(bf16[16,4,512]{2,1,0:T(4,128)(2,1)} %shard_map.68), calls=%async_computation | async-start | bytes 131072 | tf_op jit(solution)/shard_map/all_to_all | solution.py:159
  31.5 2.1 %collective-permute-start.3 = (bf16[1536,128]{1,0:T(8,128)(2,1)S(1)}, bf16[1536,128]{1,0:T(8,128)(2,1)S(1)}, u32[]{:S(2)}, u32[]{:S(2)}) collective-permute-start(bf16[1536,128]{1,0:T(8,128)(2,1)S(1)} %get-tuple-element.24), channel_id=1, source_target_pairs={{0,544},{32,512},{512,32},{544,0},{1,545},{33,513},{513,33},{545,1... | collective-permute-start | bytes 1179656 | tf_op jit(solution)/shard_map/ppermute | solution.py:167
  33.6 9.6 %all-to-all-done = bf16[16,4,512]{2,1,0:T(4,128)(2,1)S(1)} async-done(((bf16[16,4,512]{2,1,0:T(4,128)(2,1)}), bf16[16,4,512]{2,1,0:T(4,128)(2,1)S(1)}, u32[]{:S(2)}, u32[]{:S(2)}) %all-to-all-start) | async-done | bytes 65568 | tf_op jit(solution)/shard_map/all_to_all | solution.py:159
  43.2 0.0 collective-permute-done.r1
  43.2 0.0 collective-permute-done.1.r2
  43.2 0.8 broadcast_in_dim.8
  44.1 6.8 %all-to-all-start.1 = ((bf16[8,64,512]{2,1,0:T(8,128)(2,1)}), bf16[8,64,512]{2,1,0:T(8,128)(2,1)S(1)}, u32[]{:S(2)}, u32[]{:S(2)}) async-start(bf16[8,64,512]{2,1,0:T(8,128)(2,1)} %broadcast_in_dim.8), calls=%async_computation.1 | async-start | bytes 1048576 | tf_op jit(solution)/shard_map/all_to_all | solution.py:159
  50.9 0.0 collective-permute-done.3.r3
  50.9 0.7 shard_map.71
  51.6 4.9 %collective-permute-start.7 = (bf16[512,512]{1,0:T(8,128)(2,1)S(1)}, bf16[512,512]{1,0:T(8,128)(2,1)S(1)}, u32[]{:S(2)}, u32[]{:S(2)}) collective-permute-start(bf16[512,512]{1,0:T(8,128)(2,1)S(1)} %get-tuple-element.32), channel_id=1, source_target_pairs={{0,1},{1,0},{2,3},{3,2},{4,5},{5,4},{6,7},{7,6},{8,9},{9,8},{10,11... | collective-permute-start | bytes 1572872 | tf_op jit(solution)/shard_map/ppermute | solution.py:185
  56.6 1.5 %collective-permute-done.7.b = bf16[512,512]{1,0:T(8,128)(2,1)S(1)} collective-permute-done((bf16[512,512]{1,0:T(8,128)(2,1)S(1)}, bf16[512,512]{1,0:T(8,128)(2,1)S(1)}, u32[]{:S(2)}, u32[]{:S(2)}) %collective-permute-start.7) | collective-permute-done | bytes 524320 | tf_op jit(solution)/shard_map/ppermute | solution.py:185
  58.1 1.3 %shard_map.72 = bf16[512,512]{1,0:T(8,128)(2,1)} custom-call(bf16[512,512]{1,0:T(8,128)(2,1)S(1)} %get-tuple-element.31.a, bf16[512,512]{1,0:T(8,128)(2,1)S(1)} %collective-permute-done.7.b), custom_call_target="tpu_custom_call" | custom-call | flops 268435456 | bytes 1572864 | tf_op jit(solution)/shard_map/pallas_call | solution.py:186
  59.4 5.9 %all-to-all-done.1 = bf16[8,64,512]{2,1,0:T(8,128)(2,1)S(1)} async-done(((bf16[8,64,512]{2,1,0:T(8,128)(2,1)}), bf16[8,64,512]{2,1,0:T(8,128)(2,1)S(1)}, u32[]{:S(2)}, u32[]{:S(2)}) %all-to-all-start.1) | async-done | bytes 524320 | tf_op jit(solution)/shard_map/all_to_all | solution.py:159
  65.3 4.1 %all-to-all-start.2 = ((bf16[8,64,512]{2,1,0:T(8,128)(2,1)}), bf16[8,64,512]{2,1,0:T(8,128)(2,1)}, u32[]{:S(2)}, u32[]{:S(2)}) async-start(bf16[8,64,512]{2,1,0:T(8,128)(2,1)} %bitcast.1), calls=%async_computation.2 | async-start | bytes 1048576 | tf_op jit(solution)/shard_map/all_to_all | solution.py:159
  69.4 6.0 %collective-permute-start.2 = (bf16[512,512]{1,0:T(8,128)(2,1)S(1)}, bf16[512,512]{1,0:T(8,128)(2,1)S(1)}, u32[]{:S(2)}, u32[]{:S(2)}) collective-permute-start(bf16[512,512]{1,0:T(8,128)(2,1)S(1)} %bitcast.2), channel_id=1, source_target_pairs={{0,1},{1,0},{2,3},{3,2},{4,5},{5,4},{6,7},{7,6},{8,9},{9,8},{10,11... | collective-permute-start | bytes 1572872 | tf_op jit(solution)/shard_map/ppermute | solution.py:183
  75.4 1.5 %collective-permute-done.2.other = bf16[512,512]{1,0:T(8,128)(2,1)S(1)} collective-permute-done((bf16[512,512]{1,0:T(8,128)(2,1)S(1)}, bf16[512,512]{1,0:T(8,128)(2,1)S(1)}, u32[]{:S(2)}, u32[]{:S(2)}) %collective-permute-start.2) | collective-permute-done | bytes 524320 | tf_op jit(solution)/shard_map/ppermute | solution.py:183
  76.9 2.7 %shard_map.69 = (bf16[1536,128]{1,0:T(8,128)(2,1)S(1)}, bf16[1536,128]{1,0:T(8,128)(2,1)}, bf16[1536,128]{1,0:T(8,128)(2,1)S(1)}, bf16[1536,128]{1,0:T(8,128)(2,1)S(1)}) custom-call(bf16[512,512]{1,0:T(8,128)(2,1)S(1)} %bitcast.3, bf16[512,512]{1,0:T(8,128)(2,1)S(1)} %collective-permute-done.2.other, bf16[1536,128]{1,0:T(8,128)(2,1)S(1)} %get-tuple-element.18.later.r0, ...), custom_call_target="tpu_custom_call" | custom-call | flops 1073741824 | bytes 4194304 | tf_op jit(solution)/shard_map/pallas_call | solution.py:191
  79.6 1.9 %collective-permute-start.4 = (bf16[1536,128]{1,0:T(8,128)(2,1)}, bf16[1536,128]{1,0:T(8,128)(2,1)S(1)}, u32[]{:S(2)}, u32[]{:S(2)}) collective-permute-start(bf16[1536,128]{1,0:T(8,128)(2,1)} %get-tuple-element.26), channel_id=1, source_target_pairs={{0,32},{32,0},{1,33},{33,1},{2,34},{34,2},{3,35},{35,3},{4,36},{36... | collective-permute-start | bytes 1179656 | tf_op jit(solution)/shard_map/ppermute | solution.py:165
  81.5 3.3 %collective-permute-start.5 = (bf16[1536,128]{1,0:T(8,128)(2,1)S(1)}, bf16[1536,128]{1,0:T(8,128)(2,1)S(1)}, u32[]{:S(2)}, u32[]{:S(2)}) collective-permute-start(bf16[1536,128]{1,0:T(8,128)(2,1)S(1)} %get-tuple-element.27), channel_id=1, source_target_pairs={{0,512},{512,0},{1,513},{513,1},{2,514},{514,2},{3,515},{515,3},{4... | collective-permute-start | bytes 1179656 | tf_op jit(solution)/shard_map/ppermute | solution.py:166
  84.8 4.4 %collective-permute-start.6 = (bf16[1536,128]{1,0:T(8,128)(2,1)S(1)}, bf16[1536,128]{1,0:T(8,128)(2,1)S(1)}, u32[]{:S(2)}, u32[]{:S(2)}) collective-permute-start(bf16[1536,128]{1,0:T(8,128)(2,1)S(1)} %get-tuple-element.28), channel_id=1, source_target_pairs={{0,544},{32,512},{512,32},{544,0},{1,545},{33,513},{513,33},{545,1... | collective-permute-start | bytes 1179656 | tf_op jit(solution)/shard_map/ppermute | solution.py:167
  89.2 0.0 all-to-all-done.2
  89.2 1.1 %reduce_sum.21 = bf16[64,512]{1,0:T(8,128)(2,1)S(1)} reduce(bf16[8,64,512]{2,1,0:T(8,128)(2,1)} %all-to-all-done.2, bf16[]{:T(256)} %constant.2.clone.1), dimensions={0}, to_apply=%region_0.0 | reduce | flops 229376 | bytes 589826 | tf_op jit(solution)/shard_map/reduce_sum | solution.py:188
  90.4 14.4 %all_to_all.20 = bf16[16,4,512]{2,1,0:T(4,128)(2,1)S(1)} all-to-all(bf16[16,4,512]{2,1,0:T(4,128)(2,1)S(1)} %reshape.18), channel_id=1, replica_groups=mesh['xh'=2,'y'=8,'xl'=2,'z'=16,'c'=2] {'z'}, dimensions={0} | all-to-all | bytes 131072 | tf_op jit(solution)/shard_map/all_to_all | solution.py:159
  104.8 0.6 convert_reduce_fusion
  105.4 0.0 collective-permute-done.4.f1
  105.4 0.0 collective-permute-done.5.f2
  105.4 0.7 collective-permute-done.6.f3
  106.1 1.5 %shard_map.70 = (bf16[128,512]{1,0:T(8,128)(2,1)}, bf16[128,4096]{1,0:T(8,128)(2,1)}) custom-call(bf16[1536,128]{1,0:T(8,128)(2,1)S(1)} %get-tuple-element.25.f0, bf16[1536,128]{1,0:T(8,128)(2,1)S(1)} %collective-permute-done.4.f1, bf16[1536,128]{1,0:T(8,128)(2,1)S(1)} %collective-permute-done.5.f2, bf16[1536,128]{1,0:T(8,128)(2,1)S(1)} %collective-permute-done.6.f3), custom_call_target="tpu_custom_call" | custom-call | flops 268435456 | bytes 3145728 | tf_op jit(solution)/shard_map/pallas_call | solution.py:196
  (2 shorter events, 0.0 us)
Async XLA Ops:
  0.6 1.2 %copy-start = (bf16[128,4096]{1,0:T(8,128)(2,1)S(1)}, bf16[128,4096]{1,0:T(8,128)(2,1)}, u32[]{:S(2)}) copy-start(bf16[128,4096]{1,0:T(8,128)(2,1)} %tok_ref.1) | copy-start | bytes 3145732
  1.9 0.9 copy-start.1
  3.7 8.3 %copy-start.2 = (bf16[4,512]{1,0:T(4,128)(2,1)S(1)}, bf16[4,512]{1,0:T(4,128)(2,1)}, u32[]{:S(2)}) copy-start(bf16[4,512]{1,0:T(4,128)(2,1)} %codes.1) | copy-start | bytes 12292
  3.7 39.5 %collective-permute-start = (bf16[1536,128]{1,0:T(8,128)(2,1)S(1)}, bf16[1536,128]{1,0:T(8,128)(2,1)S(1)}, u32[]{:S(2)}, u32[]{:S(2)}) collective-permute-start(bf16[1536,128]{1,0:T(8,128)(2,1)S(1)} %get-tuple-element.19), channel_id=1, source_target_pairs={{0,32},{32,0},{1,33},{33,1},{2,34},{34,2},{3,35},{35,3},{4,36},{36... | collective-permute-start | bytes 1179656 | tf_op jit(solution)/shard_map/ppermute | solution.py:165
  7.8 4.3 %copy-start.3 = (bf16[4,4]{1,0:T(4,128)(2,1)S(1)}, bf16[4,4]{1,0:T(4,128)(2,1)}, u32[]{:S(2)}) copy-start(bf16[4,4]{1,0:T(4,128)(2,1)} %scales.1) | copy-start | bytes 100
  7.8 35.4 %collective-permute-start.1 = (bf16[1536,128]{1,0:T(8,128)(2,1)S(1)}, bf16[1536,128]{1,0:T(8,128)(2,1)S(1)}, u32[]{:S(2)}, u32[]{:S(2)}) collective-permute-start(bf16[1536,128]{1,0:T(8,128)(2,1)S(1)} %get-tuple-element.20), channel_id=1, source_target_pairs={{0,512},{512,0},{1,513},{513,1},{2,514},{514,2},{3,515},{515,3},{4... | collective-permute-start | bytes 1179656 | tf_op jit(solution)/shard_map/ppermute | solution.py:166
  12.8 30.4 %all-to-all-start = ((bf16[16,4,512]{2,1,0:T(4,128)(2,1)}), bf16[16,4,512]{2,1,0:T(4,128)(2,1)S(1)}, u32[]{:S(2)}, u32[]{:S(2)}) async-start(bf16[16,4,512]{2,1,0:T(4,128)(2,1)} %shard_map.68), calls=%async_computation | async-start | bytes 131072 | tf_op jit(solution)/shard_map/all_to_all | solution.py:159
  31.5 19.4 %collective-permute-start.3 = (bf16[1536,128]{1,0:T(8,128)(2,1)S(1)}, bf16[1536,128]{1,0:T(8,128)(2,1)S(1)}, u32[]{:S(2)}, u32[]{:S(2)}) collective-permute-start(bf16[1536,128]{1,0:T(8,128)(2,1)S(1)} %get-tuple-element.24), channel_id=1, source_target_pairs={{0,544},{32,512},{512,32},{544,0},{1,545},{33,513},{513,33},{545,1... | collective-permute-start | bytes 1179656 | tf_op jit(solution)/shard_map/ppermute | solution.py:167
  44.1 21.2 %all-to-all-start.1 = ((bf16[8,64,512]{2,1,0:T(8,128)(2,1)}), bf16[8,64,512]{2,1,0:T(8,128)(2,1)S(1)}, u32[]{:S(2)}, u32[]{:S(2)}) async-start(bf16[8,64,512]{2,1,0:T(8,128)(2,1)} %broadcast_in_dim.8), calls=%async_computation.1 | async-start | bytes 1048576 | tf_op jit(solution)/shard_map/all_to_all | solution.py:159
  51.6 6.4 %collective-permute-start.7 = (bf16[512,512]{1,0:T(8,128)(2,1)S(1)}, bf16[512,512]{1,0:T(8,128)(2,1)S(1)}, u32[]{:S(2)}, u32[]{:S(2)}) collective-permute-start(bf16[512,512]{1,0:T(8,128)(2,1)S(1)} %get-tuple-element.32), channel_id=1, source_target_pairs={{0,1},{1,0},{2,3},{3,2},{4,5},{5,4},{6,7},{7,6},{8,9},{9,8},{10,11... | collective-permute-start | bytes 1572872 | tf_op jit(solution)/shard_map/ppermute | solution.py:185
  65.3 23.9 %all-to-all-start.2 = ((bf16[8,64,512]{2,1,0:T(8,128)(2,1)}), bf16[8,64,512]{2,1,0:T(8,128)(2,1)}, u32[]{:S(2)}, u32[]{:S(2)}) async-start(bf16[8,64,512]{2,1,0:T(8,128)(2,1)} %bitcast.1), calls=%async_computation.2 | async-start | bytes 1048576 | tf_op jit(solution)/shard_map/all_to_all | solution.py:159
  69.4 7.5 %collective-permute-start.2 = (bf16[512,512]{1,0:T(8,128)(2,1)S(1)}, bf16[512,512]{1,0:T(8,128)(2,1)S(1)}, u32[]{:S(2)}, u32[]{:S(2)}) collective-permute-start(bf16[512,512]{1,0:T(8,128)(2,1)S(1)} %bitcast.2), channel_id=1, source_target_pairs={{0,1},{1,0},{2,3},{3,2},{4,5},{5,4},{6,7},{7,6},{8,9},{9,8},{10,11... | collective-permute-start | bytes 1572872 | tf_op jit(solution)/shard_map/ppermute | solution.py:183
  79.6 25.8 %collective-permute-start.4 = (bf16[1536,128]{1,0:T(8,128)(2,1)}, bf16[1536,128]{1,0:T(8,128)(2,1)S(1)}, u32[]{:S(2)}, u32[]{:S(2)}) collective-permute-start(bf16[1536,128]{1,0:T(8,128)(2,1)} %get-tuple-element.26), channel_id=1, source_target_pairs={{0,32},{32,0},{1,33},{33,1},{2,34},{34,2},{3,35},{35,3},{4,36},{36... | collective-permute-start | bytes 1179656 | tf_op jit(solution)/shard_map/ppermute | solution.py:165
  81.5 23.9 %collective-permute-start.5 = (bf16[1536,128]{1,0:T(8,128)(2,1)S(1)}, bf16[1536,128]{1,0:T(8,128)(2,1)S(1)}, u32[]{:S(2)}, u32[]{:S(2)}) collective-permute-start(bf16[1536,128]{1,0:T(8,128)(2,1)S(1)} %get-tuple-element.27), channel_id=1, source_target_pairs={{0,512},{512,0},{1,513},{513,1},{2,514},{514,2},{3,515},{515,3},{4... | collective-permute-start | bytes 1179656 | tf_op jit(solution)/shard_map/ppermute | solution.py:166
  84.8 21.3 %collective-permute-start.6 = (bf16[1536,128]{1,0:T(8,128)(2,1)S(1)}, bf16[1536,128]{1,0:T(8,128)(2,1)S(1)}, u32[]{:S(2)}, u32[]{:S(2)}) collective-permute-start(bf16[1536,128]{1,0:T(8,128)(2,1)S(1)} %get-tuple-element.28), channel_id=1, source_target_pairs={{0,544},{32,512},{512,32},{544,0},{1,545},{33,513},{513,33},{545,1... | collective-permute-start | bytes 1179656 | tf_op jit(solution)/shard_map/ppermute | solution.py:167

commit v4 on v2

--- a/solution.py
+++ b/solution.py
@@ -56,23 +56,39 @@
     return one_hot(iota((128, 128), 0) == iota((128, 128), 1))
 
 
-def prepare(tok_ref, grad_ref, *outs):
+def prepare(tok_ref, grad_ref, *refs):
+    outs, (tok, grad, sems) = refs[:4], refs[4:]
     xh, xl = lax.axis_index("xh"), lax.axis_index("xl")
-    split = x_split(xh)
-    for kl in range(2):
-        col = (xl if kl == 0 else 1 - xl) * (NZ * 128)
-        for z in range(NZ):
-            block = tok_ref[:, pl.ds(pl.multiple_of(col + z * 128, 128), 128)]
-            piece = dot(split, block, NT).astype(BF16)
+    wide = NZ * 128 // 2
+    copies = [pltpu.make_async_copy(grad_ref, grad, sems.at[4])]
+    for i in range(4):
+        col = (xl if i < 2 else 1 - xl) * (NZ * 128) + (i % 2) * wide
+        there = tok_ref.at[:, pl.ds(pl.multiple_of(col, 128), wide)]
+        copies.append(pltpu.make_async_copy(there, tok.at[i], sems.at[i]))
+    for copy in copies:
+        copy.start()
+    same, split = eye(), x_split(xh)
+    copies[0].wait()
+    for b in range(KV // 128):
+        piece = dot(same, grad[:, b * 128 : (b + 1) * 128], NT).astype(BF16)
+        for out in outs:
+            out[pl.ds(SLICE + b * 128, 128), :] = piece
+    for i in range(4):
+        copies[1 + i].wait()
+        for j in range(NZ // 2):
+            z = (i % 2) * (NZ // 2) + j
+            piece = dot(split, tok[i, :, j * 128 : (j + 1) * 128], NT).astype(BF16)
             for kh in range(2):
                 for c in range(2):
                     at = kh * 64 + c * 32
-                    outs[2 * kh + kl][pl.ds(c * HALF + z * 32, 32), :] = piece[at : at + 32]
-    same = eye()
-    for b in range(KV // 128):
-        piece = dot(same, grad_ref[:, b * 128 : (b + 1) * 128], NT).astype(BF16)
-        for out in outs:
-            out[pl.ds(SLICE + b * 128, 128), :] = piece
+                    outs[2 * kh + i // 2][pl.ds(c * HALF + z * 32, 32), :] = piece[at : at + 32]
+
+
+def scale_rows(codes, scales, copies):
+    for b in range(KV // BLOCK):
+        at = slice(b * BLOCK, (b + 1) * BLOCK)
+        scaled = codes[:, at].astype(F32) * scales[:, b : b + 1].astype(F32)
+        copies[:, :, at] = jnp.broadcast_to(scaled.astype(BF16)[None], (NZ, ROWS, BLOCK))
 
 
 def partial_sums(r0, r1, r2, r3, keep, send):
@@ -131,43 +147,49 @@
             input_grad[:, pl.ds(pl.multiple_of(col + z * 128, 128), 128)] = block
 
 
-def kernel(body, outs, flops, moved, scratch=()):
+def last_sum(blocks, out):
+    out[...] = jnp.sum(blocks[...].astype(F32), axis=0)
+
+
+def kernel(body, outs, flops, moved, scratch=(), in_hbm=0, vmem=24, dtype=BF16):
     return pl.pallas_call(
         body,
-        out_shape=[jax.ShapeDtypeStruct(s, BF16) for s in outs],
+        **({"in_specs": [pl.BlockSpec(memory_space=pl.ANY)] * in_hbm} if in_hbm else {}),
+        out_shape=[jax.ShapeDtypeStruct(s, dtype) for s in outs],
         scratch_shapes=list(scratch),
-        compiler_params=pltpu.CompilerParams(vmem_limit_bytes=24 * 1024 * 1024),
+        compiler_params=pltpu.CompilerParams(vmem_limit_bytes=vmem << 20),
         cost_estimate=pl.CostEstimate(flops=flops, bytes_accessed=moved, transcendentals=0),
         interpret=INTERPRET,
     )
 
 
-def dequantize(codes, scales):
-    rows = codes.shape[0]
-    blocks = codes.astype(F32).reshape(rows, KV // BLOCK, BLOCK)
-    scaled = blocks * scales.astype(F32)[:, :, None]
-    return scaled.reshape(rows, KV).astype(BF16)
-
-
 def exchange(blocks, axis):
     return lax.all_to_all(blocks, axis, split_axis=0, concat_axis=0, tiled=True)
 
 
-def to_members(blocks):
-    return (
-        blocks[0],
-        lax.ppermute(blocks[1], "xl", SWAP),
-        lax.ppermute(blocks[2], "xh", SWAP),
-        lax.ppermute(blocks[3], ("xh", "xl"), [(0, 3), (1, 2), (2, 1), (3, 0)]),
-    )
+def far(block):
+    return lax.ppermute(block, "xh", SWAP)
+
+
+def near(block):
+    return lax.ppermute(block, "xl", SWAP)
+
+
+def next_to(block):
+    return lax.ppermute(block, ("xh", "xl"), [(0, 3), (1, 2), (2, 1), (3, 0)])
 
 
 def shards(tokens, key_grad, codes, scales):
-    part = dequantize(codes, scales)
-    blocks = kernel(prepare, [(PAY, TOK)] * 4, 1 << 28, 3 << 20)(tokens, key_grad)
-    work = to_members(blocks)
-    by_z = exchange(jnp.broadcast_to(part[None], (NZ, ROWS, KV)), "z")
-    by_z = by_z.reshape(NZ * ROWS, KV)
+    (copies,) = kernel(scale_rows, [(NZ, ROWS, KV)], 1 << 12, 1 << 17)(codes, scales)
+    room = [
+        pltpu.VMEM((4, TOK, NZ * 64), BF16),
+        pltpu.VMEM((TOK, KV), BF16),
+        pltpu.SemaphoreType.DMA((5,)),
+    ]
+    blocks = kernel(prepare, [(PAY, TOK)] * 4, 1 << 28, 3 << 20, room, 2, 60)(tokens, key_grad)
+    work = far(blocks[2]), near(blocks[1]), next_to(blocks[3])
+    work = blocks[0], work[1], work[0], work[2]
+    by_z = exchange(copies, "z").reshape(NZ * ROWS, KV)
     by_y = exchange(jnp.broadcast_to(by_z[None], (NY, NZ * ROWS, KV)), "y")
     own = by_y.reshape(HALF, KV)
     other = lax.ppermute(own, "c", SWAP)
@@ -176,12 +198,15 @@
     (total,) = kernel(add_cores, [(HALF, KV)], 1 << 28, 3 << 19)(keep, got)
     total = exchange(total.reshape(NY, NZ * ROWS, KV), "y")
     total = jnp.sum(total.astype(F32), axis=0).astype(BF16)
-    total = exchange(total.reshape(NZ, ROWS, KV), "z")
-    weight_grad = jnp.sum(total.astype(F32), axis=0)
     results = kernel(
         apply_weight, [(PAY, TOK)] * 4, 1 << 30, 4 << 20, [pltpu.VMEM((SLICE, KV), BF16)]
     )(own, other, *work)
-    results = to_members(results)
+    from_far = far(results[2])
+    total, one, three = lax.optimization_barrier((total, results[1], results[3]))
+    total = exchange(total.reshape(NZ, ROWS, KV), "z")
+    total, from_far = lax.optimization_barrier((total, from_far))
+    results = results[0], near(one), from_far, next_to(three)
+    (weight_grad,) = kernel(last_sum, [(ROWS, KV)], 1 << 36, 1 << 17, dtype=F32)(total)
     d_in = 4 * SLICE
     keys, input_grad = kernel(finish, [(TOK, KV), (TOK, d_in)], 1 << 28, 3 << 20)(*results)
     return keys, input_grad, weight_grad

time: 112 us -> 117 us (1.045)
  blocking collectives: 22.8 us -> 0 us
  waiting for transfers between devices: 16.3 us -> 34.3 us
  starting transfers between devices: 58.3 us -> 66.3 us
  Pallas kernels: 7.19 us -> 11 us
  other arithmetic: 3.16 us -> 1.12 us
    all_to_all x1 -> x0, blocking collectives: 22.8 us -> none  [exchange(): return lax.all_to_all(blocks, axis, split_axis=0, concat_axis=0, tiled=True)]
    all_to_all x3 -> x4, waiting for transfers between devices: 1.71 us -> 16.9 us  [exchange(): return lax.all_to_all(blocks, axis, split_axis=0, concat_axis=0, tiled=True)]
    all_to_all x3 -> x4, starting transfers between devices: 33.1 us -> 44.6 us  [exchange(): return lax.all_to_all(blocks, axis, split_axis=0, concat_axis=0, tiled=True)]
    pallas_call x1 -> x3, Pallas kernels: 0.94 us -> 4.75 us  [the longest x1 3.4 us: shards(): kernel(prepare, [(PAY, TOK)] * 4, 1 << 28, 3 << 20, room, 2, 60)]
    ppermute x6, starting transfers between devices: 19.2 us -> 15.5 us  [the longest x2 6.26 us: far(): return lax.ppermute(block, 'xh', SWAP)]
    ppermute x6, waiting for transfers between devices: 11.6 us -> 14.3 us  [the longest x2 9.36 us: next_to(): return lax.ppermute(block, ('xh', 'xl'), [(0, 3), (1, 2), (2, 1), (3, 0)])]
    convert_element_type x2 -> x0, other arithmetic: 1.41 us -> none  [the longest x1 0.72 us: dequantize(): scaled = blocks * scales.astype(F32)[:, :, None]]
  transfers between devices with their start and end apart: 11 -> 12, of which waited for: 5 -> 7; matrix products, arithmetic and copies ran while one was open for 2% -> 2% of each run, Pallas kernels for 5% -> 8%
where the time goes in v4:
time: 117 us; the launch traced here: 116 us
  starting transfers between devices  66.3 us (57%)
  waiting for transfers between devices  34.3 us (29%)
  Pallas kernels  11 us (9%)
  local copies, waits for them, and re-layouts  2.87 us (2%)
    all_to_all x4, starting transfers between devices, exchange(): return lax.all_to_all(blocks, axis, split_axis=0, concat_axis=0, tiled=True)  44.6 us
    all_to_all x4, waiting for transfers between devices, exchange(): return lax.all_to_all(blocks, axis, split_axis=0, concat_axis=0, tiled=True)  16.9 us
    ppermute x2, waiting for transfers between devices, next_to(): return lax.ppermute(block, ('xh', 'xl'), [(0, 3), (1, 2), (2, 1), (3, 0)])  9.36 us
    ppermute x2, starting transfers between devices, far(): return lax.ppermute(block, 'xh', SWAP)  6.26 us
    ppermute x2, starting transfers between devices, near(): return lax.ppermute(block, 'xl', SWAP)  5.03 us
    ppermute x2, waiting for transfers between devices, far(): return lax.ppermute(block, 'xh', SWAP)  4.99 us
    ppermute x2, starting transfers between devices, next_to(): return lax.ppermute(block, ('xh', 'xl'), [(0, 3), (1, 2), (2, 1), (3, 0)])  4.24 us
    ppermute x1, starting transfers between devices, shards(): got = lax.ppermute(send, 'c', SWAP)  3.58 us
  transfers between devices with their start and end apart: 12, of which 7 were waited for; matrix products, arithmetic and copies ran while one was open for 2% of the time, Pallas kernels for 8%

profile of v4, /device:TPU:1, one launch (start us, length us, event | category | flops | bytes accessed | tf_op | source)
XLA Modules:
  0.0 116.3 jit_solution(13569725350909822469)
XLA Ops:
  0.6 0.0 copy-start
  0.6 0.7 copy-done
  1.3 0.0 copy-start.1
  1.3 0.7 copy-done.1
  2.0 0.7 shard_map.67
  2.7 19.4 %all-to-all-start = ((bf16[16,4,512]{2,1,0:T(4,128)(2,1)}), bf16[16,4,512]{2,1,0:T(4,128)(2,1)S(1)}, u32[]{:S(2)}, u32[]{:S(2)}) async-start(bf16[16,4,512]{2,1,0:T(4,128)(2,1)} %shard_map.67), calls=%async_computation | async-start | bytes 131072 | tf_op jit(solution)/shard_map/all_to_all | solution.py:167
  22.1 3.4 %shard_map.68 = (bf16[1536,128]{1,0:T(8,128)(2,1)}, bf16[1536,128]{1,0:T(8,128)(2,1)}, bf16[1536,128]{1,0:T(8,128)(2,1)}, bf16[1536,128]{1,0:T(8,128)(2,1)}) custom-call(bf16[128,4096]{1,0:T(8,128)(2,1)} %tok_ref.1, bf16[128,512]{1,0:T(8,128)(2,1)} %grad_ref.1), custom_call_target="tpu_custom_call" | custom-call | flops 268435456 | bytes 3145728 | tf_op jit(solution)/shard_map/pallas_call | solution.py:189
  25.5 3.1 %collective-permute-start.1 = (bf16[1536,128]{1,0:T(8,128)(2,1)}, bf16[1536,128]{1,0:T(8,128)(2,1)S(1)}, u32[]{:S(2)}, u32[]{:S(2)}) collective-permute-start(bf16[1536,128]{1,0:T(8,128)(2,1)} %get-tuple-element.21), channel_id=1, source_target_pairs={{0,32},{32,0},{1,33},{33,1},{2,34},{34,2},{3,35},{35,3},{4,36},{36... | collective-permute-start | bytes 1179656 | tf_op jit(solution)/shard_map/ppermute | solution.py:175
  28.7 4.4 %collective-permute-start.2 = (bf16[1536,128]{1,0:T(8,128)(2,1)}, bf16[1536,128]{1,0:T(8,128)(2,1)S(1)}, u32[]{:S(2)}, u32[]{:S(2)}) collective-permute-start(bf16[1536,128]{1,0:T(8,128)(2,1)} %get-tuple-element.22), channel_id=1, source_target_pairs={{0,512},{512,0},{1,513},{513,1},{2,514},{514,2},{3,515},{515,3},{4... | collective-permute-start | bytes 1179656 | tf_op jit(solution)/shard_map/ppermute | solution.py:171
  33.0 2.1 %collective-permute-start.3 = (bf16[1536,128]{1,0:T(8,128)(2,1)}, bf16[1536,128]{1,0:T(8,128)(2,1)S(1)}, u32[]{:S(2)}, u32[]{:S(2)}) collective-permute-start(bf16[1536,128]{1,0:T(8,128)(2,1)} %get-tuple-element.23), channel_id=1, source_target_pairs={{0,544},{32,512},{512,32},{544,0},{1,545},{33,513},{513,33},{545,1... | collective-permute-start | bytes 1179656 | tf_op jit(solution)/shard_map/ppermute | solution.py:179
  35.1 0.0 all-to-all-done
  35.2 0.8 broadcast_in_dim.8
  36.0 0.0 copy-start.2
  36.0 6.9 %all-to-all-start.1 = ((bf16[8,64,512]{2,1,0:T(8,128)(2,1)}), bf16[8,64,512]{2,1,0:T(8,128)(2,1)S(1)}, u32[]{:S(2)}, u32[]{:S(2)}) async-start(bf16[8,64,512]{2,1,0:T(8,128)(2,1)} %broadcast_in_dim.8), calls=%async_computation.1 | async-start | bytes 1048576 | tf_op jit(solution)/shard_map/all_to_all | solution.py:167
  43.0 0.0 collective-permute-done.1.r1
  43.0 5.0 %collective-permute-done.2.r2 = bf16[1536,128]{1,0:T(8,128)(2,1)S(1)} collective-permute-done((bf16[1536,128]{1,0:T(8,128)(2,1)}, bf16[1536,128]{1,0:T(8,128)(2,1)S(1)}, u32[]{:S(2)}, u32[]{:S(2)}) %collective-permute-start.2) | collective-permute-done | bytes 393248 | tf_op jit(solution)/shard_map/ppermute | solution.py:171
  48.0 6.7 %collective-permute-done.3.r3 = bf16[1536,128]{1,0:T(8,128)(2,1)S(1)} collective-permute-done((bf16[1536,128]{1,0:T(8,128)(2,1)}, bf16[1536,128]{1,0:T(8,128)(2,1)S(1)}, u32[]{:S(2)}, u32[]{:S(2)}) %collective-permute-start.3) | collective-permute-done | bytes 393248 | tf_op jit(solution)/shard_map/ppermute | solution.py:179
  54.6 0.0 copy-done.2
  54.6 0.7 shard_map.70
  55.4 3.6 %collective-permute-start.4 = (bf16[512,512]{1,0:T(8,128)(2,1)S(1)}, bf16[512,512]{1,0:T(8,128)(2,1)S(1)}, u32[]{:S(2)}, u32[]{:S(2)}) collective-permute-start(bf16[512,512]{1,0:T(8,128)(2,1)S(1)} %get-tuple-element.26), channel_id=1, source_target_pairs={{0,1},{1,0},{2,3},{3,2},{4,5},{5,4},{6,7},{7,6},{8,9},{9,8},{10,11... | collective-permute-start | bytes 1572872 | tf_op jit(solution)/shard_map/ppermute | solution.py:197
  59.0 1.5 %collective-permute-done.4.b = bf16[512,512]{1,0:T(8,128)(2,1)S(1)} collective-permute-done((bf16[512,512]{1,0:T(8,128)(2,1)S(1)}, bf16[512,512]{1,0:T(8,128)(2,1)S(1)}, u32[]{:S(2)}, u32[]{:S(2)}) %collective-permute-start.4) | collective-permute-done | bytes 524320 | tf_op jit(solution)/shard_map/ppermute | solution.py:197
  60.5 1.3 %shard_map.71 = bf16[512,512]{1,0:T(8,128)(2,1)} custom-call(bf16[512,512]{1,0:T(8,128)(2,1)S(1)} %get-tuple-element.25.a, bf16[512,512]{1,0:T(8,128)(2,1)S(1)} %collective-permute-done.4.b), custom_call_target="tpu_custom_call" | custom-call | flops 268435456 | bytes 1572864 | tf_op jit(solution)/shard_map/pallas_call | solution.py:198
  61.8 0.0 all-to-all-done.1
  61.8 6.8 %all-to-all-start.2 = ((bf16[8,64,512]{2,1,0:T(8,128)(2,1)}), bf16[8,64,512]{2,1,0:T(8,128)(2,1)}, u32[]{:S(2)}, u32[]{:S(2)}) async-start(bf16[8,64,512]{2,1,0:T(8,128)(2,1)} %bitcast.1), calls=%async_computation.2 | async-start | bytes 1048576 | tf_op jit(solution)/shard_map/all_to_all | solution.py:167
  68.6 2.6 %collective-permute-start = (bf16[512,512]{1,0:T(8,128)(2,1)S(1)}, bf16[512,512]{1,0:T(8,128)(2,1)S(1)}, u32[]{:S(2)}, u32[]{:S(2)}) collective-permute-start(bf16[512,512]{1,0:T(8,128)(2,1)S(1)} %bitcast.2), channel_id=1, source_target_pairs={{0,1},{1,0},{2,3},{3,2},{4,5},{5,4},{6,7},{7,6},{8,9},{9,8},{10,11... | collective-permute-start | bytes 1572872 | tf_op jit(solution)/shard_map/ppermute | solution.py:195
  71.2 1.5 %collective-permute-done.other = bf16[512,512]{1,0:T(8,128)(2,1)S(1)} collective-permute-done((bf16[512,512]{1,0:T(8,128)(2,1)S(1)}, bf16[512,512]{1,0:T(8,128)(2,1)S(1)}, u32[]{:S(2)}, u32[]{:S(2)}) %collective-permute-start) | collective-permute-done | bytes 524320 | tf_op jit(solution)/shard_map/ppermute | solution.py:195
  72.7 2.7 %shard_map.69 = (bf16[1536,128]{1,0:T(8,128)(2,1)S(1)}, bf16[1536,128]{1,0:T(8,128)(2,1)S(1)}, bf16[1536,128]{1,0:T(8,128)(2,1)}, bf16[1536,128]{1,0:T(8,128)(2,1)S(1)}) custom-call(bf16[512,512]{1,0:T(8,128)(2,1)S(1)} %bitcast.3, bf16[512,512]{1,0:T(8,128)(2,1)S(1)} %collective-permute-done.other, bf16[1536,128]{1,0:T(8,128)(2,1)S(1)} %copy-done.2, ...), custom_call_target="tpu_custom_call" | custom-call | flops 1073741824 | bytes 4194304 | tf_op jit(solution)/shard_map/pallas_call | solution.py:201
  75.4 1.9 %collective-permute-start.6 = (bf16[1536,128]{1,0:T(8,128)(2,1)}, bf16[1536,128]{1,0:T(8,128)(2,1)S(1)}, u32[]{:S(2)}, u32[]{:S(2)}) collective-permute-start(bf16[1536,128]{1,0:T(8,128)(2,1)} %get-tuple-element.31), channel_id=1, source_target_pairs={{0,512},{512,0},{1,513},{513,1},{2,514},{514,2},{3,515},{515,3},{4... | collective-permute-start | bytes 1179656 | tf_op jit(solution)/shard_map/ppermute | solution.py:171
  77.3 9.4 %all-to-all-done.2 = bf16[8,64,512]{2,1,0:T(8,128)(2,1)} async-done(((bf16[8,64,512]{2,1,0:T(8,128)(2,1)}), bf16[8,64,512]{2,1,0:T(8,128)(2,1)}, u32[]{:S(2)}, u32[]{:S(2)}) %all-to-all-start.2) | async-done | bytes 524320 | tf_op jit(solution)/shard_map/all_to_all | solution.py:167
  86.7 1.1 reduce_sum.12
  87.8 0.7 reshape.18
  88.4 11.5 %all-to-all-start.3 = ((bf16[16,4,512]{2,1,0:T(4,128)(2,1)}), bf16[16,4,512]{2,1,0:T(4,128)(2,1)S(1)}, u32[]{:S(2)}, u32[]{:S(2)}) async-start(bf16[16,4,512]{2,1,0:T(4,128)(2,1)} %reshape.18), calls=%async_computation.3 | async-start | bytes 131072 | tf_op jit(solution)/shard_map/all_to_all | solution.py:167
  99.9 1.9 %collective-permute-start.5 = (bf16[1536,128]{1,0:T(8,128)(2,1)S(1)}, bf16[1536,128]{1,0:T(8,128)(2,1)S(1)}, u32[]{:S(2)}, u32[]{:S(2)}) collective-permute-start(bf16[1536,128]{1,0:T(8,128)(2,1)S(1)} %get-tuple-element.29), channel_id=1, source_target_pairs={{0,32},{32,0},{1,33},{33,1},{2,34},{34,2},{3,35},{35,3},{4,36},{36... | collective-permute-start | bytes 1179656 | tf_op jit(solution)/shard_map/ppermute | solution.py:175
  101.8 2.1 %collective-permute-start.7 = (bf16[1536,128]{1,0:T(8,128)(2,1)S(1)}, bf16[1536,128]{1,0:T(8,128)(2,1)S(1)}, u32[]{:S(2)}, u32[]{:S(2)}) collective-permute-start(bf16[1536,128]{1,0:T(8,128)(2,1)S(1)} %get-tuple-element.33), channel_id=1, source_target_pairs={{0,544},{32,512},{512,32},{544,0},{1,545},{33,513},{513,33},{545,1... | collective-permute-start | bytes 1179656 | tf_op jit(solution)/shard_map/ppermute | solution.py:179
  104.0 0.0 collective-permute-done.6.f2
  104.0 7.5 %all-to-all-done.3.blocks = bf16[16,4,512]{2,1,0:T(4,128)(2,1)S(1)} async-done(((bf16[16,4,512]{2,1,0:T(4,128)(2,1)}), bf16[16,4,512]{2,1,0:T(4,128)(2,1)S(1)}, u32[]{:S(2)}, u32[]{:S(2)}) %all-to-all-start.3) | async-done | bytes 65568 | tf_op jit(solution)/shard_map/all_to_all | solution.py:167
  111.5 0.6 shard_map.73
  112.1 0.0 collective-permute-done.5.f1
  112.1 2.7 %collective-permute-done.7.f3 = bf16[1536,128]{1,0:T(8,128)(2,1)S(1)} collective-permute-done((bf16[1536,128]{1,0:T(8,128)(2,1)S(1)}, bf16[1536,128]{1,0:T(8,128)(2,1)S(1)}, u32[]{:S(2)}, u32[]{:S(2)}) %collective-permute-start.7) | collective-permute-done | bytes 393248 | tf_op jit(solution)/shard_map/ppermute | solution.py:179
  114.8 1.5 %shard_map.72 = (bf16[128,512]{1,0:T(8,128)(2,1)}, bf16[128,4096]{1,0:T(8,128)(2,1)}) custom-call(bf16[1536,128]{1,0:T(8,128)(2,1)S(1)} %get-tuple-element.24.f0, bf16[1536,128]{1,0:T(8,128)(2,1)S(1)} %collective-permute-done.5.f1, bf16[1536,128]{1,0:T(8,128)(2,1)S(1)} %collective-permute-done.6.f2, bf16[1536,128]{1,0:T(8,128)(2,1)S(1)} %collective-permute-done.7.f3), custom_call_target="tpu_custom_call" | custom-call | flops 268435456 | bytes 3145728 | tf_op jit(solution)/shard_map/pallas_call | solution.py:211
  (1 shorter events, 0.0 us)
Async XLA Ops:
  0.6 0.7 copy-start
  1.3 0.7 copy-start.1
  2.7 32.4 %all-to-all-start = ((bf16[16,4,512]{2,1,0:T(4,128)(2,1)}), bf16[16,4,512]{2,1,0:T(4,128)(2,1)S(1)}, u32[]{:S(2)}, u32[]{:S(2)}) async-start(bf16[16,4,512]{2,1,0:T(4,128)(2,1)} %shard_map.67), calls=%async_computation | async-start | bytes 131072 | tf_op jit(solution)/shard_map/all_to_all | solution.py:167
  25.5 17.4 %collective-permute-start.1 = (bf16[1536,128]{1,0:T(8,128)(2,1)}, bf16[1536,128]{1,0:T(8,128)(2,1)S(1)}, u32[]{:S(2)}, u32[]{:S(2)}) collective-permute-start(bf16[1536,128]{1,0:T(8,128)(2,1)} %get-tuple-element.21), channel_id=1, source_target_pairs={{0,32},{32,0},{1,33},{33,1},{2,34},{34,2},{3,35},{35,3},{4,36},{36... | collective-permute-start | bytes 1179656 | tf_op jit(solution)/shard_map/ppermute | solution.py:175
  28.7 19.3 %collective-permute-start.2 = (bf16[1536,128]{1,0:T(8,128)(2,1)}, bf16[1536,128]{1,0:T(8,128)(2,1)S(1)}, u32[]{:S(2)}, u32[]{:S(2)}) collective-permute-start(bf16[1536,128]{1,0:T(8,128)(2,1)} %get-tuple-element.22), channel_id=1, source_target_pairs={{0,512},{512,0},{1,513},{513,1},{2,514},{514,2},{3,515},{515,3},{4... | collective-permute-start | bytes 1179656 | tf_op jit(solution)/shard_map/ppermute | solution.py:171
  33.0 21.6 %collective-permute-start.3 = (bf16[1536,128]{1,0:T(8,128)(2,1)}, bf16[1536,128]{1,0:T(8,128)(2,1)S(1)}, u32[]{:S(2)}, u32[]{:S(2)}) collective-permute-start(bf16[1536,128]{1,0:T(8,128)(2,1)} %get-tuple-element.23), channel_id=1, source_target_pairs={{0,544},{32,512},{512,32},{544,0},{1,545},{33,513},{513,33},{545,1... | collective-permute-start | bytes 1179656 | tf_op jit(solution)/shard_map/ppermute | solution.py:179
  36.0 18.6 %copy-start.2 = (bf16[1536,128]{1,0:T(8,128)(2,1)S(1)}, bf16[1536,128]{1,0:T(8,128)(2,1)}, u32[]{:S(2)}) copy-start(bf16[1536,128]{1,0:T(8,128)(2,1)} %get-tuple-element.20.r0) | copy-start | bytes 1179652
  36.0 25.8 %all-to-all-start.1 = ((bf16[8,64,512]{2,1,0:T(8,128)(2,1)}), bf16[8,64,512]{2,1,0:T(8,128)(2,1)S(1)}, u32[]{:S(2)}, u32[]{:S(2)}) async-start(bf16[8,64,512]{2,1,0:T(8,128)(2,1)} %broadcast_in_dim.8), calls=%async_computation.1 | async-start | bytes 1048576 | tf_op jit(solution)/shard_map/all_to_all | solution.py:167
  55.4 5.1 %collective-permute-start.4 = (bf16[512,512]{1,0:T(8,128)(2,1)S(1)}, bf16[512,512]{1,0:T(8,128)(2,1)S(1)}, u32[]{:S(2)}, u32[]{:S(2)}) collective-permute-start(bf16[512,512]{1,0:T(8,128)(2,1)S(1)} %get-tuple-element.26), channel_id=1, source_target_pairs={{0,1},{1,0},{2,3},{3,2},{4,5},{5,4},{6,7},{7,6},{8,9},{9,8},{10,11... | collective-permute-start | bytes 1572872 | tf_op jit(solution)/shard_map/ppermute | solution.py:197
  61.8 24.9 %all-to-all-start.2 = ((bf16[8,64,512]{2,1,0:T(8,128)(2,1)}), bf16[8,64,512]{2,1,0:T(8,128)(2,1)}, u32[]{:S(2)}, u32[]{:S(2)}) async-start(bf16[8,64,512]{2,1,0:T(8,128)(2,1)} %bitcast.1), calls=%async_computation.2 | async-start | bytes 1048576 | tf_op jit(solution)/shard_map/all_to_all | solution.py:167
  68.6 4.1 %collective-permute-start = (bf16[512,512]{1,0:T(8,128)(2,1)S(1)}, bf16[512,512]{1,0:T(8,128)(2,1)S(1)}, u32[]{:S(2)}, u32[]{:S(2)}) collective-permute-start(bf16[512,512]{1,0:T(8,128)(2,1)S(1)} %bitcast.2), channel_id=1, source_target_pairs={{0,1},{1,0},{2,3},{3,2},{4,5},{5,4},{6,7},{7,6},{8,9},{9,8},{10,11... | collective-permute-start | bytes 1572872 | tf_op jit(solution)/shard_map/ppermute | solution.py:195
  75.4 28.6 %collective-permute-start.6 = (bf16[1536,128]{1,0:T(8,128)(2,1)}, bf16[1536,128]{1,0:T(8,128)(2,1)S(1)}, u32[]{:S(2)}, u32[]{:S(2)}) collective-permute-start(bf16[1536,128]{1,0:T(8,128)(2,1)} %get-tuple-element.31), channel_id=1, source_target_pairs={{0,512},{512,0},{1,513},{513,1},{2,514},{514,2},{3,515},{515,3},{4... | collective-permute-start | bytes 1179656 | tf_op jit(solution)/shard_map/ppermute | solution.py:171
  88.4 23.0 %all-to-all-start.3 = ((bf16[16,4,512]{2,1,0:T(4,128)(2,1)}), bf16[16,4,512]{2,1,0:T(4,128)(2,1)S(1)}, u32[]{:S(2)}, u32[]{:S(2)}) async-start(bf16[16,4,512]{2,1,0:T(4,128)(2,1)} %reshape.18), calls=%async_computation.3 | async-start | bytes 131072 | tf_op jit(solution)/shard_map/all_to_all | solution.py:167
  99.9 12.2 %collective-permute-start.5 = (bf16[1536,128]{1,0:T(8,128)(2,1)S(1)}, bf16[1536,128]{1,0:T(8,128)(2,1)S(1)}, u32[]{:S(2)}, u32[]{:S(2)}) collective-permute-start(bf16[1536,128]{1,0:T(8,128)(2,1)S(1)} %get-tuple-element.29), channel_id=1, source_target_pairs={{0,32},{32,0},{1,33},{33,1},{2,34},{34,2},{3,35},{35,3},{4,36},{36... | collective-permute-start | bytes 1179656 | tf_op jit(solution)/shard_map/ppermute | solution.py:175
  101.8 13.0 %collective-permute-start.7 = (bf16[1536,128]{1,0:T(8,128)(2,1)S(1)}, bf16[1536,128]{1,0:T(8,128)(2,1)S(1)}, u32[]{:S(2)}, u32[]{:S(2)}) collective-permute-start(bf16[1536,128]{1,0:T(8,128)(2,1)S(1)} %get-tuple-element.33), channel_id=1, source_target_pairs={{0,544},{32,512},{512,32},{544,0},{1,545},{33,513},{513,33},{545,1... | collective-permute-start | bytes 1179656 | tf_op jit(solution)/shard_map/ppermute | solution.py:179

commit v5 on v3

--- a/solution.py
+++ b/solution.py
@@ -75,15 +75,14 @@
             out[pl.ds(SLICE + b * 128, 128), :] = piece
 
 
-def scale_rows(codes, scales, later, copies):
-    del later
+def scale_rows(codes, scales, copies):
     for b in range(KV // BLOCK):
         at = slice(b * BLOCK, (b + 1) * BLOCK)
         scaled = codes[:, at].astype(F32) * scales[:, b : b + 1].astype(F32)
         copies[:, :, at] = jnp.broadcast_to(scaled.astype(BF16)[None], (NZ, ROWS, BLOCK))
 
 
-def partial_sums(r0, r1, r2, r3, keep, send):
+def partial_sums(r0, r2, r1, r3, keep, send):
     c = lax.axis_index("c")
     refs = (r0, r1, r2, r3)
     grads = jnp.concatenate([r[SLICE:, :] for r in refs], axis=1)
@@ -116,7 +115,7 @@
         out[SLICE:, :] = keys[:, k * TOK : (k + 1) * TOK]
 
 
-def finish(f0, f1, f2, f3, keys, input_grad):
+def finish(f0, f2, f1, f3, keys, input_grad):
     xh, xl = lax.axis_index("xh"), lax.axis_index("xl")
     refs = (f0, f1, f2, f3)
     same, split = eye(), x_split(xh)
@@ -139,14 +138,9 @@
             input_grad[:, pl.ds(pl.multiple_of(col + z * 128, 128), 128)] = block
 
 
-def kernel(body, outs, flops, moved, scratch=(), any_of=None):
-    specs = {}
-    if any_of is not None:
-        whole = [pl.BlockSpec(memory_space=pltpu.VMEM)] * any_of
-        specs = {"in_specs": [*whole, pl.BlockSpec(memory_space=pl.ANY)]}
+def kernel(body, outs, flops, moved, scratch=()):
     return pl.pallas_call(
         body,
-        **specs,
         out_shape=[jax.ShapeDtypeStruct(s, BF16) for s in outs],
         scratch_shapes=list(scratch),
         compiler_params=pltpu.CompilerParams(vmem_limit_bytes=24 * 1024 * 1024),
@@ -157,6 +151,10 @@
 
 def exchange(blocks, axis):
     return lax.all_to_all(blocks, axis, split_axis=0, concat_axis=0, tiled=True)
+
+
+def far_first(blocks):
+    return [blocks[k] for k in (0, 2, 1, 3)]
 
 
 def to_members(blocks):
@@ -171,17 +169,15 @@
 def shards(tokens, key_grad, codes, scales):
     blocks = kernel(prepare, [(PAY, TOK)] * 4, 1 << 28, 3 << 20)(tokens, key_grad)
     work = to_members(blocks)
-    (copies,) = kernel(scale_rows, [(NZ, ROWS, KV)], 1 << 12, 1 << 17, any_of=2)(
-        codes, scales, blocks[0]
-    )
+    (copies,) = kernel(scale_rows, [(NZ, ROWS, KV)], 1 << 12, 1 << 17)(codes, scales)
     by_z = exchange(copies, "z")
-    by_z, one, two = lax.optimization_barrier((by_z, work[1], work[2]))
-    work = (work[0], one, two, work[3])
+    by_z, two = lax.optimization_barrier((by_z, work[2]))
+    work = (work[0], work[1], two, work[3])
     by_z = by_z.reshape(NZ * ROWS, KV)
     by_y = exchange(jnp.broadcast_to(by_z[None], (NY, NZ * ROWS, KV)), "y")
     own = by_y.reshape(HALF, KV)
     other = lax.ppermute(own, "c", SWAP)
-    keep, send = kernel(partial_sums, [(HALF, KV)] * 2, 1 << 29, 3 << 20)(*work)
+    keep, send = kernel(partial_sums, [(HALF, KV)] * 2, 1 << 29, 3 << 20)(*far_first(work))
     got = lax.ppermute(send, "c", SWAP)
     (total,) = kernel(add_cores, [(HALF, KV)], 1 << 28, 3 << 19)(keep, got)
     total = exchange(total.reshape(NY, NZ * ROWS, KV), "y")
@@ -193,7 +189,7 @@
     )(own, other, *work)
     results = to_members(results)
     d_in = 4 * SLICE
-    keys, input_grad = kernel(finish, [(TOK, KV), (TOK, d_in)], 1 << 28, 3 << 20)(*results)
+    keys, input_grad = kernel(finish, [(TOK, KV), (TOK, d_in)], 1 << 28, 3 << 20)(*far_first(results))
     return keys, input_grad, weight_grad
 
 

time: 109 us -> 107 us (0.982)
  waiting for transfers between devices: 19.2 us -> 16.5 us
  blocking collectives: 14.4 us -> 16.1 us
  starting transfers between devices: 60.5 us -> 59 us
    all_to_all x3, waiting for transfers between devices: 15.5 us -> 13.4 us  [exchange(): return lax.all_to_all(blocks, axis, split_axis=0, concat_axis=0, tiled=True)]
    all_to_all x1, blocking collectives: 14.4 us -> 16.1 us  [exchange(): return lax.all_to_all(blocks, axis, split_axis=0, concat_axis=0, tiled=True)]
  transfers between devices with their start and end apart: 11 -> 11, of which waited for: 5 -> 4; matrix products, arithmetic and copies ran while one was open for 2% -> 3% of each run, Pallas kernels for 5% -> 5%
where the time goes in v5:
time: 107 us; the launch traced here: 105 us
  starting transfers between devices  59 us (55%)
  waiting for transfers between devices  16.5 us (15%)
  blocking collectives  16.1 us (15%)
  Pallas kernels  7.92 us (7%)
  local copies, waits for them, and re-layouts  3.01 us (3%)
  other arithmetic  1.75 us (2%)
    all_to_all x3, starting transfers between devices, exchange(): return lax.all_to_all(blocks, axis, split_axis=0, concat_axis=0, tiled=True)  29.7 us
    all_to_all x1, blocking collectives, exchange(): return lax.all_to_all(blocks, axis, split_axis=0, concat_axis=0, tiled=True)  16.1 us
    all_to_all x3, waiting for transfers between devices, exchange(): return lax.all_to_all(blocks, axis, split_axis=0, concat_axis=0, tiled=True)  13.4 us
    ppermute x2, starting transfers between devices, to_members(): lax.ppermute(blocks[2], 'xh', SWAP)  7.61 us
    ppermute x2, starting transfers between devices, to_members(): lax.ppermute(blocks[3], ('xh', 'xl'), [(0, 3), (1, 2), (2, 1), (3, 0)])  6.19 us
    ppermute x1, starting transfers between devices, shards(): other = lax.ppermute(own, 'c', SWAP)  5.63 us
    ppermute x2, starting transfers between devices, to_members(): lax.ppermute(blocks[1], 'xl', SWAP)  5.33 us
    ppermute x1, starting transfers between devices, shards(): got = lax.ppermute(send, 'c', SWAP)  4.58 us
  transfers between devices with their start and end apart: 11, of which 4 were waited for; matrix products, arithmetic and copies ran while one was open for 3% of the time, Pallas kernels for 5%

profile of v5, /device:TPU:1, one launch (start us, length us, event | category | flops | bytes accessed | tf_op | source)
XLA Modules:
  0.0 105.1 jit_solution(3914613118774291095)
XLA Ops:
  0.6 0.0 copy-start
  0.6 1.2 %copy-done = bf16[128,4096]{1,0:T(8,128)(2,1)S(1)} copy-done((bf16[128,4096]{1,0:T(8,128)(2,1)S(1)}, bf16[128,4096]{1,0:T(8,128)(2,1)}, u32[]{:S(2)}) %copy-start) | copy-done | bytes 1048600
  1.9 0.0 copy-start.1
  1.9 0.9 copy-done.1
  2.8 0.0 copy-start.2
  2.8 0.9 shard_map.68
  3.7 0.0 copy-start.3
  3.7 5.5 %collective-permute-start = (bf16[1536,128]{1,0:T(8,128)(2,1)S(1)}, bf16[1536,128]{1,0:T(8,128)(2,1)S(1)}, u32[]{:S(2)}, u32[]{:S(2)}) collective-permute-start(bf16[1536,128]{1,0:T(8,128)(2,1)S(1)} %get-tuple-element.17), channel_id=1, source_target_pairs={{0,512},{512,0},{1,513},{513,1},{2,514},{514,2},{3,515},{515,3},{4... | collective-permute-start | bytes 1179656 | tf_op jit(solution)/shard_map/ppermute | solution.py:164
  9.2 0.0 copy-done.2
  9.2 0.0 copy-done.3
  9.2 0.7 shard_map.67
  10.0 18.7 %all-to-all-start = ((bf16[16,4,512]{2,1,0:T(4,128)(2,1)}), bf16[16,4,512]{2,1,0:T(4,128)(2,1)S(1)}, u32[]{:S(2)}, u32[]{:S(2)}) async-start(bf16[16,4,512]{2,1,0:T(4,128)(2,1)} %shard_map.67), calls=%async_computation | async-start | bytes 131072 | tf_op jit(solution)/shard_map/all_to_all | solution.py:153
  28.7 2.2 %collective-permute-start.2 = (bf16[1536,128]{1,0:T(8,128)(2,1)S(1)}, bf16[1536,128]{1,0:T(8,128)(2,1)S(1)}, u32[]{:S(2)}, u32[]{:S(2)}) collective-permute-start(bf16[1536,128]{1,0:T(8,128)(2,1)S(1)} %get-tuple-element.20), channel_id=1, source_target_pairs={{0,32},{32,0},{1,33},{33,1},{2,34},{34,2},{3,35},{35,3},{4,36},{36... | collective-permute-start | bytes 1179656 | tf_op jit(solution)/shard_map/ppermute | solution.py:163
  30.9 2.5 %collective-permute-start.3 = (bf16[1536,128]{1,0:T(8,128)(2,1)S(1)}, bf16[1536,128]{1,0:T(8,128)(2,1)S(1)}, u32[]{:S(2)}, u32[]{:S(2)}) collective-permute-start(bf16[1536,128]{1,0:T(8,128)(2,1)S(1)} %get-tuple-element.22), channel_id=1, source_target_pairs={{0,544},{32,512},{512,32},{544,0},{1,545},{33,513},{513,33},{545,1... | collective-permute-start | bytes 1179656 | tf_op jit(solution)/shard_map/ppermute | solution.py:165
  33.4 6.9 %all-to-all-done = bf16[16,4,512]{2,1,0:T(4,128)(2,1)S(1)} async-done(((bf16[16,4,512]{2,1,0:T(4,128)(2,1)}), bf16[16,4,512]{2,1,0:T(4,128)(2,1)S(1)}, u32[]{:S(2)}, u32[]{:S(2)}) %all-to-all-start) | async-done | bytes 65568 | tf_op jit(solution)/shard_map/all_to_all | solution.py:153
  40.3 0.0 collective-permute-done.r2
  40.3 0.8 broadcast_in_dim.8
  41.1 6.8 %all-to-all-start.1 = ((bf16[8,64,512]{2,1,0:T(8,128)(2,1)}), bf16[8,64,512]{2,1,0:T(8,128)(2,1)S(1)}, u32[]{:S(2)}, u32[]{:S(2)}) async-start(bf16[8,64,512]{2,1,0:T(8,128)(2,1)} %broadcast_in_dim.8), calls=%async_computation.1 | async-start | bytes 1048576 | tf_op jit(solution)/shard_map/all_to_all | solution.py:153
  47.9 0.0 collective-permute-done.2.r1
  48.0 0.0 collective-permute-done.3.r3
  48.0 0.7 shard_map.71
  48.7 4.6 %collective-permute-start.7 = (bf16[512,512]{1,0:T(8,128)(2,1)S(1)}, bf16[512,512]{1,0:T(8,128)(2,1)S(1)}, u32[]{:S(2)}, u32[]{:S(2)}) collective-permute-start(bf16[512,512]{1,0:T(8,128)(2,1)S(1)} %get-tuple-element.30), channel_id=1, source_target_pairs={{0,1},{1,0},{2,3},{3,2},{4,5},{5,4},{6,7},{7,6},{8,9},{9,8},{10,11... | collective-permute-start | bytes 1572872 | tf_op jit(solution)/shard_map/ppermute | solution.py:181
  53.3 1.5 %collective-permute-done.7.b = bf16[512,512]{1,0:T(8,128)(2,1)S(1)} collective-permute-done((bf16[512,512]{1,0:T(8,128)(2,1)S(1)}, bf16[512,512]{1,0:T(8,128)(2,1)S(1)}, u32[]{:S(2)}, u32[]{:S(2)}) %collective-permute-start.7) | collective-permute-done | bytes 524320 | tf_op jit(solution)/shard_map/ppermute | solution.py:181
  54.8 1.3 %shard_map.72 = bf16[512,512]{1,0:T(8,128)(2,1)} custom-call(bf16[512,512]{1,0:T(8,128)(2,1)S(1)} %get-tuple-element.29.a, bf16[512,512]{1,0:T(8,128)(2,1)S(1)} %collective-permute-done.7.b), custom_call_target="tpu_custom_call" | custom-call | flops 268435456 | bytes 1572864 | tf_op jit(solution)/shard_map/pallas_call | solution.py:182
  56.1 6.6 %all-to-all-done.1 = bf16[8,64,512]{2,1,0:T(8,128)(2,1)S(1)} async-done(((bf16[8,64,512]{2,1,0:T(8,128)(2,1)}), bf16[8,64,512]{2,1,0:T(8,128)(2,1)S(1)}, u32[]{:S(2)}, u32[]{:S(2)}) %all-to-all-start.1) | async-done | bytes 524320 | tf_op jit(solution)/shard_map/all_to_all | solution.py:153
  62.7 4.1 %all-to-all-start.2 = ((bf16[8,64,512]{2,1,0:T(8,128)(2,1)}), bf16[8,64,512]{2,1,0:T(8,128)(2,1)}, u32[]{:S(2)}, u32[]{:S(2)}) async-start(bf16[8,64,512]{2,1,0:T(8,128)(2,1)} %bitcast.1), calls=%async_computation.2 | async-start | bytes 1048576 | tf_op jit(solution)/shard_map/all_to_all | solution.py:153
  66.8 5.6 %collective-permute-start.1 = (bf16[512,512]{1,0:T(8,128)(2,1)S(1)}, bf16[512,512]{1,0:T(8,128)(2,1)S(1)}, u32[]{:S(2)}, u32[]{:S(2)}) collective-permute-start(bf16[512,512]{1,0:T(8,128)(2,1)S(1)} %bitcast.2), channel_id=1, source_target_pairs={{0,1},{1,0},{2,3},{3,2},{4,5},{5,4},{6,7},{7,6},{8,9},{9,8},{10,11... | collective-permute-start | bytes 1572872 | tf_op jit(solution)/shard_map/ppermute | solution.py:179
  72.5 1.5 %collective-permute-done.1.other = bf16[512,512]{1,0:T(8,128)(2,1)S(1)} collective-permute-done((bf16[512,512]{1,0:T(8,128)(2,1)S(1)}, bf16[512,512]{1,0:T(8,128)(2,1)S(1)}, u32[]{:S(2)}, u32[]{:S(2)}) %collective-permute-start.1) | collective-permute-done | bytes 524320 | tf_op jit(solution)/shard_map/ppermute | solution.py:179
  74.0 2.7 %shard_map.69 = (bf16[1536,128]{1,0:T(8,128)(2,1)S(1)}, bf16[1536,128]{1,0:T(8,128)(2,1)S(1)}, bf16[1536,128]{1,0:T(8,128)(2,1)}, bf16[1536,128]{1,0:T(8,128)(2,1)S(1)}) custom-call(bf16[512,512]{1,0:T(8,128)(2,1)S(1)} %bitcast.3, bf16[512,512]{1,0:T(8,128)(2,1)S(1)} %collective-permute-done.1.other, bf16[1536,128]{1,0:T(8,128)(2,1)S(1)} %get-tuple-element.19.r0, ...), custom_call_target="tpu_custom_call" | custom-call | flops 1073741824 | bytes 4194304 | tf_op jit(solution)/shard_map/pallas_call | solution.py:187
  76.7 2.1 %collective-permute-start.4 = (bf16[1536,128]{1,0:T(8,128)(2,1)}, bf16[1536,128]{1,0:T(8,128)(2,1)S(1)}, u32[]{:S(2)}, u32[]{:S(2)}) collective-permute-start(bf16[1536,128]{1,0:T(8,128)(2,1)} %get-tuple-element.24), channel_id=1, source_target_pairs={{0,512},{512,0},{1,513},{513,1},{2,514},{514,2},{3,515},{515,3},{4... | collective-permute-start | bytes 1179656 | tf_op jit(solution)/shard_map/ppermute | solution.py:164
  78.8 3.1 %collective-permute-start.5 = (bf16[1536,128]{1,0:T(8,128)(2,1)S(1)}, bf16[1536,128]{1,0:T(8,128)(2,1)S(1)}, u32[]{:S(2)}, u32[]{:S(2)}) collective-permute-start(bf16[1536,128]{1,0:T(8,128)(2,1)S(1)} %get-tuple-element.25), channel_id=1, source_target_pairs={{0,32},{32,0},{1,33},{33,1},{2,34},{34,2},{3,35},{35,3},{4,36},{36... | collective-permute-start | bytes 1179656 | tf_op jit(solution)/shard_map/ppermute | solution.py:163
  81.9 3.7 %collective-permute-start.6 = (bf16[1536,128]{1,0:T(8,128)(2,1)S(1)}, bf16[1536,128]{1,0:T(8,128)(2,1)S(1)}, u32[]{:S(2)}, u32[]{:S(2)}) collective-permute-start(bf16[1536,128]{1,0:T(8,128)(2,1)S(1)} %get-tuple-element.26), channel_id=1, source_target_pairs={{0,544},{32,512},{512,32},{544,0},{1,545},{33,513},{513,33},{545,1... | collective-permute-start | bytes 1179656 | tf_op jit(solution)/shard_map/ppermute | solution.py:165
  85.7 0.0 all-to-all-done.2
  85.7 1.1 %reduce_sum.21 = bf16[64,512]{1,0:T(8,128)(2,1)S(1)} reduce(bf16[8,64,512]{2,1,0:T(8,128)(2,1)} %all-to-all-done.2, bf16[]{:T(256)} %constant.2.clone.1), dimensions={0}, to_apply=%region_0.0 | reduce | flops 229376 | bytes 589826 | tf_op jit(solution)/shard_map/reduce_sum | solution.py:184
  86.8 16.1 %all_to_all.20 = bf16[16,4,512]{2,1,0:T(4,128)(2,1)S(1)} all-to-all(bf16[16,4,512]{2,1,0:T(4,128)(2,1)S(1)} %reshape.18), channel_id=1, replica_groups=mesh['xh'=2,'y'=8,'xl'=2,'z'=16,'c'=2] {'z'}, dimensions={0} | all-to-all | bytes 131072 | tf_op jit(solution)/shard_map/all_to_all | solution.py:153
  102.9 0.6 convert_reduce_fusion
  103.5 0.0 collective-permute-done.4.f2
  103.5 0.0 collective-permute-done.5.f1
  103.5 0.0 collective-permute-done.6.f3
  103.5 1.5 %shard_map.70 = (bf16[128,512]{1,0:T(8,128)(2,1)}, bf16[128,4096]{1,0:T(8,128)(2,1)}) custom-call(bf16[1536,128]{1,0:T(8,128)(2,1)S(1)} %get-tuple-element.23.f0, bf16[1536,128]{1,0:T(8,128)(2,1)S(1)} %collective-permute-done.4.f2, bf16[1536,128]{1,0:T(8,128)(2,1)S(1)} %collective-permute-done.5.f1, bf16[1536,128]{1,0:T(8,128)(2,1)S(1)} %collective-permute-done.6.f3), custom_call_target="tpu_custom_call" | custom-call | flops 268435456 | bytes 3145728 | tf_op jit(solution)/shard_map/pallas_call | solution.py:192
  (2 shorter events, 0.0 us)
Async XLA Ops:
  0.6 1.2 %copy-start = (bf16[128,4096]{1,0:T(8,128)(2,1)S(1)}, bf16[128,4096]{1,0:T(8,128)(2,1)}, u32[]{:S(2)}) copy-start(bf16[128,4096]{1,0:T(8,128)(2,1)} %tok_ref.1) | copy-start | bytes 3145732
  1.9 0.9 copy-start.1
  2.8 6.5 %copy-start.2 = (bf16[4,512]{1,0:T(4,128)(2,1)S(1)}, bf16[4,512]{1,0:T(4,128)(2,1)}, u32[]{:S(2)}) copy-start(bf16[4,512]{1,0:T(4,128)(2,1)} %codes.1) | copy-start | bytes 12292
  3.7 5.5 %copy-start.3 = (bf16[4,4]{1,0:T(4,128)(2,1)S(1)}, bf16[4,4]{1,0:T(4,128)(2,1)}, u32[]{:S(2)}) copy-start(bf16[4,4]{1,0:T(4,128)(2,1)} %scales.1) | copy-start | bytes 100
  3.7 36.5 %collective-permute-start = (bf16[1536,128]{1,0:T(8,128)(2,1)S(1)}, bf16[1536,128]{1,0:T(8,128)(2,1)S(1)}, u32[]{:S(2)}, u32[]{:S(2)}) collective-permute-start(bf16[1536,128]{1,0:T(8,128)(2,1)S(1)} %get-tuple-element.17), channel_id=1, source_target_pairs={{0,512},{512,0},{1,513},{513,1},{2,514},{514,2},{3,515},{515,3},{4... | collective-permute-start | bytes 1179656 | tf_op jit(solution)/shard_map/ppermute | solution.py:164
  10.0 30.3 %all-to-all-start = ((bf16[16,4,512]{2,1,0:T(4,128)(2,1)}), bf16[16,4,512]{2,1,0:T(4,128)(2,1)S(1)}, u32[]{:S(2)}, u32[]{:S(2)}) async-start(bf16[16,4,512]{2,1,0:T(4,128)(2,1)} %shard_map.67), calls=%async_computation | async-start | bytes 131072 | tf_op jit(solution)/shard_map/all_to_all | solution.py:153
  28.7 19.3 %collective-permute-start.2 = (bf16[1536,128]{1,0:T(8,128)(2,1)S(1)}, bf16[1536,128]{1,0:T(8,128)(2,1)S(1)}, u32[]{:S(2)}, u32[]{:S(2)}) collective-permute-start(bf16[1536,128]{1,0:T(8,128)(2,1)S(1)} %get-tuple-element.20), channel_id=1, source_target_pairs={{0,32},{32,0},{1,33},{33,1},{2,34},{34,2},{3,35},{35,3},{4,36},{36... | collective-permute-start | bytes 1179656 | tf_op jit(solution)/shard_map/ppermute | solution.py:163
  30.9 17.1 %collective-permute-start.3 = (bf16[1536,128]{1,0:T(8,128)(2,1)S(1)}, bf16[1536,128]{1,0:T(8,128)(2,1)S(1)}, u32[]{:S(2)}, u32[]{:S(2)}) collective-permute-start(bf16[1536,128]{1,0:T(8,128)(2,1)S(1)} %get-tuple-element.22), channel_id=1, source_target_pairs={{0,544},{32,512},{512,32},{544,0},{1,545},{33,513},{513,33},{545,1... | collective-permute-start | bytes 1179656 | tf_op jit(solution)/shard_map/ppermute | solution.py:165
  41.1 21.5 %all-to-all-start.1 = ((bf16[8,64,512]{2,1,0:T(8,128)(2,1)}), bf16[8,64,512]{2,1,0:T(8,128)(2,1)S(1)}, u32[]{:S(2)}, u32[]{:S(2)}) async-start(bf16[8,64,512]{2,1,0:T(8,128)(2,1)} %broadcast_in_dim.8), calls=%async_computation.1 | async-start | bytes 1048576 | tf_op jit(solution)/shard_map/all_to_all | solution.py:153
  48.7 6.1 %collective-permute-start.7 = (bf16[512,512]{1,0:T(8,128)(2,1)S(1)}, bf16[512,512]{1,0:T(8,128)(2,1)S(1)}, u32[]{:S(2)}, u32[]{:S(2)}) collective-permute-start(bf16[512,512]{1,0:T(8,128)(2,1)S(1)} %get-tuple-element.30), channel_id=1, source_target_pairs={{0,1},{1,0},{2,3},{3,2},{4,5},{5,4},{6,7},{7,6},{8,9},{9,8},{10,11... | collective-permute-start | bytes 1572872 | tf_op jit(solution)/shard_map/ppermute | solution.py:181
  62.7 23.0 %all-to-all-start.2 = ((bf16[8,64,512]{2,1,0:T(8,128)(2,1)}), bf16[8,64,512]{2,1,0:T(8,128)(2,1)}, u32[]{:S(2)}, u32[]{:S(2)}) async-start(bf16[8,64,512]{2,1,0:T(8,128)(2,1)} %bitcast.1), calls=%async_computation.2 | async-start | bytes 1048576 | tf_op jit(solution)/shard_map/all_to_all | solution.py:153
  66.8 7.2 %collective-permute-start.1 = (bf16[512,512]{1,0:T(8,128)(2,1)S(1)}, bf16[512,512]{1,0:T(8,128)(2,1)S(1)}, u32[]{:S(2)}, u32[]{:S(2)}) collective-permute-start(bf16[512,512]{1,0:T(8,128)(2,1)S(1)} %bitcast.2), channel_id=1, source_target_pairs={{0,1},{1,0},{2,3},{3,2},{4,5},{5,4},{6,7},{7,6},{8,9},{9,8},{10,11... | collective-permute-start | bytes 1572872 | tf_op jit(solution)/shard_map/ppermute | solution.py:179
  76.7 26.9 %collective-permute-start.4 = (bf16[1536,128]{1,0:T(8,128)(2,1)}, bf16[1536,128]{1,0:T(8,128)(2,1)S(1)}, u32[]{:S(2)}, u32[]{:S(2)}) collective-permute-start(bf16[1536,128]{1,0:T(8,128)(2,1)} %get-tuple-element.24), channel_id=1, source_target_pairs={{0,512},{512,0},{1,513},{513,1},{2,514},{514,2},{3,515},{515,3},{4... | collective-permute-start | bytes 1179656 | tf_op jit(solution)/shard_map/ppermute | solution.py:164
  78.8 24.7 %collective-permute-start.5 = (bf16[1536,128]{1,0:T(8,128)(2,1)S(1)}, bf16[1536,128]{1,0:T(8,128)(2,1)S(1)}, u32[]{:S(2)}, u32[]{:S(2)}) collective-permute-start(bf16[1536,128]{1,0:T(8,128)(2,1)S(1)} %get-tuple-element.25), channel_id=1, source_target_pairs={{0,32},{32,0},{1,33},{33,1},{2,34},{34,2},{3,35},{35,3},{4,36},{36... | collective-permute-start | bytes 1179656 | tf_op jit(solution)/shard_map/ppermute | solution.py:163
  81.9 21.6 %collective-permute-start.6 = (bf16[1536,128]{1,0:T(8,128)(2,1)S(1)}, bf16[1536,128]{1,0:T(8,128)(2,1)S(1)}, u32[]{:S(2)}, u32[]{:S(2)}) collective-permute-start(bf16[1536,128]{1,0:T(8,128)(2,1)S(1)} %get-tuple-element.26), channel_id=1, source_target_pairs={{0,544},{32,512},{512,32},{544,0},{1,545},{33,513},{513,33},{545,1... | collective-permute-start | bytes 1179656 | tf_op jit(solution)/shard_map/ppermute | solution.py:165

commit v6 on v5

--- a/solution.py
+++ b/solution.py
@@ -75,7 +75,15 @@
             out[pl.ds(SLICE + b * 128, 128), :] = piece
 
 
-def scale_rows(codes, scales, copies):
+def scale_rows(codes_ref, scales_ref, copies, codes, scales, sems):
+    loads = [
+        pltpu.make_async_copy(codes_ref, codes, sems.at[0]),
+        pltpu.make_async_copy(scales_ref, scales, sems.at[1]),
+    ]
+    for load in loads:
+        load.start()
+    for load in loads:
+        load.wait()
     for b in range(KV // BLOCK):
         at = slice(b * BLOCK, (b + 1) * BLOCK)
         scaled = codes[:, at].astype(F32) * scales[:, b : b + 1].astype(F32)
@@ -138,12 +146,14 @@
             input_grad[:, pl.ds(pl.multiple_of(col + z * 128, 128), 128)] = block
 
 
-def kernel(body, outs, flops, moved, scratch=()):
+def kernel(body, outs, flops, moved, scratch=(), in_hbm=0, vmem=24):
+    pinned = [pl.BlockSpec(memory_space=pl.ANY)] * in_hbm
     return pl.pallas_call(
         body,
+        **({"in_specs": pinned} if in_hbm else {}),
         out_shape=[jax.ShapeDtypeStruct(s, BF16) for s in outs],
         scratch_shapes=list(scratch),
-        compiler_params=pltpu.CompilerParams(vmem_limit_bytes=24 * 1024 * 1024),
+        compiler_params=pltpu.CompilerParams(vmem_limit_bytes=vmem << 20),
         cost_estimate=pl.CostEstimate(flops=flops, bytes_accessed=moved, transcendentals=0),
         interpret=INTERPRET,
     )
@@ -167,29 +177,36 @@
 
 
 def shards(tokens, key_grad, codes, scales):
+    room = [
+        pltpu.VMEM((ROWS, KV), BF16),
+        pltpu.VMEM((ROWS, KV // BLOCK), BF16),
+        pltpu.SemaphoreType.DMA((2,)),
+    ]
+    (copies,) = kernel(scale_rows, [(NZ, ROWS, KV)], 1 << 12, 1 << 17, room, 2, 60)(codes, scales)
     blocks = kernel(prepare, [(PAY, TOK)] * 4, 1 << 28, 3 << 20)(tokens, key_grad)
     work = to_members(blocks)
-    (copies,) = kernel(scale_rows, [(NZ, ROWS, KV)], 1 << 12, 1 << 17)(codes, scales)
     by_z = exchange(copies, "z")
-    by_z, two = lax.optimization_barrier((by_z, work[2]))
-    work = (work[0], work[1], two, work[3])
     by_z = by_z.reshape(NZ * ROWS, KV)
     by_y = exchange(jnp.broadcast_to(by_z[None], (NY, NZ * ROWS, KV)), "y")
-    own = by_y.reshape(HALF, KV)
-    other = lax.ppermute(own, "c", SWAP)
     keep, send = kernel(partial_sums, [(HALF, KV)] * 2, 1 << 29, 3 << 20)(*far_first(work))
     got = lax.ppermute(send, "c", SWAP)
     (total,) = kernel(add_cores, [(HALF, KV)], 1 << 28, 3 << 19)(keep, got)
+    by_y, total = lax.optimization_barrier((by_y, total))
+    own = by_y.reshape(HALF, KV)
+    other = lax.ppermute(own, "c", SWAP)
     total = exchange(total.reshape(NY, NZ * ROWS, KV), "y")
     total = jnp.sum(total.astype(F32), axis=0).astype(BF16)
     total = exchange(total.reshape(NZ, ROWS, KV), "z")
-    weight_grad = jnp.sum(total.astype(F32), axis=0)
     results = kernel(
         apply_weight, [(PAY, TOK)] * 4, 1 << 30, 4 << 20, [pltpu.VMEM((SLICE, KV), BF16)]
     )(own, other, *work)
     results = to_members(results)
     d_in = 4 * SLICE
-    keys, input_grad = kernel(finish, [(TOK, KV), (TOK, d_in)], 1 << 28, 3 << 20)(*far_first(results))
+    keys, input_grad = kernel(finish, [(TOK, KV), (TOK, d_in)], 1 << 31, 3 << 20)(
+        *far_first(results)
+    )
+    total, keys, input_grad = lax.optimization_barrier((total, keys, input_grad))
+    weight_grad = jnp.sum(total.astype(F32), axis=0)
     return keys, input_grad, weight_grad
 
 

time: 107 us -> 110 us (1.028)
  blocking collectives: 16.1 us -> 0 us
  starting transfers between devices: 59 us -> 69.2 us
  waiting for transfers between devices: 16.5 us -> 24.8 us
    all_to_all x1 -> x0, blocking collectives: 16.1 us -> none  [exchange(): return lax.all_to_all(blocks, axis, split_axis=0, concat_axis=0, tiled=True)]
    all_to_all x3 -> x4, starting transfers between devices: 29.7 us -> 41.9 us  [exchange(): return lax.all_to_all(blocks, axis, split_axis=0, concat_axis=0, tiled=True)]
    all_to_all x3 -> x4, waiting for transfers between devices: 13.4 us -> 18.3 us  [exchange(): return lax.all_to_all(blocks, axis, split_axis=0, concat_axis=0, tiled=True)]
    ppermute x2, waiting for transfers between devices: 0.01 us -> 4.54 us  [to_members(): lax.ppermute(blocks[1], 'xl', SWAP)]
    ppermute x2, starting transfers between devices: 7.61 us -> 9.29 us  [to_members(): lax.ppermute(blocks[2], 'xh', SWAP)]
    ppermute x1, waiting for transfers between devices: 1.51 us -> 0.01 us  [shards(): other = lax.ppermute(own, 'c', SWAP)]
    ppermute x1, starting transfers between devices: 4.58 us -> 3.31 us  [shards(): got = lax.ppermute(send, 'c', SWAP)]
    ppermute x2, starting transfers between devices: 6.19 us -> 5.07 us  [to_members(): lax.ppermute(blocks[3], ('xh', 'xl'), [(0, 3), (1, 2), (2, 1), (3, 0)])]
  transfers between devices with their start and end apart: 11 -> 12, of which waited for: 4 -> 6; matrix products, arithmetic and copies ran while one was open for 3% -> 2% of each run, Pallas kernels for 5% -> 7%
where the time goes in v6:
time: 110 us; the launch traced here: 109 us
  starting transfers between devices  69.2 us (63%)
  waiting for transfers between devices  24.8 us (23%)
  Pallas kernels  8.67 us (8%)
  local copies, waits for them, and re-layouts  3.52 us (3%)
  other arithmetic  1.76 us (2%)
    all_to_all x4, starting transfers between devices, exchange(): return lax.all_to_all(blocks, axis, split_axis=0, concat_axis=0, tiled=True)  41.9 us
    all_to_all x4, waiting for transfers between devices, exchange(): return lax.all_to_all(blocks, axis, split_axis=0, concat_axis=0, tiled=True)  18.3 us
    ppermute x2, starting transfers between devices, to_members(): lax.ppermute(blocks[2], 'xh', SWAP)  9.29 us
    ppermute x1, starting transfers between devices, shards(): other = lax.ppermute(own, 'c', SWAP)  5.25 us
    ppermute x2, starting transfers between devices, to_members(): lax.ppermute(blocks[3], ('xh', 'xl'), [(0, 3), (1, 2), (2, 1), (3, 0)])  5.07 us
    ppermute x2, waiting for transfers between devices, to_members(): lax.ppermute(blocks[1], 'xl', SWAP)  4.54 us
    ppermute x2, starting transfers between devices, to_members(): lax.ppermute(blocks[1], 'xl', SWAP)  4.44 us
    ppermute x1, starting transfers between devices, shards(): got = lax.ppermute(send, 'c', SWAP)  3.31 us
  transfers between devices with their start and end apart: 12, of which 6 were waited for; matrix products, arithmetic and copies ran while one was open for 2% of the time, Pallas kernels for 7%

profile of v6, /device:TPU:1, one launch (start us, length us, event | category | flops | bytes accessed | tf_op | source)
XLA Modules:
  0.0 108.8 jit_solution(3543655279474811923)
XLA Ops:
  0.6 0.0 copy-start.1
  0.6 1.5 %shard_map.67 = bf16[16,4,512]{2,1,0:T(4,128)(2,1)} custom-call(bf16[4,512]{1,0:T(4,128)(2,1)} %codes_ref.1, bf16[4,4]{1,0:T(4,128)(2,1)} %scales_ref.1), custom_call_target="tpu_custom_call" | custom-call | flops 4096 | bytes 131072 | tf_op jit(solution)/shard_map/pallas_call | solution.py:185
  2.1 19.4 %all-to-all-start = ((bf16[16,4,512]{2,1,0:T(4,128)(2,1)}), bf16[16,4,512]{2,1,0:T(4,128)(2,1)S(1)}, u32[]{:S(2)}, u32[]{:S(2)}) async-start(bf16[16,4,512]{2,1,0:T(4,128)(2,1)} %shard_map.67), calls=%async_computation | async-start | bytes 131072 | tf_op jit(solution)/shard_map/all_to_all | solution.py:163
  21.5 0.0 copy-done.1
  21.6 0.0 copy-start
  21.6 1.2 %copy-done = bf16[128,4096]{1,0:T(8,128)(2,1)S(1)} copy-done((bf16[128,4096]{1,0:T(8,128)(2,1)S(1)}, bf16[128,4096]{1,0:T(8,128)(2,1)}, u32[]{:S(2)}) %copy-start) | copy-done | bytes 1048600
  22.8 0.9 shard_map.68
  23.7 4.7 %collective-permute-start = (bf16[1536,128]{1,0:T(8,128)(2,1)S(1)}, bf16[1536,128]{1,0:T(8,128)(2,1)S(1)}, u32[]{:S(2)}, u32[]{:S(2)}) collective-permute-start(bf16[1536,128]{1,0:T(8,128)(2,1)S(1)} %get-tuple-element.21), channel_id=1, source_target_pairs={{0,512},{512,0},{1,513},{513,1},{2,514},{514,2},{3,515},{515,3},{4... | collective-permute-start | bytes 1179656 | tf_op jit(solution)/shard_map/ppermute | solution.py:174
  28.4 2.2 %collective-permute-start.1 = (bf16[1536,128]{1,0:T(8,128)(2,1)S(1)}, bf16[1536,128]{1,0:T(8,128)(2,1)S(1)}, u32[]{:S(2)}, u32[]{:S(2)}) collective-permute-start(bf16[1536,128]{1,0:T(8,128)(2,1)S(1)} %get-tuple-element.22), channel_id=1, source_target_pairs={{0,32},{32,0},{1,33},{33,1},{2,34},{34,2},{3,35},{35,3},{4,36},{36... | collective-permute-start | bytes 1179656 | tf_op jit(solution)/shard_map/ppermute | solution.py:173
  30.6 2.5 %collective-permute-start.2 = (bf16[1536,128]{1,0:T(8,128)(2,1)S(1)}, bf16[1536,128]{1,0:T(8,128)(2,1)S(1)}, u32[]{:S(2)}, u32[]{:S(2)}) collective-permute-start(bf16[1536,128]{1,0:T(8,128)(2,1)S(1)} %get-tuple-element.23), channel_id=1, source_target_pairs={{0,544},{32,512},{512,32},{544,0},{1,545},{33,513},{513,33},{545,1... | collective-permute-start | bytes 1179656 | tf_op jit(solution)/shard_map/ppermute | solution.py:175
  33.1 0.0 all-to-all-done
  33.1 0.8 broadcast_in_dim.8
  34.0 6.8 %all-to-all-start.1 = ((bf16[8,64,512]{2,1,0:T(8,128)(2,1)}), bf16[8,64,512]{2,1,0:T(8,128)(2,1)S(1)}, u32[]{:S(2)}, u32[]{:S(2)}) async-start(bf16[8,64,512]{2,1,0:T(8,128)(2,1)} %broadcast_in_dim.8), calls=%async_computation.1 | async-start | bytes 1048576 | tf_op jit(solution)/shard_map/all_to_all | solution.py:163
  40.8 0.0 collective-permute-done.r2
  40.8 4.5 %collective-permute-done.1.r1 = bf16[1536,128]{1,0:T(8,128)(2,1)S(1)} collective-permute-done((bf16[1536,128]{1,0:T(8,128)(2,1)S(1)}, bf16[1536,128]{1,0:T(8,128)(2,1)S(1)}, u32[]{:S(2)}, u32[]{:S(2)}) %collective-permute-start.1) | collective-permute-done | bytes 393248 | tf_op jit(solution)/shard_map/ppermute | solution.py:173
  45.3 0.5 collective-permute-done.2.r3
  45.8 0.7 shard_map.69
  46.6 3.3 %collective-permute-start.3 = (bf16[512,512]{1,0:T(8,128)(2,1)S(1)}, bf16[512,512]{1,0:T(8,128)(2,1)S(1)}, u32[]{:S(2)}, u32[]{:S(2)}) collective-permute-start(bf16[512,512]{1,0:T(8,128)(2,1)S(1)} %get-tuple-element.25), channel_id=1, source_target_pairs={{0,1},{1,0},{2,3},{3,2},{4,5},{5,4},{6,7},{7,6},{8,9},{9,8},{10,11... | collective-permute-start | bytes 1572872 | tf_op jit(solution)/shard_map/ppermute | solution.py:192
  49.9 1.5 %collective-permute-done.3.b = bf16[512,512]{1,0:T(8,128)(2,1)S(1)} collective-permute-done((bf16[512,512]{1,0:T(8,128)(2,1)S(1)}, bf16[512,512]{1,0:T(8,128)(2,1)S(1)}, u32[]{:S(2)}, u32[]{:S(2)}) %collective-permute-start.3) | collective-permute-done | bytes 524320 | tf_op jit(solution)/shard_map/ppermute | solution.py:192
  51.4 1.3 %shard_map.70 = bf16[512,512]{1,0:T(8,128)(2,1)} custom-call(bf16[512,512]{1,0:T(8,128)(2,1)S(1)} %get-tuple-element.24.a, bf16[512,512]{1,0:T(8,128)(2,1)S(1)} %collective-permute-done.3.b), custom_call_target="tpu_custom_call" | custom-call | flops 268435456 | bytes 1572864 | tf_op jit(solution)/shard_map/pallas_call | solution.py:193
  52.7 3.2 %all-to-all-done.1 = bf16[8,64,512]{2,1,0:T(8,128)(2,1)S(1)} async-done(((bf16[8,64,512]{2,1,0:T(8,128)(2,1)}), bf16[8,64,512]{2,1,0:T(8,128)(2,1)S(1)}, u32[]{:S(2)}, u32[]{:S(2)}) %all-to-all-start.1) | async-done | bytes 524320 | tf_op jit(solution)/shard_map/all_to_all | solution.py:163
  55.9 5.2 %collective-permute-start.4 = (bf16[512,512]{1,0:T(8,128)(2,1)S(1)}, bf16[512,512]{1,0:T(8,128)(2,1)S(1)}, u32[]{:S(2)}, u32[]{:S(2)}) collective-permute-start(bf16[512,512]{1,0:T(8,128)(2,1)S(1)} %bitcast.2), channel_id=1, source_target_pairs={{0,1},{1,0},{2,3},{3,2},{4,5},{5,4},{6,7},{7,6},{8,9},{9,8},{10,11... | collective-permute-start | bytes 1572872 | tf_op jit(solution)/shard_map/ppermute | solution.py:196
  61.2 4.2 %all-to-all-start.2 = ((bf16[8,64,512]{2,1,0:T(8,128)(2,1)}), bf16[8,64,512]{2,1,0:T(8,128)(2,1)}, u32[]{:S(2)}, u32[]{:S(2)}) async-start(bf16[8,64,512]{2,1,0:T(8,128)(2,1)} %bitcast), calls=%async_computation.2 | async-start | bytes 1048576 | tf_op jit(solution)/shard_map/all_to_all | solution.py:163
  65.3 0.0 collective-permute-done.4.other
  65.3 2.7 %shard_map.71 = (bf16[1536,128]{1,0:T(8,128)(2,1)S(1)}, bf16[1536,128]{1,0:T(8,128)(2,1)S(1)}, bf16[1536,128]{1,0:T(8,128)(2,1)}, bf16[1536,128]{1,0:T(8,128)(2,1)S(1)}) custom-call(bf16[512,512]{1,0:T(8,128)(2,1)S(1)} %bitcast.3, bf16[512,512]{1,0:T(8,128)(2,1)S(1)} %collective-permute-done.4.other, bf16[1536,128]{1,0:T(8,128)(2,1)S(1)} %get-tuple-element.20.r0, ...), custom_call_target="tpu_custom_call" | custom-call | flops 1073741824 | bytes 4194304 | tf_op jit(solution)/shard_map/pallas_call | solution.py:200
  68.0 0.0 copy-start.2
  68.0 0.8 copy-done.2
  68.8 4.6 %collective-permute-start.5 = (bf16[1536,128]{1,0:T(8,128)(2,1)}, bf16[1536,128]{1,0:T(8,128)(2,1)S(1)}, u32[]{:S(2)}, u32[]{:S(2)}) collective-permute-start(bf16[1536,128]{1,0:T(8,128)(2,1)} %get-tuple-element.29), channel_id=1, source_target_pairs={{0,512},{512,0},{1,513},{513,1},{2,514},{514,2},{3,515},{515,3},{4... | collective-permute-start | bytes 1179656 | tf_op jit(solution)/shard_map/ppermute | solution.py:174
  73.5 2.2 %collective-permute-start.6 = (bf16[1536,128]{1,0:T(8,128)(2,1)S(1)}, bf16[1536,128]{1,0:T(8,128)(2,1)S(1)}, u32[]{:S(2)}, u32[]{:S(2)}) collective-permute-start(bf16[1536,128]{1,0:T(8,128)(2,1)S(1)} %get-tuple-element.30), channel_id=1, source_target_pairs={{0,32},{32,0},{1,33},{33,1},{2,34},{34,2},{3,35},{35,3},{4,36},{36... | collective-permute-start | bytes 1179656 | tf_op jit(solution)/shard_map/ppermute | solution.py:173
  75.7 0.0 copy-start.3
  75.7 2.6 %collective-permute-start.7 = (bf16[1536,128]{1,0:T(8,128)(2,1)S(1)}, bf16[1536,128]{1,0:T(8,128)(2,1)S(1)}, u32[]{:S(2)}, u32[]{:S(2)}) collective-permute-start(bf16[1536,128]{1,0:T(8,128)(2,1)S(1)} %get-tuple-element.31), channel_id=1, source_target_pairs={{0,544},{32,512},{512,32},{544,0},{1,545},{33,513},{513,33},{545,1... | collective-permute-start | bytes 1179656 | tf_op jit(solution)/shard_map/ppermute | solution.py:175
  78.3 5.1 %all-to-all-done.2 = bf16[8,64,512]{2,1,0:T(8,128)(2,1)} async-done(((bf16[8,64,512]{2,1,0:T(8,128)(2,1)}), bf16[8,64,512]{2,1,0:T(8,128)(2,1)}, u32[]{:S(2)}, u32[]{:S(2)}) %all-to-all-start.2) | async-done | bytes 524320 | tf_op jit(solution)/shard_map/all_to_all | solution.py:163
  83.4 1.1 %reduce_sum.21 = bf16[64,512]{1,0:T(8,128)(2,1)S(1)} reduce(bf16[8,64,512]{2,1,0:T(8,128)(2,1)} %all-to-all-done.2, bf16[]{:T(256)} %constant.2.clone.1), dimensions={0}, to_apply=%region_0.0 | reduce | flops 229376 | bytes 589826 | tf_op jit(solution)/shard_map/reduce_sum | solution.py:198
  84.5 0.7 reshape.17
  85.2 11.5 %all-to-all-start.3 = ((bf16[16,4,512]{2,1,0:T(4,128)(2,1)}), bf16[16,4,512]{2,1,0:T(4,128)(2,1)S(1)}, u32[]{:S(2)}, u32[]{:S(2)}) async-start(bf16[16,4,512]{2,1,0:T(4,128)(2,1)} %reshape.17), calls=%async_computation.3 | async-start | bytes 131072 | tf_op jit(solution)/shard_map/all_to_all | solution.py:163
  96.6 0.0 collective-permute-done.5.f2
  96.6 0.0 collective-permute-done.6.f1
  96.6 0.0 collective-permute-done.7.f3
  96.6 0.0 copy-done.3
  96.7 1.5 %shard_map.72 = (bf16[128,512]{1,0:T(8,128)(2,1)}, bf16[128,4096]{1,0:T(8,128)(2,1)}) custom-call(bf16[1536,128]{1,0:T(8,128)(2,1)S(1)} %copy-done.3, bf16[1536,128]{1,0:T(8,128)(2,1)S(1)} %collective-permute-done.5.f2, bf16[1536,128]{1,0:T(8,128)(2,1)S(1)} %collective-permute-done.6.f1, bf16[1536,128]{1,0:T(8,128)(2,1)S(1)} %collective-permute-done.7.f3), custom_call_target="tpu_custom_call" | custom-call | flops 2147483648 | bytes 3145728 | tf_op jit(solution)/shard_map/pallas_call | solution.py:205
  98.2 10.0 %all-to-all-done.3 = bf16[16,4,512]{2,1,0:T(4,128)(2,1)S(1)} async-done(((bf16[16,4,512]{2,1,0:T(4,128)(2,1)}), bf16[16,4,512]{2,1,0:T(4,128)(2,1)S(1)}, u32[]{:S(2)}, u32[]{:S(2)}) %all-to-all-start.3) | async-done | bytes 65568 | tf_op jit(solution)/shard_map/all_to_all | solution.py:163
  108.2 0.6 convert_reduce_fusion
  (1 shorter events, 0.0 us)
Async XLA Ops:
  0.6 20.9 %copy-start.1 = (bf16[128,512]{1,0:T(8,128)(2,1)S(1)}, bf16[128,512]{1,0:T(8,128)(2,1)}, u32[]{:S(2)}) copy-start(bf16[128,512]{1,0:T(8,128)(2,1)} %grad_ref.1) | copy-start | bytes 393220
  2.1 31.0 %all-to-all-start = ((bf16[16,4,512]{2,1,0:T(4,128)(2,1)}), bf16[16,4,512]{2,1,0:T(4,128)(2,1)S(1)}, u32[]{:S(2)}, u32[]{:S(2)}) async-start(bf16[16,4,512]{2,1,0:T(4,128)(2,1)} %shard_map.67), calls=%async_computation | async-start | bytes 131072 | tf_op jit(solution)/shard_map/all_to_all | solution.py:163
  21.6 1.2 %copy-start = (bf16[128,4096]{1,0:T(8,128)(2,1)S(1)}, bf16[128,4096]{1,0:T(8,128)(2,1)}, u32[]{:S(2)}) copy-start(bf16[128,4096]{1,0:T(8,128)(2,1)} %tok_ref.1) | copy-start | bytes 3145732
  23.7 17.1 %collective-permute-start = (bf16[1536,128]{1,0:T(8,128)(2,1)S(1)}, bf16[1536,128]{1,0:T(8,128)(2,1)S(1)}, u32[]{:S(2)}, u32[]{:S(2)}) collective-permute-start(bf16[1536,128]{1,0:T(8,128)(2,1)S(1)} %get-tuple-element.21), channel_id=1, source_target_pairs={{0,512},{512,0},{1,513},{513,1},{2,514},{514,2},{3,515},{515,3},{4... | collective-permute-start | bytes 1179656 | tf_op jit(solution)/shard_map/ppermute | solution.py:174
  28.4 17.0 %collective-permute-start.1 = (bf16[1536,128]{1,0:T(8,128)(2,1)S(1)}, bf16[1536,128]{1,0:T(8,128)(2,1)S(1)}, u32[]{:S(2)}, u32[]{:S(2)}) collective-permute-start(bf16[1536,128]{1,0:T(8,128)(2,1)S(1)} %get-tuple-element.22), channel_id=1, source_target_pairs={{0,32},{32,0},{1,33},{33,1},{2,34},{34,2},{3,35},{35,3},{4,36},{36... | collective-permute-start | bytes 1179656 | tf_op jit(solution)/shard_map/ppermute | solution.py:173
  30.6 15.2 %collective-permute-start.2 = (bf16[1536,128]{1,0:T(8,128)(2,1)S(1)}, bf16[1536,128]{1,0:T(8,128)(2,1)S(1)}, u32[]{:S(2)}, u32[]{:S(2)}) collective-permute-start(bf16[1536,128]{1,0:T(8,128)(2,1)S(1)} %get-tuple-element.23), channel_id=1, source_target_pairs={{0,544},{32,512},{512,32},{544,0},{1,545},{33,513},{513,33},{545,1... | collective-permute-start | bytes 1179656 | tf_op jit(solution)/shard_map/ppermute | solution.py:175
  34.0 21.9 %all-to-all-start.1 = ((bf16[8,64,512]{2,1,0:T(8,128)(2,1)}), bf16[8,64,512]{2,1,0:T(8,128)(2,1)S(1)}, u32[]{:S(2)}, u32[]{:S(2)}) async-start(bf16[8,64,512]{2,1,0:T(8,128)(2,1)} %broadcast_in_dim.8), calls=%async_computation.1 | async-start | bytes 1048576 | tf_op jit(solution)/shard_map/all_to_all | solution.py:163
  46.6 4.8 %collective-permute-start.3 = (bf16[512,512]{1,0:T(8,128)(2,1)S(1)}, bf16[512,512]{1,0:T(8,128)(2,1)S(1)}, u32[]{:S(2)}, u32[]{:S(2)}) collective-permute-start(bf16[512,512]{1,0:T(8,128)(2,1)S(1)} %get-tuple-element.25), channel_id=1, source_target_pairs={{0,1},{1,0},{2,3},{3,2},{4,5},{5,4},{6,7},{7,6},{8,9},{9,8},{10,11... | collective-permute-start | bytes 1572872 | tf_op jit(solution)/shard_map/ppermute | solution.py:192
  55.9 9.4 %collective-permute-start.4 = (bf16[512,512]{1,0:T(8,128)(2,1)S(1)}, bf16[512,512]{1,0:T(8,128)(2,1)S(1)}, u32[]{:S(2)}, u32[]{:S(2)}) collective-permute-start(bf16[512,512]{1,0:T(8,128)(2,1)S(1)} %bitcast.2), channel_id=1, source_target_pairs={{0,1},{1,0},{2,3},{3,2},{4,5},{5,4},{6,7},{7,6},{8,9},{9,8},{10,11... | collective-permute-start | bytes 1572872 | tf_op jit(solution)/shard_map/ppermute | solution.py:196
  61.2 22.2 %all-to-all-start.2 = ((bf16[8,64,512]{2,1,0:T(8,128)(2,1)}), bf16[8,64,512]{2,1,0:T(8,128)(2,1)}, u32[]{:S(2)}, u32[]{:S(2)}) async-start(bf16[8,64,512]{2,1,0:T(8,128)(2,1)} %bitcast), calls=%async_computation.2 | async-start | bytes 1048576 | tf_op jit(solution)/shard_map/all_to_all | solution.py:163
  68.0 0.8 copy-start.2
  68.8 27.8 %collective-permute-start.5 = (bf16[1536,128]{1,0:T(8,128)(2,1)}, bf16[1536,128]{1,0:T(8,128)(2,1)S(1)}, u32[]{:S(2)}, u32[]{:S(2)}) collective-permute-start(bf16[1536,128]{1,0:T(8,128)(2,1)} %get-tuple-element.29), channel_id=1, source_target_pairs={{0,512},{512,0},{1,513},{513,1},{2,514},{514,2},{3,515},{515,3},{4... | collective-permute-start | bytes 1179656 | tf_op jit(solution)/shard_map/ppermute | solution.py:174
  73.5 23.2 %collective-permute-start.6 = (bf16[1536,128]{1,0:T(8,128)(2,1)S(1)}, bf16[1536,128]{1,0:T(8,128)(2,1)S(1)}, u32[]{:S(2)}, u32[]{:S(2)}) collective-permute-start(bf16[1536,128]{1,0:T(8,128)(2,1)S(1)} %get-tuple-element.30), channel_id=1, source_target_pairs={{0,32},{32,0},{1,33},{33,1},{2,34},{34,2},{3,35},{35,3},{4,36},{36... | collective-permute-start | bytes 1179656 | tf_op jit(solution)/shard_map/ppermute | solution.py:173
  75.7 20.9 %copy-start.3 = (bf16[1536,128]{1,0:T(8,128)(2,1)S(1)}, bf16[1536,128]{1,0:T(8,128)(2,1)}, u32[]{:S(2)}) copy-start(bf16[1536,128]{1,0:T(8,128)(2,1)} %copy-done.2) | copy-start | bytes 1179652
  75.7 20.9 %collective-permute-start.7 = (bf16[1536,128]{1,0:T(8,128)(2,1)S(1)}, bf16[1536,128]{1,0:T(8,128)(2,1)S(1)}, u32[]{:S(2)}, u32[]{:S(2)}) collective-permute-start(bf16[1536,128]{1,0:T(8,128)(2,1)S(1)} %get-tuple-element.31), channel_id=1, source_target_pairs={{0,544},{32,512},{512,32},{544,0},{1,545},{33,513},{513,33},{545,1... | collective-permute-start | bytes 1179656 | tf_op jit(solution)/shard_map/ppermute | solution.py:175
  85.2 23.0 %all-to-all-start.3 = ((bf16[16,4,512]{2,1,0:T(4,128)(2,1)}), bf16[16,4,512]{2,1,0:T(4,128)(2,1)S(1)}, u32[]{:S(2)}, u32[]{:S(2)}) async-start(bf16[16,4,512]{2,1,0:T(4,128)(2,1)} %reshape.17), calls=%async_computation.3 | async-start | bytes 131072 | tf_op jit(solution)/shard_map/all_to_all | solution.py:163

commit v7 on v6

--- a/solution.py
+++ b/solution.py
@@ -103,6 +103,12 @@
 def add_cores(a, b, out):
     total = (a[...].astype(F32) + b[...].astype(F32)).astype(BF16)
     out[...] = dot(y_outer(), total, NN).astype(BF16)
+
+
+def sum_over_y(blocks, out):
+    total = jnp.sum(blocks[...].astype(F32), axis=0)
+    for z in range(NZ):
+        out[z] = total[z * ROWS : (z + 1) * ROWS].astype(BF16)
 
 
 def apply_weight(own, other, r0, r1, r2, r3, o0, o1, o2, o3, weight):
@@ -195,18 +201,19 @@
     own = by_y.reshape(HALF, KV)
     other = lax.ppermute(own, "c", SWAP)
     total = exchange(total.reshape(NY, NZ * ROWS, KV), "y")
-    total = jnp.sum(total.astype(F32), axis=0).astype(BF16)
-    total = exchange(total.reshape(NZ, ROWS, KV), "z")
+    (total,) = kernel(sum_over_y, [(NZ, ROWS, KV)], 1 << 18, 1 << 20)(total)
+    total = exchange(total, "z")
     results = kernel(
         apply_weight, [(PAY, TOK)] * 4, 1 << 30, 4 << 20, [pltpu.VMEM((SLICE, KV), BF16)]
     )(own, other, *work)
     results = to_members(results)
+    total, mine = lax.optimization_barrier((total, results[0]))
+    results = (mine, *results[1:])
+    weight_grad = jnp.sum(total.astype(F32), axis=0)
     d_in = 4 * SLICE
-    keys, input_grad = kernel(finish, [(TOK, KV), (TOK, d_in)], 1 << 31, 3 << 20)(
+    keys, input_grad = kernel(finish, [(TOK, KV), (TOK, d_in)], 1 << 28, 3 << 20)(
         *far_first(results)
     )
-    total, keys, input_grad = lax.optimization_barrier((total, keys, input_grad))
-    weight_grad = jnp.sum(total.astype(F32), axis=0)
     return keys, input_grad, weight_grad
 
 

time: 110 us -> 105 us (0.955)
  blocking collectives: 0 us -> 22.6 us
  waiting for transfers between devices: 24.8 us -> 11.3 us
  starting transfers between devices: 69.2 us -> 57 us
  local copies, waits for them, and re-layouts: 3.52 us -> 2.08 us
  other arithmetic: 1.76 us -> 0.64 us
    all_to_all x0 -> x1, blocking collectives: none -> 22.6 us  [exchange(): return lax.all_to_all(blocks, axis, split_axis=0, concat_axis=0, tiled=True)]
    all_to_all x4 -> x3, waiting for transfers between devices: 18.3 us -> 3.22 us  [exchange(): return lax.all_to_all(blocks, axis, split_axis=0, concat_axis=0, tiled=True)]
    all_to_all x4 -> x3, starting transfers between devices: 41.9 us -> 29.9 us  [exchange(): return lax.all_to_all(blocks, axis, split_axis=0, concat_axis=0, tiled=True)]
    ppermute x1, waiting for transfers between devices: 0.01 us -> 1.51 us  [shards(): other = lax.ppermute(own, 'c', SWAP)]
    reduce_sum x1 -> x0, other arithmetic: 1.12 us -> none  [shards(): total = jnp.sum(total.astype(F32), axis=0).astype(BF16)]
  transfers between devices with their start and end apart: 12 -> 11, of which waited for: 6 -> 5; matrix products, arithmetic and copies ran while one was open for 2% -> 1% of each run, Pallas kernels for 7% -> 6%
where the time goes in v7:
time: 105 us; the launch traced here: 103 us
  starting transfers between devices  57 us (54%)
  blocking collectives  22.6 us (22%)
  waiting for transfers between devices  11.3 us (11%)
  Pallas kernels  8.85 us (8%)
  local copies, waits for them, and re-layouts  2.08 us (2%)
    all_to_all x3, starting transfers between devices, exchange(): return lax.all_to_all(blocks, axis, split_axis=0, concat_axis=0, tiled=True)  29.9 us
    all_to_all x1, blocking collectives, exchange(): return lax.all_to_all(blocks, axis, split_axis=0, concat_axis=0, tiled=True)  22.6 us
    ppermute x2, starting transfers between devices, to_members(): lax.ppermute(blocks[2], 'xh', SWAP)  9.3 us
    ppermute x1, starting transfers between devices, shards(): other = lax.ppermute(own, 'c', SWAP)  5.13 us
    ppermute x2, starting transfers between devices, to_members(): lax.ppermute(blocks[3], ('xh', 'xl'), [(0, 3), (1, 2), (2, 1), (3, 0)])  4.94 us
    ppermute x2, waiting for transfers between devices, to_members(): lax.ppermute(blocks[1], 'xl', SWAP)  4.54 us
    ppermute x2, starting transfers between devices, to_members(): lax.ppermute(blocks[1], 'xl', SWAP)  4.44 us
    ppermute x1, starting transfers between devices, shards(): got = lax.ppermute(send, 'c', SWAP)  3.31 us
  transfers between devices with their start and end apart: 11, of which 5 were waited for; matrix products, arithmetic and copies ran while one was open for 1% of the time, Pallas kernels for 6%

profile of v7, /device:TPU:1, one launch (start us, length us, event | category | flops | bytes accessed | tf_op | source)
XLA Modules:
  0.0 103.2 jit_solution(13665374780753319727)
XLA Ops:
  0.6 0.0 copy-start.1
  0.6 1.5 %shard_map.67 = bf16[16,4,512]{2,1,0:T(4,128)(2,1)} custom-call(bf16[4,512]{1,0:T(4,128)(2,1)} %codes_ref.1, bf16[4,4]{1,0:T(4,128)(2,1)} %scales_ref.1), custom_call_target="tpu_custom_call" | custom-call | flops 4096 | bytes 131072 | tf_op jit(solution)/shard_map/pallas_call | solution.py:191
  2.1 19.4 %all-to-all-start = ((bf16[16,4,512]{2,1,0:T(4,128)(2,1)}), bf16[16,4,512]{2,1,0:T(4,128)(2,1)S(1)}, u32[]{:S(2)}, u32[]{:S(2)}) async-start(bf16[16,4,512]{2,1,0:T(4,128)(2,1)} %shard_map.67), calls=%async_computation | async-start | bytes 131072 | tf_op jit(solution)/shard_map/all_to_all | solution.py:169
  21.5 0.0 copy-done.1
  21.6 0.0 copy-start
  21.6 1.2 %copy-done = bf16[128,4096]{1,0:T(8,128)(2,1)S(1)} copy-done((bf16[128,4096]{1,0:T(8,128)(2,1)S(1)}, bf16[128,4096]{1,0:T(8,128)(2,1)}, u32[]{:S(2)}) %copy-start) | copy-done | bytes 1048600
  22.8 0.9 shard_map.68
  23.7 4.7 %collective-permute-start = (bf16[1536,128]{1,0:T(8,128)(2,1)S(1)}, bf16[1536,128]{1,0:T(8,128)(2,1)S(1)}, u32[]{:S(2)}, u32[]{:S(2)}) collective-permute-start(bf16[1536,128]{1,0:T(8,128)(2,1)S(1)} %get-tuple-element.20), channel_id=1, source_target_pairs={{0,512},{512,0},{1,513},{513,1},{2,514},{514,2},{3,515},{515,3},{4... | collective-permute-start | bytes 1179656 | tf_op jit(solution)/shard_map/ppermute | solution.py:180
  28.4 2.2 %collective-permute-start.1 = (bf16[1536,128]{1,0:T(8,128)(2,1)S(1)}, bf16[1536,128]{1,0:T(8,128)(2,1)S(1)}, u32[]{:S(2)}, u32[]{:S(2)}) collective-permute-start(bf16[1536,128]{1,0:T(8,128)(2,1)S(1)} %get-tuple-element.21), channel_id=1, source_target_pairs={{0,32},{32,0},{1,33},{33,1},{2,34},{34,2},{3,35},{35,3},{4,36},{36... | collective-permute-start | bytes 1179656 | tf_op jit(solution)/shard_map/ppermute | solution.py:179
  30.6 2.5 %collective-permute-start.2 = (bf16[1536,128]{1,0:T(8,128)(2,1)S(1)}, bf16[1536,128]{1,0:T(8,128)(2,1)S(1)}, u32[]{:S(2)}, u32[]{:S(2)}) collective-permute-start(bf16[1536,128]{1,0:T(8,128)(2,1)S(1)} %get-tuple-element.22), channel_id=1, source_target_pairs={{0,544},{32,512},{512,32},{544,0},{1,545},{33,513},{513,33},{545,1... | collective-permute-start | bytes 1179656 | tf_op jit(solution)/shard_map/ppermute | solution.py:181
  33.1 0.0 all-to-all-done
  33.1 0.8 broadcast_in_dim.8
  34.0 6.8 %all-to-all-start.1 = ((bf16[8,64,512]{2,1,0:T(8,128)(2,1)}), bf16[8,64,512]{2,1,0:T(8,128)(2,1)S(1)}, u32[]{:S(2)}, u32[]{:S(2)}) async-start(bf16[8,64,512]{2,1,0:T(8,128)(2,1)} %broadcast_in_dim.8), calls=%async_computation.1 | async-start | bytes 1048576 | tf_op jit(solution)/shard_map/all_to_all | solution.py:169
  40.8 0.0 collective-permute-done.r2
  40.8 4.5 %collective-permute-done.1.r1 = bf16[1536,128]{1,0:T(8,128)(2,1)S(1)} collective-permute-done((bf16[1536,128]{1,0:T(8,128)(2,1)S(1)}, bf16[1536,128]{1,0:T(8,128)(2,1)S(1)}, u32[]{:S(2)}, u32[]{:S(2)}) %collective-permute-start.1) | collective-permute-done | bytes 393248 | tf_op jit(solution)/shard_map/ppermute | solution.py:179
  45.3 0.5 collective-permute-done.2.r3
  45.8 0.7 shard_map.69
  46.6 3.3 %collective-permute-start.3 = (bf16[512,512]{1,0:T(8,128)(2,1)S(1)}, bf16[512,512]{1,0:T(8,128)(2,1)S(1)}, u32[]{:S(2)}, u32[]{:S(2)}) collective-permute-start(bf16[512,512]{1,0:T(8,128)(2,1)S(1)} %get-tuple-element.24), channel_id=1, source_target_pairs={{0,1},{1,0},{2,3},{3,2},{4,5},{5,4},{6,7},{7,6},{8,9},{9,8},{10,11... | collective-permute-start | bytes 1572872 | tf_op jit(solution)/shard_map/ppermute | solution.py:198
  49.9 1.5 %collective-permute-done.3.b = bf16[512,512]{1,0:T(8,128)(2,1)S(1)} collective-permute-done((bf16[512,512]{1,0:T(8,128)(2,1)S(1)}, bf16[512,512]{1,0:T(8,128)(2,1)S(1)}, u32[]{:S(2)}, u32[]{:S(2)}) %collective-permute-start.3) | collective-permute-done | bytes 524320 | tf_op jit(solution)/shard_map/ppermute | solution.py:198
  51.4 1.3 %shard_map.70 = bf16[512,512]{1,0:T(8,128)(2,1)} custom-call(bf16[512,512]{1,0:T(8,128)(2,1)S(1)} %get-tuple-element.23.a, bf16[512,512]{1,0:T(8,128)(2,1)S(1)} %collective-permute-done.3.b), custom_call_target="tpu_custom_call" | custom-call | flops 268435456 | bytes 1572864 | tf_op jit(solution)/shard_map/pallas_call | solution.py:199
  52.7 3.2 %all-to-all-done.1 = bf16[8,64,512]{2,1,0:T(8,128)(2,1)S(1)} async-done(((bf16[8,64,512]{2,1,0:T(8,128)(2,1)}), bf16[8,64,512]{2,1,0:T(8,128)(2,1)S(1)}, u32[]{:S(2)}, u32[]{:S(2)}) %all-to-all-start.1) | async-done | bytes 524320 | tf_op jit(solution)/shard_map/all_to_all | solution.py:169
  55.9 3.6 %all-to-all-start.2 = ((bf16[8,64,512]{2,1,0:T(8,128)(2,1)}), bf16[8,64,512]{2,1,0:T(8,128)(2,1)S(1)}, u32[]{:S(2)}, u32[]{:S(2)}) async-start(bf16[8,64,512]{2,1,0:T(8,128)(2,1)} %bitcast), calls=%async_computation.2 | async-start | bytes 1048576 | tf_op jit(solution)/shard_map/all_to_all | solution.py:169
  59.5 5.1 %collective-permute-start.4 = (bf16[512,512]{1,0:T(8,128)(2,1)S(1)}, bf16[512,512]{1,0:T(8,128)(2,1)S(1)}, u32[]{:S(2)}, u32[]{:S(2)}) collective-permute-start(bf16[512,512]{1,0:T(8,128)(2,1)S(1)} %bitcast.2), channel_id=1, source_target_pairs={{0,1},{1,0},{2,3},{3,2},{4,5},{5,4},{6,7},{7,6},{8,9},{9,8},{10,11... | collective-permute-start | bytes 1572872 | tf_op jit(solution)/shard_map/ppermute | solution.py:202
  64.7 1.5 %collective-permute-done.4.other = bf16[512,512]{1,0:T(8,128)(2,1)S(1)} collective-permute-done((bf16[512,512]{1,0:T(8,128)(2,1)S(1)}, bf16[512,512]{1,0:T(8,128)(2,1)S(1)}, u32[]{:S(2)}, u32[]{:S(2)}) %collective-permute-start.4) | collective-permute-done | bytes 524320 | tf_op jit(solution)/shard_map/ppermute | solution.py:202
  66.2 2.8 %shard_map.72 = (bf16[1536,128]{1,0:T(8,128)(2,1)S(1)}, bf16[1536,128]{1,0:T(8,128)(2,1)}, bf16[1536,128]{1,0:T(8,128)(2,1)}, bf16[1536,128]{1,0:T(8,128)(2,1)S(1)}) custom-call(bf16[512,512]{1,0:T(8,128)(2,1)S(1)} %bitcast.3, bf16[512,512]{1,0:T(8,128)(2,1)S(1)} %collective-permute-done.4.other, bf16[1536,128]{1,0:T(8,128)(2,1)S(1)} %get-tuple-element.19.r0, ...), custom_call_target="tpu_custom_call" | custom-call | flops 1073741824 | bytes 4194304 | tf_op jit(solution)/shard_map/pallas_call | solution.py:206
  69.0 4.6 %collective-permute-start.5 = (bf16[1536,128]{1,0:T(8,128)(2,1)}, bf16[1536,128]{1,0:T(8,128)(2,1)S(1)}, u32[]{:S(2)}, u32[]{:S(2)}) collective-permute-start(bf16[1536,128]{1,0:T(8,128)(2,1)} %get-tuple-element.29), channel_id=1, source_target_pairs={{0,512},{512,0},{1,513},{513,1},{2,514},{514,2},{3,515},{515,3},{4... | collective-permute-start | bytes 1179656 | tf_op jit(solution)/shard_map/ppermute | solution.py:180
  73.6 2.2 %collective-permute-start.6 = (bf16[1536,128]{1,0:T(8,128)(2,1)}, bf16[1536,128]{1,0:T(8,128)(2,1)S(1)}, u32[]{:S(2)}, u32[]{:S(2)}) collective-permute-start(bf16[1536,128]{1,0:T(8,128)(2,1)} %get-tuple-element.30), channel_id=1, source_target_pairs={{0,32},{32,0},{1,33},{33,1},{2,34},{34,2},{3,35},{35,3},{4,36},{36... | collective-permute-start | bytes 1179656 | tf_op jit(solution)/shard_map/ppermute | solution.py:179
  75.9 2.5 %collective-permute-start.7 = (bf16[1536,128]{1,0:T(8,128)(2,1)S(1)}, bf16[1536,128]{1,0:T(8,128)(2,1)S(1)}, u32[]{:S(2)}, u32[]{:S(2)}) collective-permute-start(bf16[1536,128]{1,0:T(8,128)(2,1)S(1)} %get-tuple-element.31), channel_id=1, source_target_pairs={{0,544},{32,512},{512,32},{544,0},{1,545},{33,513},{513,33},{545,1... | collective-permute-start | bytes 1179656 | tf_op jit(solution)/shard_map/ppermute | solution.py:181
  78.4 0.0 all-to-all-done.2.blocks
  78.4 0.1 shard_map.71
  78.4 22.6 %all_to_all.20 = bf16[16,4,512]{2,1,0:T(4,128)(2,1)S(1)} all-to-all(bf16[16,4,512]{2,1,0:T(4,128)(2,1)S(1)} %shard_map.71), channel_id=1, replica_groups=mesh['xh'=2,'y'=8,'xl'=2,'z'=16,'c'=2] {'z'}, dimensions={0} | all-to-all | bytes 131072 | tf_op jit(solution)/shard_map/all_to_all | solution.py:169
  101.0 0.6 convert_reduce_fusion
  101.7 0.0 collective-permute-done.5.f2
  101.7 0.0 collective-permute-done.6.f1
  101.7 0.0 collective-permute-done.7.f3
  101.7 1.5 %shard_map.73 = (bf16[128,512]{1,0:T(8,128)(2,1)}, bf16[128,4096]{1,0:T(8,128)(2,1)}) custom-call(bf16[1536,128]{1,0:T(8,128)(2,1)S(1)} %get-tuple-element.28.f0, bf16[1536,128]{1,0:T(8,128)(2,1)S(1)} %collective-permute-done.5.f2, bf16[1536,128]{1,0:T(8,128)(2,1)S(1)} %collective-permute-done.6.f1, bf16[1536,128]{1,0:T(8,128)(2,1)S(1)} %collective-permute-done.7.f3), custom_call_target="tpu_custom_call" | custom-call | flops 268435456 | bytes 3145728 | tf_op jit(solution)/shard_map/pallas_call | solution.py:214
  (1 shorter events, 0.0 us)
Async XLA Ops:
  0.6 20.9 %copy-start.1 = (bf16[128,512]{1,0:T(8,128)(2,1)S(1)}, bf16[128,512]{1,0:T(8,128)(2,1)}, u32[]{:S(2)}) copy-start(bf16[128,512]{1,0:T(8,128)(2,1)} %grad_ref.1) | copy-start | bytes 393220
  2.1 31.0 %all-to-all-start = ((bf16[16,4,512]{2,1,0:T(4,128)(2,1)}), bf16[16,4,512]{2,1,0:T(4,128)(2,1)S(1)}, u32[]{:S(2)}, u32[]{:S(2)}) async-start(bf16[16,4,512]{2,1,0:T(4,128)(2,1)} %shard_map.67), calls=%async_computation | async-start | bytes 131072 | tf_op jit(solution)/shard_map/all_to_all | solution.py:169
  21.6 1.2 %copy-start = (bf16[128,4096]{1,0:T(8,128)(2,1)S(1)}, bf16[128,4096]{1,0:T(8,128)(2,1)}, u32[]{:S(2)}) copy-start(bf16[128,4096]{1,0:T(8,128)(2,1)} %tok_ref.1) | copy-start | bytes 3145732
  23.7 17.1 %collective-permute-start = (bf16[1536,128]{1,0:T(8,128)(2,1)S(1)}, bf16[1536,128]{1,0:T(8,128)(2,1)S(1)}, u32[]{:S(2)}, u32[]{:S(2)}) collective-permute-start(bf16[1536,128]{1,0:T(8,128)(2,1)S(1)} %get-tuple-element.20), channel_id=1, source_target_pairs={{0,512},{512,0},{1,513},{513,1},{2,514},{514,2},{3,515},{515,3},{4... | collective-permute-start | bytes 1179656 | tf_op jit(solution)/shard_map/ppermute | solution.py:180
  28.4 17.0 %collective-permute-start.1 = (bf16[1536,128]{1,0:T(8,128)(2,1)S(1)}, bf16[1536,128]{1,0:T(8,128)(2,1)S(1)}, u32[]{:S(2)}, u32[]{:S(2)}) collective-permute-start(bf16[1536,128]{1,0:T(8,128)(2,1)S(1)} %get-tuple-element.21), channel_id=1, source_target_pairs={{0,32},{32,0},{1,33},{33,1},{2,34},{34,2},{3,35},{35,3},{4,36},{36... | collective-permute-start | bytes 1179656 | tf_op jit(solution)/shard_map/ppermute | solution.py:179
  30.6 15.2 %collective-permute-start.2 = (bf16[1536,128]{1,0:T(8,128)(2,1)S(1)}, bf16[1536,128]{1,0:T(8,128)(2,1)S(1)}, u32[]{:S(2)}, u32[]{:S(2)}) collective-permute-start(bf16[1536,128]{1,0:T(8,128)(2,1)S(1)} %get-tuple-element.22), channel_id=1, source_target_pairs={{0,544},{32,512},{512,32},{544,0},{1,545},{33,513},{513,33},{545,1... | collective-permute-start | bytes 1179656 | tf_op jit(solution)/shard_map/ppermute | solution.py:181
  34.0 21.9 %all-to-all-start.1 = ((bf16[8,64,512]{2,1,0:T(8,128)(2,1)}), bf16[8,64,512]{2,1,0:T(8,128)(2,1)S(1)}, u32[]{:S(2)}, u32[]{:S(2)}) async-start(bf16[8,64,512]{2,1,0:T(8,128)(2,1)} %broadcast_in_dim.8), calls=%async_computation.1 | async-start | bytes 1048576 | tf_op jit(solution)/shard_map/all_to_all | solution.py:169
  46.6 4.8 %collective-permute-start.3 = (bf16[512,512]{1,0:T(8,128)(2,1)S(1)}, bf16[512,512]{1,0:T(8,128)(2,1)S(1)}, u32[]{:S(2)}, u32[]{:S(2)}) collective-permute-start(bf16[512,512]{1,0:T(8,128)(2,1)S(1)} %get-tuple-element.24), channel_id=1, source_target_pairs={{0,1},{1,0},{2,3},{3,2},{4,5},{5,4},{6,7},{7,6},{8,9},{9,8},{10,11... | collective-permute-start | bytes 1572872 | tf_op jit(solution)/shard_map/ppermute | solution.py:198
  55.9 22.5 %all-to-all-start.2 = ((bf16[8,64,512]{2,1,0:T(8,128)(2,1)}), bf16[8,64,512]{2,1,0:T(8,128)(2,1)S(1)}, u32[]{:S(2)}, u32[]{:S(2)}) async-start(bf16[8,64,512]{2,1,0:T(8,128)(2,1)} %bitcast), calls=%async_computation.2 | async-start | bytes 1048576 | tf_op jit(solution)/shard_map/all_to_all | solution.py:169
  59.5 6.7 %collective-permute-start.4 = (bf16[512,512]{1,0:T(8,128)(2,1)S(1)}, bf16[512,512]{1,0:T(8,128)(2,1)S(1)}, u32[]{:S(2)}, u32[]{:S(2)}) collective-permute-start(bf16[512,512]{1,0:T(8,128)(2,1)S(1)} %bitcast.2), channel_id=1, source_target_pairs={{0,1},{1,0},{2,3},{3,2},{4,5},{5,4},{6,7},{7,6},{8,9},{9,8},{10,11... | collective-permute-start | bytes 1572872 | tf_op jit(solution)/shard_map/ppermute | solution.py:202
  69.0 32.7 %collective-permute-start.5 = (bf16[1536,128]{1,0:T(8,128)(2,1)}, bf16[1536,128]{1,0:T(8,128)(2,1)S(1)}, u32[]{:S(2)}, u32[]{:S(2)}) collective-permute-start(bf16[1536,128]{1,0:T(8,128)(2,1)} %get-tuple-element.29), channel_id=1, source_target_pairs={{0,512},{512,0},{1,513},{513,1},{2,514},{514,2},{3,515},{515,3},{4... | collective-permute-start | bytes 1179656 | tf_op jit(solution)/shard_map/ppermute | solution.py:180
  73.6 28.0 %collective-permute-start.6 = (bf16[1536,128]{1,0:T(8,128)(2,1)}, bf16[1536,128]{1,0:T(8,128)(2,1)S(1)}, u32[]{:S(2)}, u32[]{:S(2)}) collective-permute-start(bf16[1536,128]{1,0:T(8,128)(2,1)} %get-tuple-element.30), channel_id=1, source_target_pairs={{0,32},{32,0},{1,33},{33,1},{2,34},{34,2},{3,35},{35,3},{4,36},{36... | collective-permute-start | bytes 1179656 | tf_op jit(solution)/shard_map/ppermute | solution.py:179
  75.9 25.8 %collective-permute-start.7 = (bf16[1536,128]{1,0:T(8,128)(2,1)S(1)}, bf16[1536,128]{1,0:T(8,128)(2,1)S(1)}, u32[]{:S(2)}, u32[]{:S(2)}) collective-permute-start(bf16[1536,128]{1,0:T(8,128)(2,1)S(1)} %get-tuple-element.31), channel_id=1, source_target_pairs={{0,544},{32,512},{512,32},{544,0},{1,545},{33,513},{513,33},{545,1... | collective-permute-start | bytes 1179656 | tf_op jit(solution)/shard_map/ppermute | solution.py:181

commit v8 on v7

--- a/solution.py
+++ b/solution.py
@@ -75,7 +75,8 @@
             out[pl.ds(SLICE + b * 128, 128), :] = piece
 
 
-def scale_rows(codes_ref, scales_ref, copies, codes, scales, sems):
+def scale_rows(codes_ref, scales_ref, tok_ref, copies, codes, scales, sems):
+    del tok_ref
     loads = [
         pltpu.make_async_copy(codes_ref, codes, sems.at[0]),
         pltpu.make_async_copy(scales_ref, scales, sems.at[1]),
@@ -129,8 +130,9 @@
         out[SLICE:, :] = keys[:, k * TOK : (k + 1) * TOK]
 
 
-def finish(f0, f2, f1, f3, keys, input_grad):
+def finish(f0, f2, f1, f3, sums, keys, input_grad, weight_grad):
     xh, xl = lax.axis_index("xh"), lax.axis_index("xl")
+    weight_grad[...] = jnp.sum(sums[...].astype(F32), axis=0)
     refs = (f0, f1, f2, f3)
     same, split = eye(), x_split(xh)
     for b in range(KV // 128):
@@ -152,12 +154,15 @@
             input_grad[:, pl.ds(pl.multiple_of(col + z * 128, 128), 128)] = block
 
 
-def kernel(body, outs, flops, moved, scratch=(), in_hbm=0, vmem=24):
+def kernel(body, outs, flops, moved, scratch=(), in_hbm=0, vmem=24, last=BF16):
     pinned = [pl.BlockSpec(memory_space=pl.ANY)] * in_hbm
     return pl.pallas_call(
         body,
         **({"in_specs": pinned} if in_hbm else {}),
-        out_shape=[jax.ShapeDtypeStruct(s, BF16) for s in outs],
+        out_shape=[
+            *(jax.ShapeDtypeStruct(s, BF16) for s in outs[:-1]),
+            jax.ShapeDtypeStruct(outs[-1], last),
+        ],
         scratch_shapes=list(scratch),
         compiler_params=pltpu.CompilerParams(vmem_limit_bytes=vmem << 20),
         cost_estimate=pl.CostEstimate(flops=flops, bytes_accessed=moved, transcendentals=0),
@@ -188,7 +193,7 @@
         pltpu.VMEM((ROWS, KV // BLOCK), BF16),
         pltpu.SemaphoreType.DMA((2,)),
     ]
-    (copies,) = kernel(scale_rows, [(NZ, ROWS, KV)], 1 << 12, 1 << 17, room, 2, 60)(codes, scales)
+    (copies,) = kernel(scale_rows, [(NZ, ROWS, KV)], 1 << 12, 1 << 17, room, 3, 60)(codes, scales, tokens)
     blocks = kernel(prepare, [(PAY, TOK)] * 4, 1 << 28, 3 << 20)(tokens, key_grad)
     work = to_members(blocks)
     by_z = exchange(copies, "z")
@@ -204,15 +209,14 @@
     (total,) = kernel(sum_over_y, [(NZ, ROWS, KV)], 1 << 18, 1 << 20)(total)
     total = exchange(total, "z")
     results = kernel(
-        apply_weight, [(PAY, TOK)] * 4, 1 << 30, 4 << 20, [pltpu.VMEM((SLICE, KV), BF16)]
+        apply_weight, [(PAY, TOK)] * 4, 1 << 33, 4 << 20, [pltpu.VMEM((SLICE, KV), BF16)]
     )(own, other, *work)
     results = to_members(results)
     total, mine = lax.optimization_barrier((total, results[0]))
     results = (mine, *results[1:])
-    weight_grad = jnp.sum(total.astype(F32), axis=0)
-    d_in = 4 * SLICE
-    keys, input_grad = kernel(finish, [(TOK, KV), (TOK, d_in)], 1 << 28, 3 << 20)(
-        *far_first(results)
+    shapes = [(TOK, KV), (TOK, 4 * SLICE), (ROWS, KV)]
+    keys, input_grad, weight_grad = kernel(finish, shapes, 1 << 28, 3 << 20, last=F32)(
+        *far_first(results), total
     )
     return keys, input_grad, weight_grad
 

time: 105 us -> 109 us (1.038)
  waiting for transfers between devices: 11.3 us -> 16 us
    all_to_all x3, waiting for transfers between devices: 3.22 us -> 10.5 us  [exchange(): return lax.all_to_all(blocks, axis, split_axis=0, concat_axis=0, tiled=True)]
    ppermute x1, waiting for transfers between devices: 1.51 us -> 0.01 us  [shards(): other = lax.ppermute(own, 'c', SWAP)]
    unnamed x4, local copies, waits for them, and re-layouts: 1.22 us -> 0.01 us
    ppermute x2, waiting for transfers between devices: 4.54 us -> 3.41 us  [to_members(): lax.ppermute(blocks[1], 'xl', SWAP)]
  transfers between devices with their start and end apart: 11 -> 11, of which waited for: 5 -> 6; matrix products, arithmetic and copies ran while one was open for 1% -> 2% of each run, Pallas kernels for 6% -> 6%
where the time goes in v8:
time: 109 us; the launch traced here: 108 us
  starting transfers between devices  57 us (52%)
  blocking collectives  22.2 us (20%)
  waiting for transfers between devices  16 us (15%)
  Pallas kernels  9.84 us (9%)
  local copies, waits for them, and re-layouts  1.71 us (2%)
    all_to_all x3, starting transfers between devices, exchange(): return lax.all_to_all(blocks, axis, split_axis=0, concat_axis=0, tiled=True)  29.9 us
    all_to_all x1, blocking collectives, exchange(): return lax.all_to_all(blocks, axis, split_axis=0, concat_axis=0, tiled=True)  22.2 us
    all_to_all x3, waiting for transfers between devices, exchange(): return lax.all_to_all(blocks, axis, split_axis=0, concat_axis=0, tiled=True)  10.5 us
    ppermute x2, starting transfers between devices, to_members(): lax.ppermute(blocks[2], 'xh', SWAP)  9.28 us
    ppermute x1, starting transfers between devices, shards(): other = lax.ppermute(own, 'c', SWAP)  5.25 us
    ppermute x2, starting transfers between devices, to_members(): lax.ppermute(blocks[3], ('xh', 'xl'), [(0, 3), (1, 2), (2, 1), (3, 0)])  4.93 us
    ppermute x2, starting transfers between devices, to_members(): lax.ppermute(blocks[1], 'xl', SWAP)  4.44 us
    ppermute x2, waiting for transfers between devices, to_members(): lax.ppermute(blocks[1], 'xl', SWAP)  3.41 us
  transfers between devices with their start and end apart: 11, of which 6 were waited for; matrix products, arithmetic and copies ran while one was open for 2% of the time, Pallas kernels for 6%

profile of v8, /device:TPU:1, one launch (start us, length us, event | category | flops | bytes accessed | tf_op | source)
XLA Modules:
  0.0 107.6 jit_solution(7259214692281702162)
XLA Ops:
  0.6 0.0 copy-start
  0.6 1.5 %shard_map.67 = bf16[16,4,512]{2,1,0:T(4,128)(2,1)} custom-call(bf16[4,512]{1,0:T(4,128)(2,1)} %codes_ref.1, bf16[4,4]{1,0:T(4,128)(2,1)} %scales_ref.1, bf16[128,4096]{1,0:T(8,128)(2,1)} %tok_ref.3), custom_call_target="tpu_custom_call" | custom-call | flops 4096 | bytes 131072 | tf_op jit(solution)/shard_map/pallas_call | solution.py:196
  2.2 0.0 copy-start.1
  2.2 19.6 %all-to-all-start = ((bf16[16,4,512]{2,1,0:T(4,128)(2,1)}), bf16[16,4,512]{2,1,0:T(4,128)(2,1)}, u32[]{:S(2)}, u32[]{:S(2)}) async-start(bf16[16,4,512]{2,1,0:T(4,128)(2,1)} %shard_map.67), calls=%async_computation | async-start | bytes 131072 | tf_op jit(solution)/shard_map/all_to_all | solution.py:174
  21.8 0.0 copy-done
  21.8 0.0 copy-done.1
  21.8 1.7 %shard_map.68 = (bf16[1536,128]{1,0:T(8,128)(2,1)S(1)}, bf16[1536,128]{1,0:T(8,128)(2,1)S(1)}, bf16[1536,128]{1,0:T(8,128)(2,1)}, bf16[1536,128]{1,0:T(8,128)(2,1)S(1)}) custom-call(bf16[128,4096]{1,0:T(8,128)(2,1)S(1)} %copy-done, bf16[128,512]{1,0:T(8,128)(2,1)S(1)} %copy-done.1), custom_call_target="tpu_custom_call" | custom-call | flops 268435456 | bytes 3145728 | tf_op jit(solution)/shard_map/pallas_call | solution.py:197
  23.5 4.6 %collective-permute-start = (bf16[1536,128]{1,0:T(8,128)(2,1)}, bf16[1536,128]{1,0:T(8,128)(2,1)S(1)}, u32[]{:S(2)}, u32[]{:S(2)}) collective-permute-start(bf16[1536,128]{1,0:T(8,128)(2,1)} %get-tuple-element.18), channel_id=1, source_target_pairs={{0,512},{512,0},{1,513},{513,1},{2,514},{514,2},{3,515},{515,3},{4... | collective-permute-start | bytes 1179656 | tf_op jit(solution)/shard_map/ppermute | solution.py:185
  28.2 2.2 %collective-permute-start.1 = (bf16[1536,128]{1,0:T(8,128)(2,1)S(1)}, bf16[1536,128]{1,0:T(8,128)(2,1)S(1)}, u32[]{:S(2)}, u32[]{:S(2)}) collective-permute-start(bf16[1536,128]{1,0:T(8,128)(2,1)S(1)} %get-tuple-element.19), channel_id=1, source_target_pairs={{0,32},{32,0},{1,33},{33,1},{2,34},{34,2},{3,35},{35,3},{4,36},{36... | collective-permute-start | bytes 1179656 | tf_op jit(solution)/shard_map/ppermute | solution.py:184
  30.4 2.5 %collective-permute-start.2 = (bf16[1536,128]{1,0:T(8,128)(2,1)S(1)}, bf16[1536,128]{1,0:T(8,128)(2,1)S(1)}, u32[]{:S(2)}, u32[]{:S(2)}) collective-permute-start(bf16[1536,128]{1,0:T(8,128)(2,1)S(1)} %get-tuple-element.20), channel_id=1, source_target_pairs={{0,544},{32,512},{512,32},{544,0},{1,545},{33,513},{513,33},{545,1... | collective-permute-start | bytes 1179656 | tf_op jit(solution)/shard_map/ppermute | solution.py:186
  32.9 0.5 all-to-all-done
  33.4 0.9 broadcast_in_dim.7
  34.3 0.8 broadcast_in_dim.8
  35.1 6.8 %all-to-all-start.1 = ((bf16[8,64,512]{2,1,0:T(8,128)(2,1)}), bf16[8,64,512]{2,1,0:T(8,128)(2,1)S(1)}, u32[]{:S(2)}, u32[]{:S(2)}) async-start(bf16[8,64,512]{2,1,0:T(8,128)(2,1)} %broadcast_in_dim.8), calls=%async_computation.1 | async-start | bytes 1048576 | tf_op jit(solution)/shard_map/all_to_all | solution.py:174
  41.9 0.0 collective-permute-done.r2
  41.9 3.4 %collective-permute-done.1.r1 = bf16[1536,128]{1,0:T(8,128)(2,1)S(1)} collective-permute-done((bf16[1536,128]{1,0:T(8,128)(2,1)S(1)}, bf16[1536,128]{1,0:T(8,128)(2,1)S(1)}, u32[]{:S(2)}, u32[]{:S(2)}) %collective-permute-start.1) | collective-permute-done | bytes 393248 | tf_op jit(solution)/shard_map/ppermute | solution.py:184
  45.3 0.6 collective-permute-done.2.r3
  45.9 0.7 shard_map.69
  46.7 3.2 %collective-permute-start.3 = (bf16[512,512]{1,0:T(8,128)(2,1)S(1)}, bf16[512,512]{1,0:T(8,128)(2,1)S(1)}, u32[]{:S(2)}, u32[]{:S(2)}) collective-permute-start(bf16[512,512]{1,0:T(8,128)(2,1)S(1)} %get-tuple-element.22), channel_id=1, source_target_pairs={{0,1},{1,0},{2,3},{3,2},{4,5},{5,4},{6,7},{7,6},{8,9},{9,8},{10,11... | collective-permute-start | bytes 1572872 | tf_op jit(solution)/shard_map/ppermute | solution.py:203
  49.9 1.5 %collective-permute-done.3.b = bf16[512,512]{1,0:T(8,128)(2,1)S(1)} collective-permute-done((bf16[512,512]{1,0:T(8,128)(2,1)S(1)}, bf16[512,512]{1,0:T(8,128)(2,1)S(1)}, u32[]{:S(2)}, u32[]{:S(2)}) %collective-permute-start.3) | collective-permute-done | bytes 524320 | tf_op jit(solution)/shard_map/ppermute | solution.py:203
  51.4 1.3 %shard_map.70 = bf16[512,512]{1,0:T(8,128)(2,1)} custom-call(bf16[512,512]{1,0:T(8,128)(2,1)S(1)} %get-tuple-element.21.a, bf16[512,512]{1,0:T(8,128)(2,1)S(1)} %collective-permute-done.3.b), custom_call_target="tpu_custom_call" | custom-call | flops 268435456 | bytes 1572864 | tf_op jit(solution)/shard_map/pallas_call | solution.py:204
  52.7 4.3 %all-to-all-done.1 = bf16[8,64,512]{2,1,0:T(8,128)(2,1)S(1)} async-done(((bf16[8,64,512]{2,1,0:T(8,128)(2,1)}), bf16[8,64,512]{2,1,0:T(8,128)(2,1)S(1)}, u32[]{:S(2)}, u32[]{:S(2)}) %all-to-all-start.1) | async-done | bytes 524320 | tf_op jit(solution)/shard_map/all_to_all | solution.py:174
  57.0 5.2 %collective-permute-start.4 = (bf16[512,512]{1,0:T(8,128)(2,1)S(1)}, bf16[512,512]{1,0:T(8,128)(2,1)S(1)}, u32[]{:S(2)}, u32[]{:S(2)}) collective-permute-start(bf16[512,512]{1,0:T(8,128)(2,1)S(1)} %bitcast.2), channel_id=1, source_target_pairs={{0,1},{1,0},{2,3},{3,2},{4,5},{5,4},{6,7},{7,6},{8,9},{9,8},{10,11... | collective-permute-start | bytes 1572872 | tf_op jit(solution)/shard_map/ppermute | solution.py:207
  62.3 3.5 %all-to-all-start.2 = ((bf16[8,64,512]{2,1,0:T(8,128)(2,1)}), bf16[8,64,512]{2,1,0:T(8,128)(2,1)S(1)}, u32[]{:S(2)}, u32[]{:S(2)}) async-start(bf16[8,64,512]{2,1,0:T(8,128)(2,1)} %bitcast), calls=%async_computation.2 | async-start | bytes 1048576 | tf_op jit(solution)/shard_map/all_to_all | solution.py:174
  65.8 0.0 collective-permute-done.4.other
  65.8 3.0 %shard_map.72 = (bf16[1536,128]{1,0:T(8,128)(2,1)S(1)}, bf16[1536,128]{1,0:T(8,128)(2,1)}, bf16[1536,128]{1,0:T(8,128)(2,1)}, bf16[1536,128]{1,0:T(8,128)(2,1)}) custom-call(bf16[512,512]{1,0:T(8,128)(2,1)S(1)} %bitcast.3, bf16[512,512]{1,0:T(8,128)(2,1)S(1)} %collective-permute-done.4.other, bf16[1536,128]{1,0:T(8,128)(2,1)S(1)} %get-tuple-element.17.r0, ...), custom_call_target="tpu_custom_call" | custom-call | flops 8589934592 | bytes 4194304 | tf_op jit(solution)/shard_map/pallas_call | solution.py:211
  68.8 4.6 %collective-permute-start.5 = (bf16[1536,128]{1,0:T(8,128)(2,1)}, bf16[1536,128]{1,0:T(8,128)(2,1)S(1)}, u32[]{:S(2)}, u32[]{:S(2)}) collective-permute-start(bf16[1536,128]{1,0:T(8,128)(2,1)} %get-tuple-element.27), channel_id=1, source_target_pairs={{0,512},{512,0},{1,513},{513,1},{2,514},{514,2},{3,515},{515,3},{4... | collective-permute-start | bytes 1179656 | tf_op jit(solution)/shard_map/ppermute | solution.py:185
  73.4 2.2 %collective-permute-start.6 = (bf16[1536,128]{1,0:T(8,128)(2,1)}, bf16[1536,128]{1,0:T(8,128)(2,1)S(1)}, u32[]{:S(2)}, u32[]{:S(2)}) collective-permute-start(bf16[1536,128]{1,0:T(8,128)(2,1)} %get-tuple-element.28), channel_id=1, source_target_pairs={{0,32},{32,0},{1,33},{33,1},{2,34},{34,2},{3,35},{35,3},{4,36},{36... | collective-permute-start | bytes 1179656 | tf_op jit(solution)/shard_map/ppermute | solution.py:184
  75.7 2.5 %collective-permute-start.7 = (bf16[1536,128]{1,0:T(8,128)(2,1)}, bf16[1536,128]{1,0:T(8,128)(2,1)S(1)}, u32[]{:S(2)}, u32[]{:S(2)}) collective-permute-start(bf16[1536,128]{1,0:T(8,128)(2,1)} %get-tuple-element.29), channel_id=1, source_target_pairs={{0,544},{32,512},{512,32},{544,0},{1,545},{33,513},{513,33},{545,1... | collective-permute-start | bytes 1179656 | tf_op jit(solution)/shard_map/ppermute | solution.py:186
  78.1 5.6 %all-to-all-done.2.blocks = bf16[8,64,512]{2,1,0:T(8,128)(2,1)S(1)} async-done(((bf16[8,64,512]{2,1,0:T(8,128)(2,1)}), bf16[8,64,512]{2,1,0:T(8,128)(2,1)S(1)}, u32[]{:S(2)}, u32[]{:S(2)}) %all-to-all-start.2) | async-done | bytes 524320 | tf_op jit(solution)/shard_map/all_to_all | solution.py:174
  83.8 0.1 shard_map.71
  83.9 22.2 %all_to_all.20.sums = bf16[16,4,512]{2,1,0:T(4,128)(2,1)S(1)} all-to-all(bf16[16,4,512]{2,1,0:T(4,128)(2,1)S(1)} %shard_map.71), channel_id=1, replica_groups=mesh['xh'=2,'y'=8,'xl'=2,'z'=16,'c'=2] {'z'}, dimensions={0} | all-to-all | bytes 131072 | tf_op jit(solution)/shard_map/all_to_all | solution.py:174
  106.1 0.0 collective-permute-done.5.f2
  106.1 0.0 collective-permute-done.6.f1
  106.1 0.0 collective-permute-done.7.f3
  106.1 1.5 %shard_map.73 = (bf16[128,512]{1,0:T(8,128)(2,1)}, bf16[128,4096]{1,0:T(8,128)(2,1)}, f32[4,512]{1,0:T(4,128)}) custom-call(bf16[1536,128]{1,0:T(8,128)(2,1)S(1)} %get-tuple-element.26.f0, bf16[1536,128]{1,0:T(8,128)(2,1)S(1)} %collective-permute-done.5.f2, bf16[1536,128]{1,0:T(8,128)(2,1)S(1)} %collective-permute-done.6.f1, ...), custom_call_target="tpu_custom_call" | custom-call | flops 268435456 | bytes 3145728 | tf_op jit(solution)/shard_map/pallas_call | solution.py:218
Async XLA Ops:
  0.6 21.2 %copy-start = (bf16[128,4096]{1,0:T(8,128)(2,1)S(1)}, bf16[128,4096]{1,0:T(8,128)(2,1)}, u32[]{:S(2)}) copy-start(bf16[128,4096]{1,0:T(8,128)(2,1)} %tok_ref.3) | copy-start | bytes 3145732
  2.2 19.6 %copy-start.1 = (bf16[128,512]{1,0:T(8,128)(2,1)S(1)}, bf16[128,512]{1,0:T(8,128)(2,1)}, u32[]{:S(2)}) copy-start(bf16[128,512]{1,0:T(8,128)(2,1)} %grad_ref.1) | copy-start | bytes 393220
  2.2 31.2 %all-to-all-start = ((bf16[16,4,512]{2,1,0:T(4,128)(2,1)}), bf16[16,4,512]{2,1,0:T(4,128)(2,1)}, u32[]{:S(2)}, u32[]{:S(2)}) async-start(bf16[16,4,512]{2,1,0:T(4,128)(2,1)} %shard_map.67), calls=%async_computation | async-start | bytes 131072 | tf_op jit(solution)/shard_map/all_to_all | solution.py:174
  23.5 18.4 %collective-permute-start = (bf16[1536,128]{1,0:T(8,128)(2,1)}, bf16[1536,128]{1,0:T(8,128)(2,1)S(1)}, u32[]{:S(2)}, u32[]{:S(2)}) collective-permute-start(bf16[1536,128]{1,0:T(8,128)(2,1)} %get-tuple-element.18), channel_id=1, source_target_pairs={{0,512},{512,0},{1,513},{513,1},{2,514},{514,2},{3,515},{515,3},{4... | collective-permute-start | bytes 1179656 | tf_op jit(solution)/shard_map/ppermute | solution.py:185
  28.2 17.2 %collective-permute-start.1 = (bf16[1536,128]{1,0:T(8,128)(2,1)S(1)}, bf16[1536,128]{1,0:T(8,128)(2,1)S(1)}, u32[]{:S(2)}, u32[]{:S(2)}) collective-permute-start(bf16[1536,128]{1,0:T(8,128)(2,1)S(1)} %get-tuple-element.19), channel_id=1, source_target_pairs={{0,32},{32,0},{1,33},{33,1},{2,34},{34,2},{3,35},{35,3},{4,36},{36... | collective-permute-start | bytes 1179656 | tf_op jit(solution)/shard_map/ppermute | solution.py:184
  30.4 15.5 %collective-permute-start.2 = (bf16[1536,128]{1,0:T(8,128)(2,1)S(1)}, bf16[1536,128]{1,0:T(8,128)(2,1)S(1)}, u32[]{:S(2)}, u32[]{:S(2)}) collective-permute-start(bf16[1536,128]{1,0:T(8,128)(2,1)S(1)} %get-tuple-element.20), channel_id=1, source_target_pairs={{0,544},{32,512},{512,32},{544,0},{1,545},{33,513},{513,33},{545,1... | collective-permute-start | bytes 1179656 | tf_op jit(solution)/shard_map/ppermute | solution.py:186
  35.1 21.9 %all-to-all-start.1 = ((bf16[8,64,512]{2,1,0:T(8,128)(2,1)}), bf16[8,64,512]{2,1,0:T(8,128)(2,1)S(1)}, u32[]{:S(2)}, u32[]{:S(2)}) async-start(bf16[8,64,512]{2,1,0:T(8,128)(2,1)} %broadcast_in_dim.8), calls=%async_computation.1 | async-start | bytes 1048576 | tf_op jit(solution)/shard_map/all_to_all | solution.py:174
  46.7 4.7 %collective-permute-start.3 = (bf16[512,512]{1,0:T(8,128)(2,1)S(1)}, bf16[512,512]{1,0:T(8,128)(2,1)S(1)}, u32[]{:S(2)}, u32[]{:S(2)}) collective-permute-start(bf16[512,512]{1,0:T(8,128)(2,1)S(1)} %get-tuple-element.22), channel_id=1, source_target_pairs={{0,1},{1,0},{2,3},{3,2},{4,5},{5,4},{6,7},{7,6},{8,9},{9,8},{10,11... | collective-permute-start | bytes 1572872 | tf_op jit(solution)/shard_map/ppermute | solution.py:203
  57.0 8.8 %collective-permute-start.4 = (bf16[512,512]{1,0:T(8,128)(2,1)S(1)}, bf16[512,512]{1,0:T(8,128)(2,1)S(1)}, u32[]{:S(2)}, u32[]{:S(2)}) collective-permute-start(bf16[512,512]{1,0:T(8,128)(2,1)S(1)} %bitcast.2), channel_id=1, source_target_pairs={{0,1},{1,0},{2,3},{3,2},{4,5},{5,4},{6,7},{7,6},{8,9},{9,8},{10,11... | collective-permute-start | bytes 1572872 | tf_op jit(solution)/shard_map/ppermute | solution.py:207
  62.3 21.5 %all-to-all-start.2 = ((bf16[8,64,512]{2,1,0:T(8,128)(2,1)}), bf16[8,64,512]{2,1,0:T(8,128)(2,1)S(1)}, u32[]{:S(2)}, u32[]{:S(2)}) async-start(bf16[8,64,512]{2,1,0:T(8,128)(2,1)} %bitcast), calls=%async_computation.2 | async-start | bytes 1048576 | tf_op jit(solution)/shard_map/all_to_all | solution.py:174
  68.8 37.3 %collective-permute-start.5 = (bf16[1536,128]{1,0:T(8,128)(2,1)}, bf16[1536,128]{1,0:T(8,128)(2,1)S(1)}, u32[]{:S(2)}, u32[]{:S(2)}) collective-permute-start(bf16[1536,128]{1,0:T(8,128)(2,1)} %get-tuple-element.27), channel_id=1, source_target_pairs={{0,512},{512,0},{1,513},{513,1},{2,514},{514,2},{3,515},{515,3},{4... | collective-permute-start | bytes 1179656 | tf_op jit(solution)/shard_map/ppermute | solution.py:185
  73.4 32.7 %collective-permute-start.6 = (bf16[1536,128]{1,0:T(8,128)(2,1)}, bf16[1536,128]{1,0:T(8,128)(2,1)S(1)}, u32[]{:S(2)}, u32[]{:S(2)}) collective-permute-start(bf16[1536,128]{1,0:T(8,128)(2,1)} %get-tuple-element.28), channel_id=1, source_target_pairs={{0,32},{32,0},{1,33},{33,1},{2,34},{34,2},{3,35},{35,3},{4,36},{36... | collective-permute-start | bytes 1179656 | tf_op jit(solution)/shard_map/ppermute | solution.py:184
  75.7 30.4 %collective-permute-start.7 = (bf16[1536,128]{1,0:T(8,128)(2,1)}, bf16[1536,128]{1,0:T(8,128)(2,1)S(1)}, u32[]{:S(2)}, u32[]{:S(2)}) collective-permute-start(bf16[1536,128]{1,0:T(8,128)(2,1)} %get-tuple-element.29), channel_id=1, source_target_pairs={{0,544},{32,512},{512,32},{544,0},{1,545},{33,513},{513,33},{545,1... | collective-permute-start | bytes 1179656 | tf_op jit(solution)/shard_map/ppermute | solution.py:186

commit v9 on v8

--- a/solution.py
+++ b/solution.py
@@ -89,6 +89,14 @@
         at = slice(b * BLOCK, (b + 1) * BLOCK)
         scaled = codes[:, at].astype(F32) * scales[:, b : b + 1].astype(F32)
         copies[:, :, at] = jnp.broadcast_to(scaled.astype(BF16)[None], (NZ, ROWS, BLOCK))
+
+
+def spread(blocks, copies, rows):
+    for z in range(NZ):
+        rows[z * ROWS : (z + 1) * ROWS, :] = blocks[z].astype(F32)
+    same = rows[...].astype(BF16)
+    for y in range(NY):
+        copies[y] = same
 
 
 def partial_sums(r0, r2, r1, r3, keep, send):
@@ -197,8 +205,14 @@
     blocks = kernel(prepare, [(PAY, TOK)] * 4, 1 << 28, 3 << 20)(tokens, key_grad)
     work = to_members(blocks)
     by_z = exchange(copies, "z")
-    by_z = by_z.reshape(NZ * ROWS, KV)
-    by_y = exchange(jnp.broadcast_to(by_z[None], (NY, NZ * ROWS, KV)), "y")
+    (by_z,) = kernel(
+        spread,
+        [(NY, NZ * ROWS, KV)],
+        1 << 18,
+        1 << 19,
+        [pltpu.VMEM((NZ * ROWS, KV), F32)],
+    )(by_z)
+    by_y = exchange(by_z, "y")
     keep, send = kernel(partial_sums, [(HALF, KV)] * 2, 1 << 29, 3 << 20)(*far_first(work))
     got = lax.ppermute(send, "c", SWAP)
     (total,) = kernel(add_cores, [(HALF, KV)], 1 << 28, 3 << 19)(keep, got)

time: 109 us -> 108 us (level)
  local copies, waits for them, and re-layouts: 1.71 us -> 0.01 us
    broadcast_in_dim x2 -> x0, local copies, waits for them, and re-layouts: 1.7 us -> none  [shards(): by_y = exchange(jnp.broadcast_to(by_z[None], (NY, NZ * ROWS, KV)), 'y')]
    all_to_all x3, waiting for transfers between devices: 10.5 us -> 9.28 us  [exchange(): return lax.all_to_all(blocks, axis, split_axis=0, concat_axis=0, tiled=True)]
  transfers between devices with their start and end apart: 11 -> 11, of which waited for: 6 -> 6; matrix products, arithmetic and copies ran while one was open for 2% -> 0% of each run, Pallas kernels for 6% -> 7%
where the time goes in v9:
time: 108 us; the launch traced here: 107 us
  starting transfers between devices  57 us (53%)
  blocking collectives  22.5 us (21%)
  waiting for transfers between devices  15.8 us (15%)
  Pallas kernels  10.8 us (10%)
    all_to_all x3, starting transfers between devices, exchange(): return lax.all_to_all(blocks, axis, split_axis=0, concat_axis=0, tiled=True)  29.9 us
    all_to_all x1, blocking collectives, exchange(): return lax.all_to_all(blocks, axis, split_axis=0, concat_axis=0, tiled=True)  22.5 us
    ppermute x2, starting transfers between devices, to_members(): lax.ppermute(blocks[2], 'xh', SWAP)  9.28 us
    all_to_all x3, waiting for transfers between devices, exchange(): return lax.all_to_all(blocks, axis, split_axis=0, concat_axis=0, tiled=True)  9.28 us
    ppermute x1, starting transfers between devices, shards(): other = lax.ppermute(own, 'c', SWAP)  5.25 us
    ppermute x2, starting transfers between devices, to_members(): lax.ppermute(blocks[3], ('xh', 'xl'), [(0, 3), (1, 2), (2, 1), (3, 0)])  4.93 us
    ppermute x2, waiting for transfers between devices, to_members(): lax.ppermute(blocks[1], 'xl', SWAP)  4.45 us
    ppermute x2, starting transfers between devices, to_members(): lax.ppermute(blocks[1], 'xl', SWAP)  4.44 us
  transfers between devices with their start and end apart: 11, of which 6 were waited for; matrix products, arithmetic and copies ran while one was open for 0% of the time, Pallas kernels for 7%

profile of v9, /device:TPU:1, one launch (start us, length us, event | category | flops | bytes accessed | tf_op | source)
XLA Modules:
  0.0 106.9 jit_solution(17707547831605032675)
XLA Ops:
  0.6 0.0 copy-start
  0.6 1.5 %shard_map.67 = bf16[16,4,512]{2,1,0:T(4,128)(2,1)} custom-call(bf16[4,512]{1,0:T(4,128)(2,1)} %codes_ref.1, bf16[4,4]{1,0:T(4,128)(2,1)} %scales_ref.1, bf16[128,4096]{1,0:T(8,128)(2,1)} %tok_ref.3), custom_call_target="tpu_custom_call" | custom-call | flops 4096 | bytes 131072 | tf_op jit(solution)/shard_map/pallas_call | solution.py:204
  2.2 0.0 copy-start.1
  2.2 19.6 %all-to-all-start = ((bf16[16,4,512]{2,1,0:T(4,128)(2,1)}), bf16[16,4,512]{2,1,0:T(4,128)(2,1)S(1)}, u32[]{:S(2)}, u32[]{:S(2)}) async-start(bf16[16,4,512]{2,1,0:T(4,128)(2,1)} %shard_map.67), calls=%async_computation | async-start | bytes 131072 | tf_op jit(solution)/shard_map/all_to_all | solution.py:182
  21.7 0.0 copy-done
  21.8 0.0 copy-done.1
  21.8 1.9 %shard_map.69 = (bf16[1536,128]{1,0:T(8,128)(2,1)S(1)}, bf16[1536,128]{1,0:T(8,128)(2,1)}, bf16[1536,128]{1,0:T(8,128)(2,1)}, bf16[1536,128]{1,0:T(8,128)(2,1)S(1)}) custom-call(bf16[128,4096]{1,0:T(8,128)(2,1)S(1)} %copy-done, bf16[128,512]{1,0:T(8,128)(2,1)S(1)} %copy-done.1), custom_call_target="tpu_custom_call" | custom-call | flops 268435456 | bytes 3145728 | tf_op jit(solution)/shard_map/pallas_call | solution.py:205
  23.6 4.6 %collective-permute-start = (bf16[1536,128]{1,0:T(8,128)(2,1)}, bf16[1536,128]{1,0:T(8,128)(2,1)S(1)}, u32[]{:S(2)}, u32[]{:S(2)}) collective-permute-start(bf16[1536,128]{1,0:T(8,128)(2,1)} %get-tuple-element.18), channel_id=1, source_target_pairs={{0,512},{512,0},{1,513},{513,1},{2,514},{514,2},{3,515},{515,3},{4... | collective-permute-start | bytes 1179656 | tf_op jit(solution)/shard_map/ppermute | solution.py:193
  28.3 2.2 %collective-permute-start.1 = (bf16[1536,128]{1,0:T(8,128)(2,1)}, bf16[1536,128]{1,0:T(8,128)(2,1)S(1)}, u32[]{:S(2)}, u32[]{:S(2)}) collective-permute-start(bf16[1536,128]{1,0:T(8,128)(2,1)} %get-tuple-element.19), channel_id=1, source_target_pairs={{0,32},{32,0},{1,33},{33,1},{2,34},{34,2},{3,35},{35,3},{4,36},{36... | collective-permute-start | bytes 1179656 | tf_op jit(solution)/shard_map/ppermute | solution.py:192
  30.5 2.5 %collective-permute-start.2 = (bf16[1536,128]{1,0:T(8,128)(2,1)S(1)}, bf16[1536,128]{1,0:T(8,128)(2,1)S(1)}, u32[]{:S(2)}, u32[]{:S(2)}) collective-permute-start(bf16[1536,128]{1,0:T(8,128)(2,1)S(1)} %get-tuple-element.20), channel_id=1, source_target_pairs={{0,544},{32,512},{512,32},{544,0},{1,545},{33,513},{513,33},{545,1... | collective-permute-start | bytes 1179656 | tf_op jit(solution)/shard_map/ppermute | solution.py:194
  33.0 0.4 all-to-all-done.blocks
  33.3 0.9 shard_map.68
  34.2 6.8 %all-to-all-start.1 = ((bf16[8,64,512]{2,1,0:T(8,128)(2,1)}), bf16[8,64,512]{2,1,0:T(8,128)(2,1)S(1)}, u32[]{:S(2)}, u32[]{:S(2)}) async-start(bf16[8,64,512]{2,1,0:T(8,128)(2,1)} %shard_map.68), calls=%async_computation.1 | async-start | bytes 1048576 | tf_op jit(solution)/shard_map/all_to_all | solution.py:182
  41.0 0.0 collective-permute-done.r2
  41.0 4.4 %collective-permute-done.1.r1 = bf16[1536,128]{1,0:T(8,128)(2,1)S(1)} collective-permute-done((bf16[1536,128]{1,0:T(8,128)(2,1)}, bf16[1536,128]{1,0:T(8,128)(2,1)S(1)}, u32[]{:S(2)}, u32[]{:S(2)}) %collective-permute-start.1) | collective-permute-done | bytes 393248 | tf_op jit(solution)/shard_map/ppermute | solution.py:192
  45.4 0.6 collective-permute-done.2.r3
  46.0 0.7 shard_map.70
  46.8 3.2 %collective-permute-start.3 = (bf16[512,512]{1,0:T(8,128)(2,1)S(1)}, bf16[512,512]{1,0:T(8,128)(2,1)S(1)}, u32[]{:S(2)}, u32[]{:S(2)}) collective-permute-start(bf16[512,512]{1,0:T(8,128)(2,1)S(1)} %get-tuple-element.22), channel_id=1, source_target_pairs={{0,1},{1,0},{2,3},{3,2},{4,5},{5,4},{6,7},{7,6},{8,9},{9,8},{10,11... | collective-permute-start | bytes 1572872 | tf_op jit(solution)/shard_map/ppermute | solution.py:217
  50.0 1.5 %collective-permute-done.3.b = bf16[512,512]{1,0:T(8,128)(2,1)S(1)} collective-permute-done((bf16[512,512]{1,0:T(8,128)(2,1)S(1)}, bf16[512,512]{1,0:T(8,128)(2,1)S(1)}, u32[]{:S(2)}, u32[]{:S(2)}) %collective-permute-start.3) | collective-permute-done | bytes 524320 | tf_op jit(solution)/shard_map/ppermute | solution.py:217
  51.5 1.3 %shard_map.71 = bf16[512,512]{1,0:T(8,128)(2,1)} custom-call(bf16[512,512]{1,0:T(8,128)(2,1)S(1)} %get-tuple-element.21.a, bf16[512,512]{1,0:T(8,128)(2,1)S(1)} %collective-permute-done.3.b), custom_call_target="tpu_custom_call" | custom-call | flops 268435456 | bytes 1572864 | tf_op jit(solution)/shard_map/pallas_call | solution.py:218
  52.8 3.3 %all-to-all-done.1 = bf16[8,64,512]{2,1,0:T(8,128)(2,1)S(1)} async-done(((bf16[8,64,512]{2,1,0:T(8,128)(2,1)}), bf16[8,64,512]{2,1,0:T(8,128)(2,1)S(1)}, u32[]{:S(2)}, u32[]{:S(2)}) %all-to-all-start.1) | async-done | bytes 524320 | tf_op jit(solution)/shard_map/all_to_all | solution.py:182
  56.1 5.2 %collective-permute-start.4 = (bf16[512,512]{1,0:T(8,128)(2,1)S(1)}, bf16[512,512]{1,0:T(8,128)(2,1)S(1)}, u32[]{:S(2)}, u32[]{:S(2)}) collective-permute-start(bf16[512,512]{1,0:T(8,128)(2,1)S(1)} %bitcast.2), channel_id=1, source_target_pairs={{0,1},{1,0},{2,3},{3,2},{4,5},{5,4},{6,7},{7,6},{8,9},{9,8},{10,11... | collective-permute-start | bytes 1572872 | tf_op jit(solution)/shard_map/ppermute | solution.py:221
  61.3 3.5 %all-to-all-start.2 = ((bf16[8,64,512]{2,1,0:T(8,128)(2,1)}), bf16[8,64,512]{2,1,0:T(8,128)(2,1)S(1)}, u32[]{:S(2)}, u32[]{:S(2)}) async-start(bf16[8,64,512]{2,1,0:T(8,128)(2,1)} %bitcast), calls=%async_computation.2 | async-start | bytes 1048576 | tf_op jit(solution)/shard_map/all_to_all | solution.py:182
  64.9 0.0 collective-permute-done.4.other
  64.9 3.0 %shard_map.73 = (bf16[1536,128]{1,0:T(8,128)(2,1)S(1)}, bf16[1536,128]{1,0:T(8,128)(2,1)}, bf16[1536,128]{1,0:T(8,128)(2,1)}, bf16[1536,128]{1,0:T(8,128)(2,1)}) custom-call(bf16[512,512]{1,0:T(8,128)(2,1)S(1)} %bitcast.3, bf16[512,512]{1,0:T(8,128)(2,1)S(1)} %collective-permute-done.4.other, bf16[1536,128]{1,0:T(8,128)(2,1)S(1)} %get-tuple-element.17.r0, ...), custom_call_target="tpu_custom_call" | custom-call | flops 8589934592 | bytes 4194304 | tf_op jit(solution)/shard_map/pallas_call | solution.py:225
  67.8 4.6 %collective-permute-start.5 = (bf16[1536,128]{1,0:T(8,128)(2,1)}, bf16[1536,128]{1,0:T(8,128)(2,1)S(1)}, u32[]{:S(2)}, u32[]{:S(2)}) collective-permute-start(bf16[1536,128]{1,0:T(8,128)(2,1)} %get-tuple-element.27), channel_id=1, source_target_pairs={{0,512},{512,0},{1,513},{513,1},{2,514},{514,2},{3,515},{515,3},{4... | collective-permute-start | bytes 1179656 | tf_op jit(solution)/shard_map/ppermute | solution.py:193
  72.5 2.2 %collective-permute-start.6 = (bf16[1536,128]{1,0:T(8,128)(2,1)}, bf16[1536,128]{1,0:T(8,128)(2,1)S(1)}, u32[]{:S(2)}, u32[]{:S(2)}) collective-permute-start(bf16[1536,128]{1,0:T(8,128)(2,1)} %get-tuple-element.28), channel_id=1, source_target_pairs={{0,32},{32,0},{1,33},{33,1},{2,34},{34,2},{3,35},{35,3},{4,36},{36... | collective-permute-start | bytes 1179656 | tf_op jit(solution)/shard_map/ppermute | solution.py:192
  74.7 2.5 %collective-permute-start.7 = (bf16[1536,128]{1,0:T(8,128)(2,1)}, bf16[1536,128]{1,0:T(8,128)(2,1)S(1)}, u32[]{:S(2)}, u32[]{:S(2)}) collective-permute-start(bf16[1536,128]{1,0:T(8,128)(2,1)} %get-tuple-element.29), channel_id=1, source_target_pairs={{0,544},{32,512},{512,32},{544,0},{1,545},{33,513},{513,33},{545,1... | collective-permute-start | bytes 1179656 | tf_op jit(solution)/shard_map/ppermute | solution.py:194
  77.2 5.6 %all-to-all-done.2.blocks = bf16[8,64,512]{2,1,0:T(8,128)(2,1)S(1)} async-done(((bf16[8,64,512]{2,1,0:T(8,128)(2,1)}), bf16[8,64,512]{2,1,0:T(8,128)(2,1)S(1)}, u32[]{:S(2)}, u32[]{:S(2)}) %all-to-all-start.2) | async-done | bytes 524320 | tf_op jit(solution)/shard_map/all_to_all | solution.py:182
  82.8 0.1 shard_map.72
  82.9 22.5 %all_to_all.20.sums = bf16[16,4,512]{2,1,0:T(4,128)(2,1)S(1)} all-to-all(bf16[16,4,512]{2,1,0:T(4,128)(2,1)S(1)} %shard_map.72), channel_id=1, replica_groups=mesh['xh'=2,'y'=8,'xl'=2,'z'=16,'c'=2] {'z'}, dimensions={0} | all-to-all | bytes 131072 | tf_op jit(solution)/shard_map/all_to_all | solution.py:182
  105.4 0.0 collective-permute-done.5.f2
  105.4 0.0 collective-permute-done.6.f1
  105.4 0.0 collective-permute-done.7.f3
  105.4 1.5 %shard_map.74 = (bf16[128,512]{1,0:T(8,128)(2,1)}, bf16[128,4096]{1,0:T(8,128)(2,1)}, f32[4,512]{1,0:T(4,128)}) custom-call(bf16[1536,128]{1,0:T(8,128)(2,1)S(1)} %get-tuple-element.26.f0, bf16[1536,128]{1,0:T(8,128)(2,1)S(1)} %collective-permute-done.5.f2, bf16[1536,128]{1,0:T(8,128)(2,1)S(1)} %collective-permute-done.6.f1, ...), custom_call_target="tpu_custom_call" | custom-call | flops 268435456 | bytes 3145728 | tf_op jit(solution)/shard_map/pallas_call | solution.py:232
Async XLA Ops:
  0.6 21.1 %copy-start = (bf16[128,4096]{1,0:T(8,128)(2,1)S(1)}, bf16[128,4096]{1,0:T(8,128)(2,1)}, u32[]{:S(2)}) copy-start(bf16[128,4096]{1,0:T(8,128)(2,1)} %tok_ref.3) | copy-start | bytes 3145732
  2.2 19.6 %copy-start.1 = (bf16[128,512]{1,0:T(8,128)(2,1)S(1)}, bf16[128,512]{1,0:T(8,128)(2,1)}, u32[]{:S(2)}) copy-start(bf16[128,512]{1,0:T(8,128)(2,1)} %grad_ref.1) | copy-start | bytes 393220
  2.2 31.1 %all-to-all-start = ((bf16[16,4,512]{2,1,0:T(4,128)(2,1)}), bf16[16,4,512]{2,1,0:T(4,128)(2,1)S(1)}, u32[]{:S(2)}, u32[]{:S(2)}) async-start(bf16[16,4,512]{2,1,0:T(4,128)(2,1)} %shard_map.67), calls=%async_computation | async-start | bytes 131072 | tf_op jit(solution)/shard_map/all_to_all | solution.py:182
  23.6 17.4 %collective-permute-start = (bf16[1536,128]{1,0:T(8,128)(2,1)}, bf16[1536,128]{1,0:T(8,128)(2,1)S(1)}, u32[]{:S(2)}, u32[]{:S(2)}) collective-permute-start(bf16[1536,128]{1,0:T(8,128)(2,1)} %get-tuple-element.18), channel_id=1, source_target_pairs={{0,512},{512,0},{1,513},{513,1},{2,514},{514,2},{3,515},{515,3},{4... | collective-permute-start | bytes 1179656 | tf_op jit(solution)/shard_map/ppermute | solution.py:193
  28.3 17.2 %collective-permute-start.1 = (bf16[1536,128]{1,0:T(8,128)(2,1)}, bf16[1536,128]{1,0:T(8,128)(2,1)S(1)}, u32[]{:S(2)}, u32[]{:S(2)}) collective-permute-start(bf16[1536,128]{1,0:T(8,128)(2,1)} %get-tuple-element.19), channel_id=1, source_target_pairs={{0,32},{32,0},{1,33},{33,1},{2,34},{34,2},{3,35},{35,3},{4,36},{36... | collective-permute-start | bytes 1179656 | tf_op jit(solution)/shard_map/ppermute | solution.py:192
  30.5 15.5 %collective-permute-start.2 = (bf16[1536,128]{1,0:T(8,128)(2,1)S(1)}, bf16[1536,128]{1,0:T(8,128)(2,1)S(1)}, u32[]{:S(2)}, u32[]{:S(2)}) collective-permute-start(bf16[1536,128]{1,0:T(8,128)(2,1)S(1)} %get-tuple-element.20), channel_id=1, source_target_pairs={{0,544},{32,512},{512,32},{544,0},{1,545},{33,513},{513,33},{545,1... | collective-permute-start | bytes 1179656 | tf_op jit(solution)/shard_map/ppermute | solution.py:194
  34.2 21.9 %all-to-all-start.1 = ((bf16[8,64,512]{2,1,0:T(8,128)(2,1)}), bf16[8,64,512]{2,1,0:T(8,128)(2,1)S(1)}, u32[]{:S(2)}, u32[]{:S(2)}) async-start(bf16[8,64,512]{2,1,0:T(8,128)(2,1)} %shard_map.68), calls=%async_computation.1 | async-start | bytes 1048576 | tf_op jit(solution)/shard_map/all_to_all | solution.py:182
  46.8 4.7 %collective-permute-start.3 = (bf16[512,512]{1,0:T(8,128)(2,1)S(1)}, bf16[512,512]{1,0:T(8,128)(2,1)S(1)}, u32[]{:S(2)}, u32[]{:S(2)}) collective-permute-start(bf16[512,512]{1,0:T(8,128)(2,1)S(1)} %get-tuple-element.22), channel_id=1, source_target_pairs={{0,1},{1,0},{2,3},{3,2},{4,5},{5,4},{6,7},{7,6},{8,9},{9,8},{10,11... | collective-permute-start | bytes 1572872 | tf_op jit(solution)/shard_map/ppermute | solution.py:217
  56.1 8.8 %collective-permute-start.4 = (bf16[512,512]{1,0:T(8,128)(2,1)S(1)}, bf16[512,512]{1,0:T(8,128)(2,1)S(1)}, u32[]{:S(2)}, u32[]{:S(2)}) collective-permute-start(bf16[512,512]{1,0:T(8,128)(2,1)S(1)} %bitcast.2), channel_id=1, source_target_pairs={{0,1},{1,0},{2,3},{3,2},{4,5},{5,4},{6,7},{7,6},{8,9},{9,8},{10,11... | collective-permute-start | bytes 1572872 | tf_op jit(solution)/shard_map/ppermute | solution.py:221
  61.3 21.5 %all-to-all-start.2 = ((bf16[8,64,512]{2,1,0:T(8,128)(2,1)}), bf16[8,64,512]{2,1,0:T(8,128)(2,1)S(1)}, u32[]{:S(2)}, u32[]{:S(2)}) async-start(bf16[8,64,512]{2,1,0:T(8,128)(2,1)} %bitcast), calls=%async_computation.2 | async-start | bytes 1048576 | tf_op jit(solution)/shard_map/all_to_all | solution.py:182
  67.8 37.6 %collective-permute-start.5 = (bf16[1536,128]{1,0:T(8,128)(2,1)}, bf16[1536,128]{1,0:T(8,128)(2,1)S(1)}, u32[]{:S(2)}, u32[]{:S(2)}) collective-permute-start(bf16[1536,128]{1,0:T(8,128)(2,1)} %get-tuple-element.27), channel_id=1, source_target_pairs={{0,512},{512,0},{1,513},{513,1},{2,514},{514,2},{3,515},{515,3},{4... | collective-permute-start | bytes 1179656 | tf_op jit(solution)/shard_map/ppermute | solution.py:193
  72.5 32.9 %collective-permute-start.6 = (bf16[1536,128]{1,0:T(8,128)(2,1)}, bf16[1536,128]{1,0:T(8,128)(2,1)S(1)}, u32[]{:S(2)}, u32[]{:S(2)}) collective-permute-start(bf16[1536,128]{1,0:T(8,128)(2,1)} %get-tuple-element.28), channel_id=1, source_target_pairs={{0,32},{32,0},{1,33},{33,1},{2,34},{34,2},{3,35},{35,3},{4,36},{36... | collective-permute-start | bytes 1179656 | tf_op jit(solution)/shard_map/ppermute | solution.py:192
  74.7 30.7 %collective-permute-start.7 = (bf16[1536,128]{1,0:T(8,128)(2,1)}, bf16[1536,128]{1,0:T(8,128)(2,1)S(1)}, u32[]{:S(2)}, u32[]{:S(2)}) collective-permute-start(bf16[1536,128]{1,0:T(8,128)(2,1)} %get-tuple-element.29), channel_id=1, source_target_pairs={{0,544},{32,512},{512,32},{544,0},{1,545},{33,513},{513,33},{545,1... | collective-permute-start | bytes 1179656 | tf_op jit(solution)/shard_map/ppermute | solution.py:194

commit v10 on v9

--- a/solution.py
+++ b/solution.py
@@ -223,7 +223,7 @@
     (total,) = kernel(sum_over_y, [(NZ, ROWS, KV)], 1 << 18, 1 << 20)(total)
     total = exchange(total, "z")
     results = kernel(
-        apply_weight, [(PAY, TOK)] * 4, 1 << 33, 4 << 20, [pltpu.VMEM((SLICE, KV), BF16)]
+        apply_weight, [(PAY, TOK)] * 4, 1 << 30, 4 << 20, [pltpu.VMEM((SLICE, KV), BF16)]
     )(own, other, *work)
     results = to_members(results)
     total, mine = lax.optimization_barrier((total, results[0]))

time: 108 us -> 104 us (0.963)
  waiting for transfers between devices: 15.8 us -> 11.7 us
    all_to_all x3, waiting for transfers between devices: 9.28 us -> 3.65 us  [exchange(): return lax.all_to_all(blocks, axis, split_axis=0, concat_axis=0, tiled=True)]
    ppermute x1, waiting for transfers between devices: 0.01 us -> 1.51 us  [shards(): other = lax.ppermute(own, 'c', SWAP)]
where the time goes in v10:
time: 104 us; the launch traced here: 102 us
  starting transfers between devices  57 us (55%)
  blocking collectives  22.2 us (21%)
  waiting for transfers between devices  11.7 us (11%)
  Pallas kernels  10.7 us (10%)
    all_to_all x3, starting transfers between devices, exchange(): return lax.all_to_all(blocks, axis, split_axis=0, concat_axis=0, tiled=True)  29.9 us
    all_to_all x1, blocking collectives, exchange(): return lax.all_to_all(blocks, axis, split_axis=0, concat_axis=0, tiled=True)  22.2 us
    ppermute x2, starting transfers between devices, to_members(): lax.ppermute(blocks[2], 'xh', SWAP)  9.28 us
    ppermute x1, starting transfers between devices, shards(): other = lax.ppermute(own, 'c', SWAP)  5.24 us
    ppermute x2, starting transfers between devices, to_members(): lax.ppermute(blocks[3], ('xh', 'xl'), [(0, 3), (1, 2), (2, 1), (3, 0)])  4.93 us
    ppermute x2, waiting for transfers between devices, to_members(): lax.ppermute(blocks[1], 'xl', SWAP)  4.45 us
    ppermute x2, starting transfers between devices, to_members(): lax.ppermute(blocks[1], 'xl', SWAP)  4.43 us
    all_to_all x3, waiting for transfers between devices, exchange(): return lax.all_to_all(blocks, axis, split_axis=0, concat_axis=0, tiled=True)  3.65 us
  transfers between devices with their start and end apart: 11, of which 6 were waited for; matrix products, arithmetic and copies ran while one was open for 0% of the time, Pallas kernels for 7%

profile of v10, /device:TPU:1, one launch (start us, length us, event | category | flops | bytes accessed | tf_op | source)
XLA Modules:
  0.0 102.4 jit_solution(17344178091692235982)
XLA Ops:
  0.6 0.0 copy-start
  0.6 1.5 %shard_map.67 = bf16[16,4,512]{2,1,0:T(4,128)(2,1)} custom-call(bf16[4,512]{1,0:T(4,128)(2,1)} %codes_ref.1, bf16[4,4]{1,0:T(4,128)(2,1)} %scales_ref.1, bf16[128,4096]{1,0:T(8,128)(2,1)} %tok_ref.3), custom_call_target="tpu_custom_call" | custom-call | flops 4096 | bytes 131072 | tf_op jit(solution)/shard_map/pallas_call | solution.py:204
  2.2 0.0 copy-start.1
  2.2 19.6 %all-to-all-start = ((bf16[16,4,512]{2,1,0:T(4,128)(2,1)}), bf16[16,4,512]{2,1,0:T(4,128)(2,1)S(1)}, u32[]{:S(2)}, u32[]{:S(2)}) async-start(bf16[16,4,512]{2,1,0:T(4,128)(2,1)} %shard_map.67), calls=%async_computation | async-start | bytes 131072 | tf_op jit(solution)/shard_map/all_to_all | solution.py:182
  21.7 0.0 copy-done
  21.8 0.0 copy-done.1
  21.8 1.9 %shard_map.69 = (bf16[1536,128]{1,0:T(8,128)(2,1)S(1)}, bf16[1536,128]{1,0:T(8,128)(2,1)}, bf16[1536,128]{1,0:T(8,128)(2,1)}, bf16[1536,128]{1,0:T(8,128)(2,1)S(1)}) custom-call(bf16[128,4096]{1,0:T(8,128)(2,1)S(1)} %copy-done, bf16[128,512]{1,0:T(8,128)(2,1)S(1)} %copy-done.1), custom_call_target="tpu_custom_call" | custom-call | flops 268435456 | bytes 3145728 | tf_op jit(solution)/shard_map/pallas_call | solution.py:205
  23.6 4.6 %collective-permute-start = (bf16[1536,128]{1,0:T(8,128)(2,1)}, bf16[1536,128]{1,0:T(8,128)(2,1)S(1)}, u32[]{:S(2)}, u32[]{:S(2)}) collective-permute-start(bf16[1536,128]{1,0:T(8,128)(2,1)} %get-tuple-element.18), channel_id=1, source_target_pairs={{0,512},{512,0},{1,513},{513,1},{2,514},{514,2},{3,515},{515,3},{4... | collective-permute-start | bytes 1179656 | tf_op jit(solution)/shard_map/ppermute | solution.py:193
  28.3 2.2 %collective-permute-start.1 = (bf16[1536,128]{1,0:T(8,128)(2,1)}, bf16[1536,128]{1,0:T(8,128)(2,1)S(1)}, u32[]{:S(2)}, u32[]{:S(2)}) collective-permute-start(bf16[1536,128]{1,0:T(8,128)(2,1)} %get-tuple-element.19), channel_id=1, source_target_pairs={{0,32},{32,0},{1,33},{33,1},{2,34},{34,2},{3,35},{35,3},{4,36},{36... | collective-permute-start | bytes 1179656 | tf_op jit(solution)/shard_map/ppermute | solution.py:192
  30.5 2.5 %collective-permute-start.2 = (bf16[1536,128]{1,0:T(8,128)(2,1)S(1)}, bf16[1536,128]{1,0:T(8,128)(2,1)S(1)}, u32[]{:S(2)}, u32[]{:S(2)}) collective-permute-start(bf16[1536,128]{1,0:T(8,128)(2,1)S(1)} %get-tuple-element.20), channel_id=1, source_target_pairs={{0,544},{32,512},{512,32},{544,0},{1,545},{33,513},{513,33},{545,1... | collective-permute-start | bytes 1179656 | tf_op jit(solution)/shard_map/ppermute | solution.py:194
  33.0 0.4 all-to-all-done.blocks
  33.3 0.9 shard_map.68
  34.2 6.8 %all-to-all-start.1 = ((bf16[8,64,512]{2,1,0:T(8,128)(2,1)}), bf16[8,64,512]{2,1,0:T(8,128)(2,1)S(1)}, u32[]{:S(2)}, u32[]{:S(2)}) async-start(bf16[8,64,512]{2,1,0:T(8,128)(2,1)} %shard_map.68), calls=%async_computation.1 | async-start | bytes 1048576 | tf_op jit(solution)/shard_map/all_to_all | solution.py:182
  41.0 0.0 collective-permute-done.r2
  41.0 4.4 %collective-permute-done.1.r1 = bf16[1536,128]{1,0:T(8,128)(2,1)S(1)} collective-permute-done((bf16[1536,128]{1,0:T(8,128)(2,1)}, bf16[1536,128]{1,0:T(8,128)(2,1)S(1)}, u32[]{:S(2)}, u32[]{:S(2)}) %collective-permute-start.1) | collective-permute-done | bytes 393248 | tf_op jit(solution)/shard_map/ppermute | solution.py:192
  45.4 0.6 collective-permute-done.2.r3
  46.0 0.7 shard_map.70
  46.8 3.2 %collective-permute-start.3 = (bf16[512,512]{1,0:T(8,128)(2,1)S(1)}, bf16[512,512]{1,0:T(8,128)(2,1)S(1)}, u32[]{:S(2)}, u32[]{:S(2)}) collective-permute-start(bf16[512,512]{1,0:T(8,128)(2,1)S(1)} %get-tuple-element.22), channel_id=1, source_target_pairs={{0,1},{1,0},{2,3},{3,2},{4,5},{5,4},{6,7},{7,6},{8,9},{9,8},{10,11... | collective-permute-start | bytes 1572872 | tf_op jit(solution)/shard_map/ppermute | solution.py:217
  50.0 1.5 %collective-permute-done.3.b = bf16[512,512]{1,0:T(8,128)(2,1)S(1)} collective-permute-done((bf16[512,512]{1,0:T(8,128)(2,1)S(1)}, bf16[512,512]{1,0:T(8,128)(2,1)S(1)}, u32[]{:S(2)}, u32[]{:S(2)}) %collective-permute-start.3) | collective-permute-done | bytes 524320 | tf_op jit(solution)/shard_map/ppermute | solution.py:217
  51.5 1.3 %shard_map.71 = bf16[512,512]{1,0:T(8,128)(2,1)} custom-call(bf16[512,512]{1,0:T(8,128)(2,1)S(1)} %get-tuple-element.21.a, bf16[512,512]{1,0:T(8,128)(2,1)S(1)} %collective-permute-done.3.b), custom_call_target="tpu_custom_call" | custom-call | flops 268435456 | bytes 1572864 | tf_op jit(solution)/shard_map/pallas_call | solution.py:218
  52.8 3.3 %all-to-all-done.1 = bf16[8,64,512]{2,1,0:T(8,128)(2,1)S(1)} async-done(((bf16[8,64,512]{2,1,0:T(8,128)(2,1)}), bf16[8,64,512]{2,1,0:T(8,128)(2,1)S(1)}, u32[]{:S(2)}, u32[]{:S(2)}) %all-to-all-start.1) | async-done | bytes 524320 | tf_op jit(solution)/shard_map/all_to_all | solution.py:182
  56.1 3.5 %all-to-all-start.2 = ((bf16[8,64,512]{2,1,0:T(8,128)(2,1)}), bf16[8,64,512]{2,1,0:T(8,128)(2,1)S(1)}, u32[]{:S(2)}, u32[]{:S(2)}) async-start(bf16[8,64,512]{2,1,0:T(8,128)(2,1)} %bitcast), calls=%async_computation.2 | async-start | bytes 1048576 | tf_op jit(solution)/shard_map/all_to_all | solution.py:182
  59.6 5.2 %collective-permute-start.4 = (bf16[512,512]{1,0:T(8,128)(2,1)S(1)}, bf16[512,512]{1,0:T(8,128)(2,1)S(1)}, u32[]{:S(2)}, u32[]{:S(2)}) collective-permute-start(bf16[512,512]{1,0:T(8,128)(2,1)S(1)} %bitcast.2), channel_id=1, source_target_pairs={{0,1},{1,0},{2,3},{3,2},{4,5},{5,4},{6,7},{7,6},{8,9},{9,8},{10,11... | collective-permute-start | bytes 1572872 | tf_op jit(solution)/shard_map/ppermute | solution.py:221
  64.9 1.5 %collective-permute-done.4.other = bf16[512,512]{1,0:T(8,128)(2,1)S(1)} collective-permute-done((bf16[512,512]{1,0:T(8,128)(2,1)S(1)}, bf16[512,512]{1,0:T(8,128)(2,1)S(1)}, u32[]{:S(2)}, u32[]{:S(2)}) %collective-permute-start.4) | collective-permute-done | bytes 524320 | tf_op jit(solution)/shard_map/ppermute | solution.py:221
  66.4 2.8 %shard_map.73 = (bf16[1536,128]{1,0:T(8,128)(2,1)S(1)}, bf16[1536,128]{1,0:T(8,128)(2,1)}, bf16[1536,128]{1,0:T(8,128)(2,1)}, bf16[1536,128]{1,0:T(8,128)(2,1)S(1)}) custom-call(bf16[512,512]{1,0:T(8,128)(2,1)S(1)} %bitcast.3, bf16[512,512]{1,0:T(8,128)(2,1)S(1)} %collective-permute-done.4.other, bf16[1536,128]{1,0:T(8,128)(2,1)S(1)} %get-tuple-element.17.r0, ...), custom_call_target="tpu_custom_call" | custom-call | flops 1073741824 | bytes 4194304 | tf_op jit(solution)/shard_map/pallas_call | solution.py:225
  69.2 4.6 %collective-permute-start.5 = (bf16[1536,128]{1,0:T(8,128)(2,1)}, bf16[1536,128]{1,0:T(8,128)(2,1)S(1)}, u32[]{:S(2)}, u32[]{:S(2)}) collective-permute-start(bf16[1536,128]{1,0:T(8,128)(2,1)} %get-tuple-element.27), channel_id=1, source_target_pairs={{0,512},{512,0},{1,513},{513,1},{2,514},{514,2},{3,515},{515,3},{4... | collective-permute-start | bytes 1179656 | tf_op jit(solution)/shard_map/ppermute | solution.py:193
  73.8 2.2 %collective-permute-start.6 = (bf16[1536,128]{1,0:T(8,128)(2,1)}, bf16[1536,128]{1,0:T(8,128)(2,1)S(1)}, u32[]{:S(2)}, u32[]{:S(2)}) collective-permute-start(bf16[1536,128]{1,0:T(8,128)(2,1)} %get-tuple-element.28), channel_id=1, source_target_pairs={{0,32},{32,0},{1,33},{33,1},{2,34},{34,2},{3,35},{35,3},{4,36},{36... | collective-permute-start | bytes 1179656 | tf_op jit(solution)/shard_map/ppermute | solution.py:192
  76.1 2.5 %collective-permute-start.7 = (bf16[1536,128]{1,0:T(8,128)(2,1)S(1)}, bf16[1536,128]{1,0:T(8,128)(2,1)S(1)}, u32[]{:S(2)}, u32[]{:S(2)}) collective-permute-start(bf16[1536,128]{1,0:T(8,128)(2,1)S(1)} %get-tuple-element.29), channel_id=1, source_target_pairs={{0,544},{32,512},{512,32},{544,0},{1,545},{33,513},{513,33},{545,1... | collective-permute-start | bytes 1179656 | tf_op jit(solution)/shard_map/ppermute | solution.py:194
  78.5 0.0 all-to-all-done.2.blocks
  78.6 0.1 shard_map.72
  78.6 22.2 %all_to_all.20.sums = bf16[16,4,512]{2,1,0:T(4,128)(2,1)S(1)} all-to-all(bf16[16,4,512]{2,1,0:T(4,128)(2,1)S(1)} %shard_map.72), channel_id=1, replica_groups=mesh['xh'=2,'y'=8,'xl'=2,'z'=16,'c'=2] {'z'}, dimensions={0} | all-to-all | bytes 131072 | tf_op jit(solution)/shard_map/all_to_all | solution.py:182
  100.9 0.0 collective-permute-done.5.f2
  100.9 0.0 collective-permute-done.6.f1
  100.9 0.0 collective-permute-done.7.f3
  100.9 1.5 %shard_map.74 = (bf16[128,512]{1,0:T(8,128)(2,1)}, bf16[128,4096]{1,0:T(8,128)(2,1)}, f32[4,512]{1,0:T(4,128)}) custom-call(bf16[1536,128]{1,0:T(8,128)(2,1)S(1)} %get-tuple-element.26.f0, bf16[1536,128]{1,0:T(8,128)(2,1)S(1)} %collective-permute-done.5.f2, bf16[1536,128]{1,0:T(8,128)(2,1)S(1)} %collective-permute-done.6.f1, ...), custom_call_target="tpu_custom_call" | custom-call | flops 268435456 | bytes 3145728 | tf_op jit(solution)/shard_map/pallas_call | solution.py:232
Async XLA Ops:
  0.6 21.1 %copy-start = (bf16[128,4096]{1,0:T(8,128)(2,1)S(1)}, bf16[128,4096]{1,0:T(8,128)(2,1)}, u32[]{:S(2)}) copy-start(bf16[128,4096]{1,0:T(8,128)(2,1)} %tok_ref.3) | copy-start | bytes 3145732
  2.2 19.6 %copy-start.1 = (bf16[128,512]{1,0:T(8,128)(2,1)S(1)}, bf16[128,512]{1,0:T(8,128)(2,1)}, u32[]{:S(2)}) copy-start(bf16[128,512]{1,0:T(8,128)(2,1)} %grad_ref.1) | copy-start | bytes 393220
  2.2 31.1 %all-to-all-start = ((bf16[16,4,512]{2,1,0:T(4,128)(2,1)}), bf16[16,4,512]{2,1,0:T(4,128)(2,1)S(1)}, u32[]{:S(2)}, u32[]{:S(2)}) async-start(bf16[16,4,512]{2,1,0:T(4,128)(2,1)} %shard_map.67), calls=%async_computation | async-start | bytes 131072 | tf_op jit(solution)/shard_map/all_to_all | solution.py:182
  23.6 17.4 %collective-permute-start = (bf16[1536,128]{1,0:T(8,128)(2,1)}, bf16[1536,128]{1,0:T(8,128)(2,1)S(1)}, u32[]{:S(2)}, u32[]{:S(2)}) collective-permute-start(bf16[1536,128]{1,0:T(8,128)(2,1)} %get-tuple-element.18), channel_id=1, source_target_pairs={{0,512},{512,0},{1,513},{513,1},{2,514},{514,2},{3,515},{515,3},{4... | collective-permute-start | bytes 1179656 | tf_op jit(solution)/shard_map/ppermute | solution.py:193
  28.3 17.2 %collective-permute-start.1 = (bf16[1536,128]{1,0:T(8,128)(2,1)}, bf16[1536,128]{1,0:T(8,128)(2,1)S(1)}, u32[]{:S(2)}, u32[]{:S(2)}) collective-permute-start(bf16[1536,128]{1,0:T(8,128)(2,1)} %get-tuple-element.19), channel_id=1, source_target_pairs={{0,32},{32,0},{1,33},{33,1},{2,34},{34,2},{3,35},{35,3},{4,36},{36... | collective-permute-start | bytes 1179656 | tf_op jit(solution)/shard_map/ppermute | solution.py:192
  30.5 15.5 %collective-permute-start.2 = (bf16[1536,128]{1,0:T(8,128)(2,1)S(1)}, bf16[1536,128]{1,0:T(8,128)(2,1)S(1)}, u32[]{:S(2)}, u32[]{:S(2)}) collective-permute-start(bf16[1536,128]{1,0:T(8,128)(2,1)S(1)} %get-tuple-element.20), channel_id=1, source_target_pairs={{0,544},{32,512},{512,32},{544,0},{1,545},{33,513},{513,33},{545,1... | collective-permute-start | bytes 1179656 | tf_op jit(solution)/shard_map/ppermute | solution.py:194
  34.2 21.9 %all-to-all-start.1 = ((bf16[8,64,512]{2,1,0:T(8,128)(2,1)}), bf16[8,64,512]{2,1,0:T(8,128)(2,1)S(1)}, u32[]{:S(2)}, u32[]{:S(2)}) async-start(bf16[8,64,512]{2,1,0:T(8,128)(2,1)} %shard_map.68), calls=%async_computation.1 | async-start | bytes 1048576 | tf_op jit(solution)/shard_map/all_to_all | solution.py:182
  46.8 4.7 %collective-permute-start.3 = (bf16[512,512]{1,0:T(8,128)(2,1)S(1)}, bf16[512,512]{1,0:T(8,128)(2,1)S(1)}, u32[]{:S(2)}, u32[]{:S(2)}) collective-permute-start(bf16[512,512]{1,0:T(8,128)(2,1)S(1)} %get-tuple-element.22), channel_id=1, source_target_pairs={{0,1},{1,0},{2,3},{3,2},{4,5},{5,4},{6,7},{7,6},{8,9},{9,8},{10,11... | collective-permute-start | bytes 1572872 | tf_op jit(solution)/shard_map/ppermute | solution.py:217
  56.1 22.5 %all-to-all-start.2 = ((bf16[8,64,512]{2,1,0:T(8,128)(2,1)}), bf16[8,64,512]{2,1,0:T(8,128)(2,1)S(1)}, u32[]{:S(2)}, u32[]{:S(2)}) async-start(bf16[8,64,512]{2,1,0:T(8,128)(2,1)} %bitcast), calls=%async_computation.2 | async-start | bytes 1048576 | tf_op jit(solution)/shard_map/all_to_all | solution.py:182
  59.6 6.8 %collective-permute-start.4 = (bf16[512,512]{1,0:T(8,128)(2,1)S(1)}, bf16[512,512]{1,0:T(8,128)(2,1)S(1)}, u32[]{:S(2)}, u32[]{:S(2)}) collective-permute-start(bf16[512,512]{1,0:T(8,128)(2,1)S(1)} %bitcast.2), channel_id=1, source_target_pairs={{0,1},{1,0},{2,3},{3,2},{4,5},{5,4},{6,7},{7,6},{8,9},{9,8},{10,11... | collective-permute-start | bytes 1572872 | tf_op jit(solution)/shard_map/ppermute | solution.py:221
  69.2 31.7 %collective-permute-start.5 = (bf16[1536,128]{1,0:T(8,128)(2,1)}, bf16[1536,128]{1,0:T(8,128)(2,1)S(1)}, u32[]{:S(2)}, u32[]{:S(2)}) collective-permute-start(bf16[1536,128]{1,0:T(8,128)(2,1)} %get-tuple-element.27), channel_id=1, source_target_pairs={{0,512},{512,0},{1,513},{513,1},{2,514},{514,2},{3,515},{515,3},{4... | collective-permute-start | bytes 1179656 | tf_op jit(solution)/shard_map/ppermute | solution.py:193
  73.8 27.0 %collective-permute-start.6 = (bf16[1536,128]{1,0:T(8,128)(2,1)}, bf16[1536,128]{1,0:T(8,128)(2,1)S(1)}, u32[]{:S(2)}, u32[]{:S(2)}) collective-permute-start(bf16[1536,128]{1,0:T(8,128)(2,1)} %get-tuple-element.28), channel_id=1, source_target_pairs={{0,32},{32,0},{1,33},{33,1},{2,34},{34,2},{3,35},{35,3},{4,36},{36... | collective-permute-start | bytes 1179656 | tf_op jit(solution)/shard_map/ppermute | solution.py:192
  76.1 24.8 %collective-permute-start.7 = (bf16[1536,128]{1,0:T(8,128)(2,1)S(1)}, bf16[1536,128]{1,0:T(8,128)(2,1)S(1)}, u32[]{:S(2)}, u32[]{:S(2)}) collective-permute-start(bf16[1536,128]{1,0:T(8,128)(2,1)S(1)} %get-tuple-element.29), channel_id=1, source_target_pairs={{0,544},{32,512},{512,32},{544,0},{1,545},{33,513},{513,33},{545,1... | collective-permute-start | bytes 1179656 | tf_op jit(solution)/shard_map/ppermute | solution.py:194
